TPU v7x, 32 devices: a whole 2x2x4 slice. The times are simulated.
32 devices in a mesh: group: 8 (over y, x, core), narrow: 4 (over z).
Axes of the slice: x: 2, y: 2, z: 4, core: 2. Of those that a mesh axis runs over, the one named last changes fastest.
Arguments:
- patches: bfloat16 [512, 3675], P(('group', 'narrow')), may hold values from -8 to 8
- counts: int32 [512], P(('group', 'narrow')), may hold values from 1 to 49
- weights: float32 [49], replicated, may hold values from 0.3 to 3
- probes: float32 [512, 16], P(('group', 'narrow')), may hold values from -6 to 6
- plan: int32 [4, 8], replicated, may hold values from 0 to 7, as said below
Outputs:
- product: float32 [512, 16], P(('group', 'narrow'))
Inputs may be any that keep to these rules, and one draw needn't show every extreme that they name: Each row pairs the 8 blocks: plan[m, plan[m, b]] = b and plan[m, b] != b.
All inputs are finite; a program needn't handle non-finite values.
Results may differ from a plain program's by a relative error of at most 0.008.
Values may be sent and summed in bfloat16 or wider, within the bound.
No kernel may reach another device: no remote copies, remote signals or barrier semaphores. Data moves between devices by JAX's collectives and lax.ppermute only.
A program may use at most 64 MiB of HBM per device.

v0:
```python
import functools
import math

import jax
import jax.numpy as jnp
from jax import lax
from jax.experimental import pallas as pl
from jax.experimental.pallas import tpu as pltpu
from jax.sharding import PartitionSpec as P

P_SIZE = 49
PV = 75
NPROBE = 16
LANES = 128
NORM_AT = PV
ALPHA_AT = PV + 3
FEATURES = 5
STRIDE = PV + FEATURES
WIDE = P_SIZE * STRIDE
PACKED = (WIDE + 1 + 2 * NPROBE + LANES - 1) // LANES * LANES
TAIL = WIDE // LANES * LANES
COUNT_AT = WIDE - TAIL
PROBE_AT = COUNT_AT + 1
ROWS = 1024
COLS = 512
SCALE = 2.0 * math.log2(math.e) / (2.0 * PV)
NT = (((1,), (1,)), ((), ()))
NN = (((1,), (0,)), ((), ()))
VMEM = pl.BlockSpec(memory_space=pltpu.VMEM)
SMEM = pl.BlockSpec(memory_space=pltpu.SMEM)
ANY = pl.BlockSpec(memory_space=pl.ANY)


def dot(a, b, dims=NN):
    return lax.dot_general(a, b, dims, preferred_element_type=jnp.float32)


def iota(shape, dim):
    return lax.broadcasted_iota(jnp.int32, shape, dim)


def parts(value):
    hi = value.astype(jnp.bfloat16).astype(jnp.float32)
    rest = value - hi
    mid = rest.astype(jnp.bfloat16).astype(jnp.float32)
    return hi, mid, (rest - mid).astype(jnp.bfloat16).astype(jnp.float32)


def pack_kernel(patches_ref, counts_ref, weights_ref, probes_ref, out_ref):
    images, wide = patches_ref.shape
    shape = (images, LANES)
    lane = iota(shape, 1)
    square = (images, images)
    along = jnp.broadcast_to(counts_ref[...].astype(jnp.float32), square)
    count = jnp.sum(jnp.where(iota(square, 0) == iota(square, 1), along, 0.0), axis=1, keepdims=True)
    weight = jnp.concatenate([weights_ref[...], jnp.zeros((1, LANES - P_SIZE), jnp.float32)], axis=1)
    alpha = weight * (lane.astype(jnp.float32) < count).astype(jnp.float32) / count
    patches = []
    for p in range(P_SIZE):
        values = patches_ref[:, p * PV : min(p * PV + LANES, wide)]
        if values.shape[1] < LANES:
            values = jnp.concatenate([values, jnp.zeros((images, LANES - values.shape[1]), jnp.bfloat16)], axis=1)
        patches.append(jnp.where(lane < PV, values, jnp.bfloat16(0)))
    stacked = jnp.concatenate(patches, axis=0).astype(jnp.float32)
    squares = stacked * stacked
    ones = jnp.ones((LANES, LANES), jnp.bfloat16)
    high = squares.astype(jnp.bfloat16)
    norm = dot(high, ones) + dot((squares - high.astype(jnp.float32)).astype(jnp.bfloat16), ones)
    norms = [part.astype(jnp.bfloat16) for part in parts(-0.5 * norm)]
    alphas = [part.astype(jnp.bfloat16) for part in parts(alpha)[:2]]
    tiles = [None] * (PACKED // LANES)

    def put(values, start):
        tile, shift = divmod(start, LANES)
        moved = pltpu.roll(values, shift, 1) if shift else values
        first = jnp.where(lane >= shift, moved, jnp.bfloat16(0)) if shift else moved
        tiles[tile] = first if tiles[tile] is None else tiles[tile] + first
        if shift and tile + 1 < len(tiles):
            tiles[tile + 1] = jnp.where(lane < shift, moved, jnp.bfloat16(0))

    for p in range(P_SIZE):
        values = patches[p]
        for step, part in enumerate(norms):
            values = jnp.where(lane == NORM_AT + step, part[p * images : (p + 1) * images], values)
        for step, part in enumerate(alphas):
            values = jnp.where(lane == ALPHA_AT + step, pltpu.roll(part, (ALPHA_AT + step - p) % LANES, 1), values)
        put(values, p * STRIDE)
    probe_hi, probe_low, unused = parts(probes_ref[...])
    rest = jnp.concatenate(
        [count, probe_hi, probe_low, jnp.zeros((images, LANES - 1 - 2 * NPROBE), jnp.float32)], axis=1
    )
    put(rest.astype(jnp.bfloat16), WIDE)
    for tile, values in enumerate(tiles):
        out_ref[:, tile * LANES : (tile + 1) * LANES] = values


def pack(patches, counts, weights, probes):
    return pl.pallas_call(
        pack_kernel,
        out_shape=jax.ShapeDtypeStruct((patches.shape[0], PACKED), jnp.bfloat16),
        in_specs=[VMEM] * 4,
        out_specs=VMEM,
        name="pack",
    )(patches, counts[None, :], weights[None, :], probes)


def order(tail):
    number = tail.shape[0]
    count = tail[:, COUNT_AT : COUNT_AT + 1]
    key = count * number + (number - 1 - iota((number, 1), 0)).astype(jnp.float32)
    square = (number, number)
    key_here = jnp.broadcast_to(key, square)
    key_along = jnp.sum(jnp.where(iota(square, 0) == iota(square, 1), key_here, 0.0), axis=0, keepdims=True)
    rank = jnp.sum((key_here > key_along).astype(jnp.float32), axis=0, keepdims=True)
    chosen = (iota(square, 0).astype(jnp.float32) == rank).astype(jnp.bfloat16)
    patch = iota((number, LANES), 1).astype(jnp.float32)
    valid = jnp.sum((count > patch).astype(jnp.float32), axis=0, keepdims=True)
    taken = ((valid.astype(jnp.int32) + 15) // 16 * 16).astype(jnp.float32)
    before = (iota((LANES, LANES), 0) < iota((LANES, LANES), 1)).astype(jnp.bfloat16)
    first = dot(jnp.broadcast_to(taken, (8, LANES)).astype(jnp.bfloat16), before)
    return chosen, first.astype(jnp.int32)


def spread(sorted_ref, chosen, first_ref, at, x_ref, owner_ref, size):
    number = sorted_ref.shape[0]
    lane = iota((number, LANES), 1)
    for p in range(P_SIZE):
        values = jnp.where(lane < STRIDE, sorted_ref[:, p * STRIDE : p * STRIDE + LANES], jnp.bfloat16(0))
        start = pl.multiple_of(first_ref[at, p], 16)
        x_ref[pl.ds(start, number), :] = values
        owner_ref[pl.ds(start, number), :] = chosen
    total = pl.multiple_of(first_ref[at, P_SIZE], 16)
    x_ref[pl.ds(total, size), :] = jnp.zeros((size, LANES), jnp.bfloat16)
    owner_ref[pl.ds(total, size), :] = jnp.zeros((size, number), jnp.bfloat16)
    return (total + size - 1) // size


def energies(images, meetings, counted, *refs):
    near_number, far_number = counted
    plan_ref, mine_ref = refs[:2]
    near_parts = refs[2 : 2 + near_number]
    far_parts = refs[2 + near_number : 2 + near_number + far_number]
    (out_ref, near_ref, far_ref, row_sorted, col_sorted, row_x, col_x, row_owner, col_owner, col_u, product,
     first_v, first_s, sem, near_sem, far_sem) = refs[2 + near_number + far_number :]
    copies = []
    for target, sources, sems in ((far_ref, far_parts, far_sem), (near_ref, near_parts, near_sem)):
        at = 0
        for index, source in enumerate(sources):
            size = source.shape[0]
            copies.append(pltpu.make_async_copy(source, target.at[pl.ds(at, size), :], sems.at[index]))
            at += size
    for copy in copies:
        copy.start()

    mine = mine_ref[0]
    far = far_ref.shape[0]
    cols = images * meetings
    line = iota((cols, far), 0)
    source = jnp.zeros((cols, far), jnp.int32)
    for meeting in range(meetings):
        here = (line >= meeting * images) & (line < (meeting + 1) * images)
        apart = plan_ref[meeting, mine] ^ mine
        slot = (apart & 1) * (far // images // 2) + (apart >> 1)
        source = jnp.where(here, slot * images + line - meeting * images, source)
    met = (iota((cols, far), 1) == source).astype(jnp.bfloat16)
    for target in (row_sorted, col_sorted):
        target[:, PACKED:] = jnp.zeros((target.shape[0], LANES), jnp.bfloat16)
    for copy in copies:
        copy.wait()

    row_order, row_first = order(near_ref[:, TAIL : TAIL + LANES].astype(jnp.float32))
    col_tail = dot(met, far_ref[:, TAIL : TAIL + LANES])
    col_order, col_first = order(col_tail)
    first_v[0:8, :] = row_first
    first_v[8:16, :] = col_first
    copy = pltpu.make_async_copy(first_v, first_s, sem)
    copy.start()
    row_sorted[:, 0:PACKED] = dot(row_order, near_ref[...]).astype(jnp.bfloat16)
    col_sorted[:, 0:PACKED] = dot(dot(col_order, met).astype(jnp.bfloat16), far_ref[...]).astype(jnp.bfloat16)
    copy.wait()
    col_steps = spread(col_sorted, col_order, first_s, 8, col_x, col_owner, COLS)
    row_steps = spread(row_sorted, row_order, first_s, 0, row_x, row_owner, ROWS)

    pick = (NPROBE, LANES)
    pick_norm = ((iota(pick, 1) >= NORM_AT) & (iota(pick, 1) < ALPHA_AT)).astype(jnp.bfloat16)
    pick_alpha = ((iota(pick, 1) >= ALPHA_AT) & (iota(pick, 1) < STRIDE)).astype(jnp.bfloat16)
    both = (2 * NPROBE, LANES)
    pick_probe = (iota(both, 1) == iota(both, 0) + PROBE_AT).astype(jnp.bfloat16)
    probes = dot(pick_probe, col_tail.astype(jnp.bfloat16), NT).astype(jnp.bfloat16)

    def turn(step, unused):
        here = pl.ds(pl.multiple_of(step * COLS, COLS), COLS)
        mine = dot(probes, col_owner[here, :], NT)
        alpha = dot(pick_alpha, col_x[here, :], NT)
        col_u[:, here] = (alpha * (mine[:NPROBE] + mine[NPROBE:])).astype(jnp.bfloat16)
        return unused

    lax.fori_loop(0, col_steps, turn, 0)
    product[...] = jnp.zeros_like(product)
    row_lane = iota((ROWS, LANES), 1)

    def one_row(row, unused):
        rows = pl.ds(pl.multiple_of(row * ROWS, ROWS), ROWS)
        x_rows = row_x[rows, :]
        norm = dot(pick_norm, x_rows, NT)[0:1]
        alpha = dot(pick_alpha, x_rows, NT)
        x_rows = jnp.where(
            row_lane < NORM_AT, x_rows, jnp.where(row_lane < ALPHA_AT, jnp.bfloat16(1), jnp.bfloat16(0))
        )

        def one_col(col, total):
            here = pl.ds(pl.multiple_of(col * COLS, COLS), COLS)
            inner = dot(col_x[here, :], x_rows, NT)
            energy = jnp.exp2((inner + norm) * SCALE).astype(jnp.bfloat16)
            return total + dot(col_u[:, here], energy)

        total = lax.fori_loop(0, col_steps, one_col, jnp.zeros((NPROBE, ROWS), jnp.float32))
        weighted = jnp.concatenate(parts(total * alpha), axis=0).astype(jnp.bfloat16)
        sums = dot(weighted, row_owner[rows, :])
        product[...] += sums[0:NPROBE] + sums[NPROBE : 2 * NPROBE] + sums[2 * NPROBE :]
        return unused

    lax.fori_loop(0, row_steps, one_row, 0)
    out_ref[...] = product[...].T


def local_terms(plan, mine, near, far, images):
    meetings = plan.shape[0]
    rows, reach = sum(a.shape[0] for a in near), sum(a.shape[0] for a in far)
    cols = images * meetings
    room = lambda number, size: (number * P_SIZE + 15) // size * size + size + number + size
    return pl.pallas_call(
        functools.partial(energies, images, meetings, (len(near), len(far))),
        out_shape=jax.ShapeDtypeStruct((rows, NPROBE), jnp.float32),
        in_specs=[SMEM, SMEM] + [ANY] * (len(near) + len(far)),
        out_specs=VMEM,
        scratch_shapes=[
            pltpu.VMEM((rows, PACKED), jnp.bfloat16),
            pltpu.VMEM((reach, PACKED), jnp.bfloat16),
            pltpu.VMEM((rows, PACKED + LANES), jnp.bfloat16),
            pltpu.VMEM((cols, PACKED + LANES), jnp.bfloat16),
            pltpu.VMEM((room(rows, ROWS), LANES), jnp.bfloat16),
            pltpu.VMEM((room(cols, COLS), LANES), jnp.bfloat16),
            pltpu.VMEM((room(rows, ROWS), rows), jnp.bfloat16),
            pltpu.VMEM((room(cols, COLS), cols), jnp.bfloat16),
            pltpu.VMEM((NPROBE, room(cols, COLS)), jnp.bfloat16),
            pltpu.VMEM((NPROBE, rows), jnp.float32),
            pltpu.VMEM((16, LANES), jnp.int32),
            pltpu.SMEM((16, LANES), jnp.int32),
            pltpu.SemaphoreType.DMA,
            pltpu.SemaphoreType.DMA((len(near),)),
            pltpu.SemaphoreType.DMA((len(far),)),
        ],
        compiler_params=pltpu.CompilerParams(vmem_limit_bytes=52 * 2**20),
        name="energies",
    )(plan, mine, *near, *far)


def shards(patches, counts, weights, probes, plan):
    images = patches.shape[0]
    packed = pack(patches, counts, weights, probes)
    groups, subs = lax.axis_size("group"), lax.axis_size("narrow")

    def swap(array, apart):
        return lax.ppermute(array, "group", [(i, i ^ apart) for i in range(groups)])

    def turn(array, step):
        return lax.ppermute(array, "narrow", [(i, (i + step) % subs) for i in range(subs)])

    even = [packed] + [swap(packed, apart) for apart in range(2, groups, 2)]
    far = even + [swap(array, 1) for array in even]
    near = [packed] + [turn(packed, step) for step in range(1, subs)]
    mine = lax.axis_index("group").reshape(1)
    terms = local_terms(plan, mine, near, far, images)
    total = terms[:images]
    for step in range(1, subs):
        total = total + turn(terms[step * images : (step + 1) * images], -step)
    return total


def solution(mesh):
    return jax.shard_map(
        shards,
        mesh=mesh,
        in_specs=(
            P(("group", "narrow"), None),
            P(("group", "narrow")),
            P(),
            P(("group", "narrow"), None),
            P(),
        ),
        out_specs=P(("group", "narrow"), None),
        check_vma=False,
    )
```

profile of v0, /device:TPU:4, one launch (start us, length us, event | category | flops | bytes accessed | tf_op | source)
XLA Modules:
  0.0 44.4 jit_solution(9361721072658596249)
XLA Ops:
  0.0 2.1 %pack.1.refs_2_.refs_6_ = bf16[16,3968]{1,0:T(8,128)(2,1)} custom-call(bf16[16,3675]{1,0:T(8,128)(2,1)} %patches_ref.1, s32[1,16]{1,0:T(1,128)} %bitcast.3, f32[1,49]{1,0:T(1,128)} %bitcast.4, f32[16,16]{1,0:T(8,128)} %probes_ref.1), custom_call_target="tpu_custom_call" | custom-call | tf_op jit(solution)/shard_map/pack/pallas_call | solution.py:98
  2.1 0.0 collective-permute-start.6
  2.1 1.4 %collective-permute-start.5 = (bf16[16,3968]{1,0:T(8,128)(2,1)}, bf16[16,3968]{1,0:T(8,128)(2,1)S(1)}, u32[]{:S(2)}, u32[]{:S(2)}) collective-permute-start(bf16[16,3968]{1,0:T(8,128)(2,1)} %pack.1.refs_2_.refs_6_), channel_id=1, source_target_pairs={{0,24},{4,28},{8,16},{12,20},{16,8},{20,12},{24,0},{28,4},{1,25},{... | collective-permute-start | bytes 380936 | tf_op jit(solution)/shard_map/ppermute | solution.py:265
  3.5 1.5 %collective-permute-start.4 = (bf16[16,3968]{1,0:T(8,128)(2,1)}, bf16[16,3968]{1,0:T(8,128)(2,1)S(1)}, u32[]{:S(2)}, u32[]{:S(2)}) collective-permute-start(bf16[16,3968]{1,0:T(8,128)(2,1)} %pack.1.refs_2_.refs_6_), channel_id=1, source_target_pairs={{0,16},{4,20},{8,24},{12,28},{16,0},{20,4},{24,8},{28,12},{1,17},{... | collective-permute-start | bytes 380936 | tf_op jit(solution)/shard_map/ppermute | solution.py:265
  5.0 0.5 %collective-permute-start.3 = (bf16[16,3968]{1,0:T(8,128)(2,1)}, bf16[16,3968]{1,0:T(8,128)(2,1)S(1)}, u32[]{:S(2)}, u32[]{:S(2)}) collective-permute-start(bf16[16,3968]{1,0:T(8,128)(2,1)} %pack.1.refs_2_.refs_6_), channel_id=1, source_target_pairs={{0,8},{4,12},{8,0},{12,4},{16,24},{20,28},{24,16},{28,20},{1,9},{5... | collective-permute-start | bytes 380936 | tf_op jit(solution)/shard_map/ppermute | solution.py:265
  5.6 3.6 %collective-permute-start.2 = (bf16[16,3968]{1,0:T(8,128)(2,1)}, bf16[16,3968]{1,0:T(8,128)(2,1)S(1)}, u32[]{:S(2)}, u32[]{:S(2)}) collective-permute-start(bf16[16,3968]{1,0:T(8,128)(2,1)} %pack.1.refs_2_.refs_6_), channel_id=1, source_target_pairs={{0,3},{1,0},{2,1},{3,2},{4,7},{5,4},{6,5},{7,6},{8,11},{9,8},{10,9... | collective-permute-start | bytes 380936 | tf_op jit(solution)/shard_map/ppermute | solution.py:268
  9.2 0.0 collective-permute-start.1
  9.2 0.3 collective-permute-done.5.refs_9_
  9.4 1.6 %collective-permute-start = (bf16[16,3968]{1,0:T(8,128)(2,1)}, bf16[16,3968]{1,0:T(8,128)(2,1)S(1)}, u32[]{:S(2)}, u32[]{:S(2)}) collective-permute-start(bf16[16,3968]{1,0:T(8,128)(2,1)} %pack.1.refs_2_.refs_6_), channel_id=1, source_target_pairs={{0,1},{1,2},{2,3},{3,0},{4,5},{5,6},{6,7},{7,4},{8,9},{9,10},{10,1... | collective-permute-start | bytes 380936 | tf_op jit(solution)/shard_map/ppermute | solution.py:268
  11.0 0.7 %collective-permute-done.4.refs_8_ = bf16[16,3968]{1,0:T(8,128)(2,1)S(1)} collective-permute-done((bf16[16,3968]{1,0:T(8,128)(2,1)}, bf16[16,3968]{1,0:T(8,128)(2,1)S(1)}, u32[]{:S(2)}, u32[]{:S(2)}) %collective-permute-start.4) | collective-permute-done | bytes 127008 | tf_op jit(solution)/shard_map/ppermute | solution.py:265
  11.7 0.0 collective-permute-start.9
  11.8 0.0 collective-permute-done.3.refs_7_
  11.8 0.5 %collective-permute-start.8 = (bf16[16,3968]{1,0:T(8,128)(2,1)S(1)}, bf16[16,3968]{1,0:T(8,128)(2,1)S(1)}, u32[]{:S(2)}, u32[]{:S(2)}) collective-permute-start(bf16[16,3968]{1,0:T(8,128)(2,1)S(1)} %collective-permute-done.4.refs_8_), channel_id=1, source_target_pairs={{0,4},{4,0},{8,12},{12,8},{16,20},{20,16},{24,28},{28,24},{1,5},{5... | collective-permute-start | bytes 380936 | tf_op jit(solution)/shard_map/ppermute | solution.py:265
  12.3 1.1 %collective-permute-done.2.refs_5_ = bf16[16,3968]{1,0:T(8,128)(2,1)S(1)} collective-permute-done((bf16[16,3968]{1,0:T(8,128)(2,1)}, bf16[16,3968]{1,0:T(8,128)(2,1)S(1)}, u32[]{:S(2)}, u32[]{:S(2)}) %collective-permute-start.2) | collective-permute-done | bytes 127008 | tf_op jit(solution)/shard_map/ppermute | solution.py:268
  13.3 0.0 collective-permute-start.7
  13.3 6.7 %collective-permute-done.1.refs_4_ = bf16[16,3968]{1,0:T(8,128)(2,1)S(1)} collective-permute-done((bf16[16,3968]{1,0:T(8,128)(2,1)}, bf16[16,3968]{1,0:T(8,128)(2,1)S(1)}, u32[]{:S(2)}, u32[]{:S(2)}) %collective-permute-start.1) | collective-permute-done | bytes 127008 | tf_op jit(solution)/shard_map/ppermute | solution.py:268
  20.0 0.0 collective-permute-done.7.refs_11_
  20.1 0.9 %copy-done = bf16[16,3968]{1,0:T(8,128)(2,1)S(1)} copy-done((bf16[16,3968]{1,0:T(8,128)(2,1)S(1)}, bf16[16,3968]{1,0:T(8,128)(2,1)}, u32[]{:S(2)}) %copy-start) | copy-done | bytes 127000
  21.0 13.7 %energies.1 = f32[64,16]{1,0:T(8,128)S(1)} custom-call(s32[4,8]{1,0:T(4,128)S(1)} %copy-done.1, s32[1]{0:T(128)} %bitcast.refs_1_, bf16[16,3968]{1,0:T(8,128)(2,1)S(1)} %copy-done, bf16[16,3968]{1,0:T(8,128)(2,1)S(1)} %collective-permute-done.refs_3_, bf16[16,3968]{1,0:T(8,128)(2,1)S(1)} %collective-permute-done.1.refs_4_, ...), custom_call_target="tpu_custom_call" | custom-call | tf_op jit(solution)/shard_map/energies/pallas_call | solution.py:232
  34.7 3.7 %collective-permute-start.10 = (f32[16,16]{1,0:T(8,128)S(1)}, f32[16,16]{1,0:T(8,128)S(1)}, u32[]{:S(2)}, u32[]{:S(2)}) collective-permute-start(f32[16,16]{1,0:T(8,128)S(1)} %get-tuple-element.5), channel_id=1, source_target_pairs={{0,3},{1,0},{2,1},{3,2},{4,7},{5,4},{6,5},{7,6},{8,11},{9,8},{10,9... | collective-permute-start | bytes 3080 | tf_op jit(solution)/shard_map/ppermute | solution.py:268
  38.4 1.0 %collective-permute-start.11 = (f32[16,16]{1,0:T(8,128)S(1)}, f32[16,16]{1,0:T(8,128)S(1)}, u32[]{:S(2)}, u32[]{:S(2)}) collective-permute-start(f32[16,16]{1,0:T(8,128)S(1)} %get-tuple-element.7), channel_id=1, source_target_pairs={{0,2},{1,3},{2,0},{3,1},{4,6},{5,7},{6,4},{7,5},{8,10},{9,11},{10,... | collective-permute-start | bytes 3080 | tf_op jit(solution)/shard_map/ppermute | solution.py:268
  39.4 0.3 collective-permute-done.10
  39.7 4.1 %collective-permute-done.12 = f32[16,16]{1,0:T(8,128)S(1)} collective-permute-done((f32[16,16]{1,0:T(8,128)S(1)}, f32[16,16]{1,0:T(8,128)S(1)}, u32[]{:S(2)}, u32[]{:S(2)}) %collective-permute-start.12) | collective-permute-done | bytes 1056 | tf_op jit(solution)/shard_map/ppermute | solution.py:268
  43.8 0.6 %fusion.1 = f32[16,16]{1,0:T(8,128)} fusion(f32[16,16]{1,0:T(8,128)S(1)} %collective-permute-done.12, f32[16,16]{1,0:T(8,128)S(1)} %collective-permute-done.11, f32[16,16]{1,0:T(8,128)S(1)} %collective-permute-done.10, f32[64,16]{1,0:T(8,128)S(1)} %energies.1), kind=kLoop, calls=%fused_computation.2 | loop fusion | flops 768 | bytes 5120 | tf_op jit(solution)/shard_map/add | solution.py:277
  (10 shorter events, 0.0 us)
Async XLA Ops:
  2.1 7.1 %collective-permute-start.6 = (bf16[16,3968]{1,0:T(8,128)(2,1)}, bf16[16,3968]{1,0:T(8,128)(2,1)S(1)}, u32[]{:S(2)}, u32[]{:S(2)}) collective-permute-start(bf16[16,3968]{1,0:T(8,128)(2,1)} %pack.1.refs_2_.refs_6_), channel_id=1, source_target_pairs={{0,4},{4,0},{8,12},{12,8},{16,20},{20,16},{24,28},{28,24},{1,5},{5... | collective-permute-start | bytes 380936 | tf_op jit(solution)/shard_map/ppermute | solution.py:265
  2.1 7.4 %collective-permute-start.5 = (bf16[16,3968]{1,0:T(8,128)(2,1)}, bf16[16,3968]{1,0:T(8,128)(2,1)S(1)}, u32[]{:S(2)}, u32[]{:S(2)}) collective-permute-start(bf16[16,3968]{1,0:T(8,128)(2,1)} %pack.1.refs_2_.refs_6_), channel_id=1, source_target_pairs={{0,24},{4,28},{8,16},{12,20},{16,8},{20,12},{24,0},{28,4},{1,25},{... | collective-permute-start | bytes 380936 | tf_op jit(solution)/shard_map/ppermute | solution.py:265
  3.5 8.2 %collective-permute-start.4 = (bf16[16,3968]{1,0:T(8,128)(2,1)}, bf16[16,3968]{1,0:T(8,128)(2,1)S(1)}, u32[]{:S(2)}, u32[]{:S(2)}) collective-permute-start(bf16[16,3968]{1,0:T(8,128)(2,1)} %pack.1.refs_2_.refs_6_), channel_id=1, source_target_pairs={{0,16},{4,20},{8,24},{12,28},{16,0},{20,4},{24,8},{28,12},{1,17},{... | collective-permute-start | bytes 380936 | tf_op jit(solution)/shard_map/ppermute | solution.py:265
  5.0 6.7 %collective-permute-start.3 = (bf16[16,3968]{1,0:T(8,128)(2,1)}, bf16[16,3968]{1,0:T(8,128)(2,1)S(1)}, u32[]{:S(2)}, u32[]{:S(2)}) collective-permute-start(bf16[16,3968]{1,0:T(8,128)(2,1)} %pack.1.refs_2_.refs_6_), channel_id=1, source_target_pairs={{0,8},{4,12},{8,0},{12,4},{16,24},{20,28},{24,16},{28,20},{1,9},{5... | collective-permute-start | bytes 380936 | tf_op jit(solution)/shard_map/ppermute | solution.py:265
  5.6 7.8 %collective-permute-start.2 = (bf16[16,3968]{1,0:T(8,128)(2,1)}, bf16[16,3968]{1,0:T(8,128)(2,1)S(1)}, u32[]{:S(2)}, u32[]{:S(2)}) collective-permute-start(bf16[16,3968]{1,0:T(8,128)(2,1)} %pack.1.refs_2_.refs_6_), channel_id=1, source_target_pairs={{0,3},{1,0},{2,1},{3,2},{4,7},{5,4},{6,5},{7,6},{8,11},{9,8},{10,9... | collective-permute-start | bytes 380936 | tf_op jit(solution)/shard_map/ppermute | solution.py:268
  9.2 10.8 %collective-permute-start.1 = (bf16[16,3968]{1,0:T(8,128)(2,1)}, bf16[16,3968]{1,0:T(8,128)(2,1)S(1)}, u32[]{:S(2)}, u32[]{:S(2)}) collective-permute-start(bf16[16,3968]{1,0:T(8,128)(2,1)} %pack.1.refs_2_.refs_6_), channel_id=1, source_target_pairs={{0,2},{1,3},{2,0},{3,1},{4,6},{5,7},{6,4},{7,5},{8,10},{9,11},{10,... | collective-permute-start | bytes 380936 | tf_op jit(solution)/shard_map/ppermute | solution.py:268
  9.4 10.6 %collective-permute-start = (bf16[16,3968]{1,0:T(8,128)(2,1)}, bf16[16,3968]{1,0:T(8,128)(2,1)S(1)}, u32[]{:S(2)}, u32[]{:S(2)}) collective-permute-start(bf16[16,3968]{1,0:T(8,128)(2,1)} %pack.1.refs_2_.refs_6_), channel_id=1, source_target_pairs={{0,1},{1,2},{2,3},{3,0},{4,5},{5,6},{6,7},{7,4},{8,9},{9,10},{10,1... | collective-permute-start | bytes 380936 | tf_op jit(solution)/shard_map/ppermute | solution.py:268
  11.7 8.3 %collective-permute-start.9 = (bf16[16,3968]{1,0:T(8,128)(2,1)S(1)}, bf16[16,3968]{1,0:T(8,128)(2,1)S(1)}, u32[]{:S(2)}, u32[]{:S(2)}) collective-permute-start(bf16[16,3968]{1,0:T(8,128)(2,1)S(1)} %collective-permute-done.5.refs_9_), channel_id=1, source_target_pairs={{0,4},{4,0},{8,12},{12,8},{16,20},{20,16},{24,28},{28,24},{1,5},{5... | collective-permute-start | bytes 380936 | tf_op jit(solution)/shard_map/ppermute | solution.py:265
  11.8 8.3 %collective-permute-start.8 = (bf16[16,3968]{1,0:T(8,128)(2,1)S(1)}, bf16[16,3968]{1,0:T(8,128)(2,1)S(1)}, u32[]{:S(2)}, u32[]{:S(2)}) collective-permute-start(bf16[16,3968]{1,0:T(8,128)(2,1)S(1)} %collective-permute-done.4.refs_8_), channel_id=1, source_target_pairs={{0,4},{4,0},{8,12},{12,8},{16,20},{20,16},{24,28},{28,24},{1,5},{5... | collective-permute-start | bytes 380936 | tf_op jit(solution)/shard_map/ppermute | solution.py:265
  13.3 6.7 %collective-permute-start.7 = (bf16[16,3968]{1,0:T(8,128)(2,1)S(1)}, bf16[16,3968]{1,0:T(8,128)(2,1)S(1)}, u32[]{:S(2)}, u32[]{:S(2)}) collective-permute-start(bf16[16,3968]{1,0:T(8,128)(2,1)S(1)} %collective-permute-done.3.refs_7_), channel_id=1, source_target_pairs={{0,4},{4,0},{8,12},{12,8},{16,20},{20,16},{24,28},{28,24},{1,5},{5... | collective-permute-start | bytes 380936 | tf_op jit(solution)/shard_map/ppermute | solution.py:265
  13.3 6.7 %copy-start.1 = (s32[4,8]{1,0:T(4,128)S(1)}, s32[4,8]{1,0:T(4,128)}, u32[]{:S(2)}) copy-start(s32[4,8]{1,0:T(4,128)} %refs_0_.1) | copy-start | bytes 388
  20.1 0.9 %copy-start = (bf16[16,3968]{1,0:T(8,128)(2,1)S(1)}, bf16[16,3968]{1,0:T(8,128)(2,1)}, u32[]{:S(2)}) copy-start(bf16[16,3968]{1,0:T(8,128)(2,1)} %pack.1.refs_2_.refs_6_) | copy-start | bytes 380932
  34.7 5.1 %collective-permute-start.10 = (f32[16,16]{1,0:T(8,128)S(1)}, f32[16,16]{1,0:T(8,128)S(1)}, u32[]{:S(2)}, u32[]{:S(2)}) collective-permute-start(f32[16,16]{1,0:T(8,128)S(1)} %get-tuple-element.5), channel_id=1, source_target_pairs={{0,3},{1,0},{2,1},{3,2},{4,7},{5,4},{6,5},{7,6},{8,11},{9,8},{10,9... | collective-permute-start | bytes 3080 | tf_op jit(solution)/shard_map/ppermute | solution.py:268
  38.4 5.4 %collective-permute-start.12 = (f32[16,16]{1,0:T(8,128)S(1)}, f32[16,16]{1,0:T(8,128)S(1)}, u32[]{:S(2)}, u32[]{:S(2)}) collective-permute-start(f32[16,16]{1,0:T(8,128)S(1)} %get-tuple-element.6), channel_id=1, source_target_pairs={{0,1},{1,2},{2,3},{3,0},{4,5},{5,6},{6,7},{7,4},{8,9},{9,10},{10,1... | collective-permute-start | bytes 3080 | tf_op jit(solution)/shard_map/ppermute | solution.py:268
  38.4 5.4 %collective-permute-start.11 = (f32[16,16]{1,0:T(8,128)S(1)}, f32[16,16]{1,0:T(8,128)S(1)}, u32[]{:S(2)}, u32[]{:S(2)}) collective-permute-start(f32[16,16]{1,0:T(8,128)S(1)} %get-tuple-element.7), channel_id=1, source_target_pairs={{0,2},{1,3},{2,0},{3,1},{4,6},{5,7},{6,4},{7,5},{8,10},{9,11},{10,... | collective-permute-start | bytes 3080 | tf_op jit(solution)/shard_map/ppermute | solution.py:268
where the time goes:
time: 44.6 us; the launch traced here: 44.4 us
  Pallas kernels  15.8 us (35%)
  starting transfers between devices  13.9 us (31%)
  waiting for transfers between devices  13.2 us (30%)
  local copies, waits for them, and re-layouts  0.9 us (2%)
  other arithmetic  0.6 us (1%)
    pallas_call x1, Pallas kernels, local_terms(): pl.pallas_call(functools.partial(energies, images, meetings, (len(near),...  13.7 us
    ppermute x6, waiting for transfers between devices, turn(): lax.ppermute(array, 'narrow', [(i, (i + step) % subs) for i in range(subs)])  12.2 us
    ppermute x6, starting transfers between devices, turn(): lax.ppermute(array, 'narrow', [(i, (i + step) % subs) for i in range(subs)])  9.93 us
    ppermute x7, starting transfers between devices, swap(): return lax.ppermute(array, 'group', [(i, i ^ apart) for i in range(groups)])  4 us
    pallas_call x1, Pallas kernels, pack(): pl.pallas_call(pack_kernel, out_shape=jax.ShapeDtypeStruct((patches.shape...  2.08 us
    ppermute x7, waiting for transfers between devices, swap(): return lax.ppermute(array, 'group', [(i, i ^ apart) for i in range(groups)])  0.98 us
    unnamed x4, local copies, waits for them, and re-layouts  0.9 us
  transfers between devices with their start and end apart: 13, of which 6 were waited for; matrix products, arithmetic and copies ran while one was open for 0% of the time, Pallas kernels for 0%

commit v1 on v0

v1 whole, which is shorter than its diff:
```python
import functools
import math

import jax
import jax.numpy as jnp
from jax import lax
from jax.experimental import pallas as pl
from jax.experimental.pallas import tpu as pltpu
from jax.sharding import PartitionSpec as P

P_SIZE = 49
PV = 75
NPROBE = 16
LANES = 128
NORM_AT = PV
ALPHA_AT = PV + 3
FEATURES = 5
STRIDE = PV + FEATURES
WIDE = P_SIZE * STRIDE
PACKED = (WIDE + 1 + 2 * NPROBE + LANES - 1) // LANES * LANES
TAIL = WIDE // LANES * LANES
COUNT_AT = WIDE - TAIL
PROBE_AT = COUNT_AT + 1
OWNER_AT = STRIDE
ROWS = (1024, 256)
COLS = (1024, 256)
SCALE = 2.0 * math.log2(math.e) / (2.0 * PV)
NT = (((1,), (1,)), ((), ()))
NN = (((1,), (0,)), ((), ()))
VMEM = pl.BlockSpec(memory_space=pltpu.VMEM)
SMEM = pl.BlockSpec(memory_space=pltpu.SMEM)
HBM = pl.BlockSpec(memory_space=pltpu.HBM)


def dot(a, b, dims=NN):
    return lax.dot_general(a, b, dims, preferred_element_type=jnp.float32)


def iota(shape, dim):
    return lax.broadcasted_iota(jnp.int32, shape, dim)


def parts(value):
    hi = value.astype(jnp.bfloat16).astype(jnp.float32)
    rest = value - hi
    mid = rest.astype(jnp.bfloat16).astype(jnp.float32)
    return hi, mid, (rest - mid).astype(jnp.bfloat16).astype(jnp.float32)


def pack_kernel(mine_ref, *refs):
    sources, (out_ref, met_ref), targets, sem = refs[:5], refs[5:7], refs[7:12], refs[12]
    copies = [pltpu.make_async_copy(s, t, sem.at[k]) for k, (s, t) in enumerate(zip(sources, targets))]
    for copy in copies:
        copy.start()
    for copy in copies:
        copy.wait()
    patches_ref, counts_ref, weights_ref, probes_ref, plan_ref = targets
    images, wide = patches_ref.shape
    cols, far = met_ref.shape
    plan = plan_ref[...]
    mine = mine_ref[0]
    partner = jnp.sum(jnp.where(iota(plan.shape, 1) == mine, plan, 0), axis=1, keepdims=True)
    line = iota((cols, far), 0)
    source = jnp.zeros((cols, far), jnp.int32)
    for meeting in range(plan.shape[0]):
        here = (line >= meeting * images) & (line < (meeting + 1) * images)
        apart = partner[meeting : meeting + 1, :] ^ mine
        slot = (apart & 1) * (far // images // 2) + (apart >> 1)
        source = jnp.where(here, slot * images + line - meeting * images, source)
    met_ref[...] = (iota((cols, far), 1) == source).astype(jnp.bfloat16)

    shape = (images, LANES)
    lane = iota(shape, 1)
    square = (images, images)
    along = jnp.broadcast_to(counts_ref[...].astype(jnp.float32), square)
    count = jnp.sum(jnp.where(iota(square, 0) == iota(square, 1), along, 0.0), axis=1, keepdims=True)
    weight = jnp.concatenate([weights_ref[...], jnp.zeros((1, LANES - P_SIZE), jnp.float32)], axis=1)
    alpha = weight * (lane.astype(jnp.float32) < count).astype(jnp.float32) / count
    patches = []
    for p in range(P_SIZE):
        values = patches_ref[:, p * PV : min(p * PV + LANES, wide)]
        if values.shape[1] < LANES:
            values = jnp.concatenate([values, jnp.zeros((images, LANES - values.shape[1]), jnp.bfloat16)], axis=1)
        patches.append(jnp.where(lane < PV, values, jnp.bfloat16(0)))
    stacked = jnp.concatenate(patches, axis=0).astype(jnp.float32)
    squares = stacked * stacked
    ones = jnp.ones((LANES, LANES), jnp.bfloat16)
    high = squares.astype(jnp.bfloat16)
    norm = dot(high, ones) + dot((squares - high.astype(jnp.float32)).astype(jnp.bfloat16), ones)
    norms = [part.astype(jnp.bfloat16) for part in parts(-0.5 * norm)]
    alphas = [part.astype(jnp.bfloat16) for part in parts(alpha)[:2]]
    tiles = [None] * (PACKED // LANES)

    def put(values, start):
        tile, shift = divmod(start, LANES)
        moved = pltpu.roll(values, shift, 1) if shift else values
        first = jnp.where(lane >= shift, moved, jnp.bfloat16(0)) if shift else moved
        tiles[tile] = first if tiles[tile] is None else tiles[tile] + first
        if shift and tile + 1 < len(tiles):
            tiles[tile + 1] = jnp.where(lane < shift, moved, jnp.bfloat16(0))

    for p in range(P_SIZE):
        values = patches[p]
        for step, part in enumerate(norms):
            values = jnp.where(lane == NORM_AT + step, part[p * images : (p + 1) * images], values)
        for step, part in enumerate(alphas):
            values = jnp.where(lane == ALPHA_AT + step, pltpu.roll(part, (ALPHA_AT + step - p) % LANES, 1), values)
        put(values, p * STRIDE)
    probe_hi, probe_low, unused = parts(probes_ref[...])
    rest = jnp.concatenate(
        [count, probe_hi, probe_low, jnp.zeros((images, LANES - 1 - 2 * NPROBE), jnp.float32)], axis=1
    )
    put(rest.astype(jnp.bfloat16), WIDE)
    for tile, values in enumerate(tiles):
        out_ref[:, tile * LANES : (tile + 1) * LANES] = values


def pack(patches, counts, weights, probes, plan, mine):
    images = patches.shape[0]
    given = (patches, counts[None, :], weights[None, :], probes, plan)
    return pl.pallas_call(
        pack_kernel,
        out_shape=(
            jax.ShapeDtypeStruct((images, PACKED), jnp.bfloat16),
            jax.ShapeDtypeStruct((images * plan.shape[0], images * plan.shape[1]), jnp.bfloat16),
        ),
        in_specs=[SMEM] + [HBM] * len(given),
        out_specs=(VMEM, VMEM),
        scratch_shapes=[pltpu.VMEM(a.shape, a.dtype) for a in given] + [pltpu.SemaphoreType.DMA((len(given),))],
        compiler_params=pltpu.CompilerParams(vmem_limit_bytes=8 * 2**20),
        name="pack",
    )(mine, *given)


def order(tail):
    number = tail.shape[0]
    count = tail[:, COUNT_AT : COUNT_AT + 1]
    key = count * number + (number - 1 - iota((number, 1), 0)).astype(jnp.float32)
    square = (number, number)
    key_here = jnp.broadcast_to(key, square)
    key_along = jnp.sum(jnp.where(iota(square, 0) == iota(square, 1), key_here, 0.0), axis=0, keepdims=True)
    rank = jnp.sum((key_here > key_along).astype(jnp.float32), axis=0, keepdims=True)
    chosen = (iota(square, 0).astype(jnp.float32) == rank).astype(jnp.bfloat16)
    patch = iota((number, LANES), 1).astype(jnp.float32)
    valid = jnp.sum((count > patch).astype(jnp.float32), axis=0, keepdims=True)
    before = (iota((LANES, LANES), 0) < iota((LANES, LANES), 1)).astype(jnp.bfloat16)
    first = dot(jnp.broadcast_to(valid, (8, LANES)).astype(jnp.bfloat16), before)
    return chosen, first.astype(jnp.int32)


def spread(sorted_ref, chosen, first_ref, at, x_ref, room):
    number = sorted_ref.shape[0]
    lane = iota((number, LANES), 1)
    owner = jnp.sum(jnp.where(chosen > 0, iota((number, number), 1).astype(jnp.float32), 0.0), axis=1, keepdims=True)
    owner = jnp.where(lane == OWNER_AT, owner, 0.0)
    for p in range(P_SIZE):
        values = jnp.where(lane < STRIDE, sorted_ref[:, p * STRIDE : p * STRIDE + LANES], owner)
        x_ref[pl.ds(first_ref[at, p], number), :] = values
    total = first_ref[at, P_SIZE]
    x_ref[pl.ds(total, room), :] = jnp.zeros((room, LANES), jnp.float32)
    return total


def cover(total, sizes, step, carry):
    large, small = sizes
    number = (total + large - small) // large
    carry = lax.fori_loop(0, number, lambda k, c: step(pl.multiple_of(k * large, large), large, c), carry)
    rest = (total - number * large + small - 1) // small
    start = pl.multiple_of(number * large, large)
    return lax.fori_loop(0, rest, lambda k, c: step(start, small, c), carry)


def rank_kernel(*refs):
    chosen_ref, first_ref = refs[-2:]
    tail = jnp.concatenate([part[:, TAIL : TAIL + LANES] for part in refs[:-2]], axis=0)
    chosen, first = order(tail.astype(jnp.float32))
    chosen_ref[...] = chosen
    first_ref[...] = first


def rank(near):
    images = sum(a.shape[0] for a in near)
    return pl.pallas_call(
        rank_kernel,
        out_shape=(jax.ShapeDtypeStruct((images, images), jnp.bfloat16), jax.ShapeDtypeStruct((8, LANES), jnp.int32)),
        in_specs=[VMEM] * len(near),
        out_specs=(VMEM, VMEM),
        compiler_params=pltpu.CompilerParams(vmem_limit_bytes=8 * 2**20),
        cost_estimate=pl.CostEstimate(flops=2 * 10**10, bytes_accessed=10**6, transcendentals=0),
        name="rank",
    )(*near)


def energies(counted, *refs):
    near_number, far_number = counted
    row_first, row_order, met_ref = refs[:3]
    near_parts = refs[3 : 3 + near_number]
    far_parts = refs[3 + near_number : 3 + near_number + far_number]
    (out_ref, row_sorted, col_sorted, row_x, col_f, col_x, col_u, product, first_v, first_s, sem) = refs[
        3 + near_number + far_number :
    ]
    cols = met_ref.shape[0]
    met = met_ref[...]
    for target in (row_sorted, col_sorted):
        target[:, PACKED:] = jnp.zeros((target.shape[0], LANES), jnp.float32)
    tails = jnp.concatenate([part[:, TAIL : TAIL + LANES] for part in far_parts], axis=0)
    col_tail = dot(met, tails)
    col_order, col_first = order(col_tail)
    first_v[...] = col_first
    copy = pltpu.make_async_copy(first_v, first_s, sem)
    copy.start()
    row_sorted[:, 0:PACKED] = dot(row_order[...], jnp.concatenate([part[...] for part in near_parts], axis=0))
    col_chosen = dot(col_order, met).astype(jnp.bfloat16)
    col_sorted[:, 0:PACKED] = dot(col_chosen, jnp.concatenate([part[...] for part in far_parts], axis=0))
    row_total = spread(row_sorted, row_order[...], row_first, 0, row_x, ROWS[0])
    copy.wait()
    col_total = spread(col_sorted, col_order, first_s, 0, col_f, COLS[0])

    line, lane = iota((NPROBE, LANES), 0), iota((NPROBE, LANES), 1)
    pick = (
        ((line == 0) & (lane >= NORM_AT) & (lane < ALPHA_AT))
        | ((line == 1) & (lane >= ALPHA_AT) & (lane < STRIDE))
        | ((line == 2) & (lane == OWNER_AT))
    ).astype(jnp.bfloat16)
    both = (2 * NPROBE, LANES)
    pick_probe = (iota(both, 1) == iota(both, 0) + PROBE_AT).astype(jnp.bfloat16)
    probes = dot(pick_probe, col_tail.astype(jnp.bfloat16), NT).astype(jnp.bfloat16)

    def owned(picked, number, size):
        return (iota((number, size), 0).astype(jnp.float32) == picked[2:3]).astype(jnp.bfloat16)

    def prepare(start, size, unused):
        here = pl.ds(start, size)
        x_cols = col_f[here, :].astype(jnp.bfloat16)
        col_x[here, :] = x_cols
        picked = dot(pick, x_cols, NT)
        mine = dot(probes, owned(picked, cols, size))
        col_u[:, here] = (picked[1:2] * (mine[:NPROBE] + mine[NPROBE:])).astype(jnp.bfloat16)
        return unused

    cover(col_total, COLS, prepare, 0)
    product[...] = jnp.zeros_like(product)

    def one_row(start, size, unused):
        x_rows = row_x[pl.ds(start, size), :].astype(jnp.bfloat16)
        picked = dot(pick, x_rows, NT)
        row_lane = iota((size, LANES), 1)
        x_rows = jnp.where(
            row_lane < NORM_AT, x_rows, jnp.where(row_lane < ALPHA_AT, jnp.bfloat16(1), jnp.bfloat16(0))
        )

        def one_col(start, size, total):
            here = pl.ds(start, size)
            inner = dot(col_x[here, :], x_rows, NT)
            energy = jnp.exp2((inner + picked[0:1]) * SCALE).astype(jnp.bfloat16)
            return total + dot(col_u[:, here], energy)

        total = cover(col_total, COLS, one_col, jnp.zeros((NPROBE, size), jnp.float32))
        weighted = jnp.concatenate(parts(total * picked[1:2]), axis=0).astype(jnp.bfloat16)
        sums = dot(weighted, owned(picked, product.shape[1], size), NT)
        product[...] += sums[0:NPROBE] + sums[NPROBE : 2 * NPROBE] + sums[2 * NPROBE :]
        return unused

    cover(row_total, ROWS, one_row, 0)
    out_ref[...] = product[...].T


def local_terms(met, ranked, near, far):
    row_order, row_first = ranked
    rows, cols = row_order.shape[0], met.shape[0]
    row_room = rows * P_SIZE + rows + ROWS[0]
    col_room = (cols * P_SIZE + cols) // COLS[0] * COLS[0] + 2 * COLS[0]
    return pl.pallas_call(
        functools.partial(energies, (len(near), len(far))),
        out_shape=jax.ShapeDtypeStruct((rows, NPROBE), jnp.float32),
        in_specs=[SMEM] + [VMEM] * (2 + len(near) + len(far)),
        out_specs=VMEM,
        scratch_shapes=[
            pltpu.VMEM((rows, PACKED + LANES), jnp.float32),
            pltpu.VMEM((cols, PACKED + LANES), jnp.float32),
            pltpu.VMEM((row_room, LANES), jnp.float32),
            pltpu.VMEM((col_room, LANES), jnp.float32),
            pltpu.VMEM((col_room, LANES), jnp.bfloat16),
            pltpu.VMEM((NPROBE, col_room), jnp.bfloat16),
            pltpu.VMEM((NPROBE, rows), jnp.float32),
            pltpu.VMEM((8, LANES), jnp.int32),
            pltpu.SMEM((8, LANES), jnp.int32),
            pltpu.SemaphoreType.DMA,
        ],
        compiler_params=pltpu.CompilerParams(vmem_limit_bytes=40 * 2**20),
        name="energies",
    )(row_first, row_order, met, *near, *far)


def shards(patches, counts, weights, probes, plan):
    images = patches.shape[0]
    mine = lax.axis_index("group").reshape(1)
    packed, met = pack(patches, counts, weights, probes, plan, mine)
    groups, subs = lax.axis_size("group"), lax.axis_size("narrow")

    def swap(array, apart):
        return lax.ppermute(array, "group", [(i, i ^ apart) for i in range(groups)])

    def across(array, apart):
        return lax.ppermute(array, "narrow", [(i, i ^ apart) for i in range(subs)])

    even = [packed] + [swap(packed, apart) for apart in range(2, groups, 2)]
    far = even + [swap(array, 1) for array in even]
    near = [packed]
    for apart in range(1, subs):
        low = apart & -apart
        near.append(across(near[apart - low], low))
    terms = local_terms(met, rank(near), near, far)
    total = terms[:images]
    for apart in range(1, subs):
        total = total + across(terms[apart * images : (apart + 1) * images], apart)
    return total


def solution(mesh):
    return jax.shard_map(
        shards,
        mesh=mesh,
        in_specs=(
            P(("group", "narrow"), None),
            P(("group", "narrow")),
            P(),
            P(("group", "narrow"), None),
            P(),
        ),
        out_specs=P(("group", "narrow"), None),
        check_vma=False,
    )
```

time: 44.6 us -> 35.6 us (0.80)
  the two profiles are of different devices: /device:TPU:4 before, /device:TPU:0 now
where the time goes in v1:
time: 35.6 us; the launch traced here: 35.4 us
  starting transfers between devices  14.4 us (40%)
  waiting for transfers between devices  9.71 us (27%)
  Pallas kernels  9.06 us (25%)
  local copies, waits for them, and re-layouts  1.6 us (4%)
  other arithmetic  0.6 us (2%)
    ppermute x6, starting transfers between devices, across(): return lax.ppermute(array, 'narrow', [(i, i ^ apart) for i in range(subs)])  10.5 us
    pallas_call x1, Pallas kernels, local_terms(): pl.pallas_call(functools.partial(energies, (len(near), len(far))), out_sh...  8.17 us
    ppermute x6, waiting for transfers between devices, across(): return lax.ppermute(array, 'narrow', [(i, i ^ apart) for i in range(subs)])  8 us
    ppermute x7, starting transfers between devices, swap(): return lax.ppermute(array, 'group', [(i, i ^ apart) for i in range(groups)])  3.9 us
    ppermute x7, waiting for transfers between devices, swap(): return lax.ppermute(array, 'group', [(i, i ^ apart) for i in range(groups)])  1.7 us
    unnamed x10, local copies, waits for them, and re-layouts  1.6 us
  transfers between devices with their start and end apart: 13, of which 7 were waited for; matrix products, arithmetic and copies ran while one was open for 0% of the time, Pallas kernels for 1%

profile of v1, /device:TPU:0, one launch (start us, length us, event | category | flops | bytes accessed | tf_op | source)
XLA Modules:
  0.0 35.4 jit_solution(4142557428597331347)
XLA Ops:
  0.0 0.7 %copy-done.1 = f32[16,16]{1,0:T(8,128)S(1)} copy-done((f32[16,16]{1,0:T(8,128)S(1)}, f32[16,16]{1,0:T(8,128)}, u32[]{:S(2)}) %copy-start.1) | copy-done | bytes 1048
  0.7 0.9 %copy-done = bf16[16,3675]{1,0:T(8,128)(2,1)S(1)} copy-done((bf16[16,3675]{1,0:T(8,128)(2,1)S(1)}, bf16[16,3675]{1,0:T(8,128)(2,1)}, u32[]{:S(2)}) %copy-start) | copy-done | bytes 117624
  1.6 0.7 %pack.1 = (bf16[16,3968]{1,0:T(8,128)(2,1)S(1)}, bf16[64,128]{1,0:T(8,128)(2,1)S(1)}) custom-call(s32[1]{0:T(128)} %bitcast.mine_ref, bf16[16,3675]{1,0:T(8,128)(2,1)S(1)} %copy-done, s32[1,16]{1,0:T(1,128)S(1)} %bitcast.3, f32[1,49]{1,0:T(1,128)S(1)} %bitcast.4, f32[16,16]{1,0:T(8,128)S(1)} %copy-done.1, s32[4,8]{1,0:T(4,128)S(1)} %copy-done.2), custom_call_target="tpu_custom_call" | custom-call | tf_op jit(solution)/shard_map/pack/pallas_call | solution.py:121
  2.3 4.1 %collective-permute-start.1 = (bf16[16,3968]{1,0:T(8,128)(2,1)S(1)}, bf16[16,3968]{1,0:T(8,128)(2,1)S(1)}, u32[]{:S(2)}, u32[]{:S(2)}) collective-permute-start(bf16[16,3968]{1,0:T(8,128)(2,1)S(1)} %get-tuple-element.9.refs_0_.refs_3_.refs_7_), channel_id=1, source_target_pairs={{0,2},{1,3},{2,0},{3,1},{4,6},{5,7},{6,4},{7,5},{8,10},{9,11},{10,... | collective-permute-start | bytes 380936 | tf_op jit(solution)/shard_map/ppermute | solution.py:305
  6.4 2.4 %collective-permute-start.5 = (bf16[16,3968]{1,0:T(8,128)(2,1)S(1)}, bf16[16,3968]{1,0:T(8,128)(2,1)S(1)}, u32[]{:S(2)}, u32[]{:S(2)}) collective-permute-start(bf16[16,3968]{1,0:T(8,128)(2,1)S(1)} %get-tuple-element.9.refs_0_.refs_3_.refs_7_), channel_id=1, source_target_pairs={{0,24},{4,28},{8,16},{12,20},{16,8},{20,12},{24,0},{28,4},{1,25},{... | collective-permute-start | bytes 380936 | tf_op jit(solution)/shard_map/ppermute | solution.py:302
  8.9 0.5 %collective-permute-start.4 = (bf16[16,3968]{1,0:T(8,128)(2,1)S(1)}, bf16[16,3968]{1,0:T(8,128)(2,1)S(1)}, u32[]{:S(2)}, u32[]{:S(2)}) collective-permute-start(bf16[16,3968]{1,0:T(8,128)(2,1)S(1)} %get-tuple-element.9.refs_0_.refs_3_.refs_7_), channel_id=1, source_target_pairs={{0,16},{4,20},{8,24},{12,28},{16,0},{20,4},{24,8},{28,12},{1,17},{... | collective-permute-start | bytes 380936 | tf_op jit(solution)/shard_map/ppermute | solution.py:302
  9.4 0.5 %collective-permute-start.3 = (bf16[16,3968]{1,0:T(8,128)(2,1)S(1)}, bf16[16,3968]{1,0:T(8,128)(2,1)S(1)}, u32[]{:S(2)}, u32[]{:S(2)}) collective-permute-start(bf16[16,3968]{1,0:T(8,128)(2,1)S(1)} %get-tuple-element.9.refs_0_.refs_3_.refs_7_), channel_id=1, source_target_pairs={{0,8},{4,12},{8,0},{12,4},{16,24},{20,28},{24,16},{28,20},{1,9},{5... | collective-permute-start | bytes 380936 | tf_op jit(solution)/shard_map/ppermute | solution.py:302
  9.9 1.6 %collective-permute-start = (bf16[16,3968]{1,0:T(8,128)(2,1)S(1)}, bf16[16,3968]{1,0:T(8,128)(2,1)S(1)}, u32[]{:S(2)}, u32[]{:S(2)}) collective-permute-start(bf16[16,3968]{1,0:T(8,128)(2,1)S(1)} %get-tuple-element.9.refs_0_.refs_3_.refs_7_), channel_id=1, source_target_pairs={{0,1},{1,0},{2,3},{3,2},{4,5},{5,4},{6,7},{7,6},{8,9},{9,8},{10,11... | collective-permute-start | bytes 380936 | tf_op jit(solution)/shard_map/ppermute | solution.py:305
  11.5 1.2 %collective-permute-done.1.refs_2_.refs_5_ = bf16[16,3968]{1,0:T(8,128)(2,1)S(1)} collective-permute-done((bf16[16,3968]{1,0:T(8,128)(2,1)S(1)}, bf16[16,3968]{1,0:T(8,128)(2,1)S(1)}, u32[]{:S(2)}, u32[]{:S(2)}) %collective-permute-start.1) | collective-permute-done | bytes 127008 | tf_op jit(solution)/shard_map/ppermute | solution.py:305
  12.6 0.7 %collective-permute-start.2 = (bf16[16,3968]{1,0:T(8,128)(2,1)S(1)}, bf16[16,3968]{1,0:T(8,128)(2,1)S(1)}, u32[]{:S(2)}, u32[]{:S(2)}) collective-permute-start(bf16[16,3968]{1,0:T(8,128)(2,1)S(1)} %collective-permute-done.1.refs_2_.refs_5_), channel_id=1, source_target_pairs={{0,1},{1,0},{2,3},{3,2},{4,5},{5,4},{6,7},{7,6},{8,9},{9,8},{10,11... | collective-permute-start | bytes 380936 | tf_op jit(solution)/shard_map/ppermute | solution.py:305
  13.3 0.0 collective-permute-done.5.refs_10_
  13.3 1.6 %collective-permute-done.4.refs_9_ = bf16[16,3968]{1,0:T(8,128)(2,1)S(1)} collective-permute-done((bf16[16,3968]{1,0:T(8,128)(2,1)S(1)}, bf16[16,3968]{1,0:T(8,128)(2,1)S(1)}, u32[]{:S(2)}, u32[]{:S(2)}) %collective-permute-start.4) | collective-permute-done | bytes 127008 | tf_op jit(solution)/shard_map/ppermute | solution.py:302
  14.9 0.1 collective-permute-done.3.refs_8_
  15.0 0.4 %collective-permute-start.8 = (bf16[16,3968]{1,0:T(8,128)(2,1)S(1)}, bf16[16,3968]{1,0:T(8,128)(2,1)S(1)}, u32[]{:S(2)}, u32[]{:S(2)}) collective-permute-start(bf16[16,3968]{1,0:T(8,128)(2,1)S(1)} %collective-permute-done.4.refs_9_), channel_id=1, source_target_pairs={{0,4},{4,0},{8,12},{12,8},{16,20},{20,16},{24,28},{28,24},{1,5},{5... | collective-permute-start | bytes 380936 | tf_op jit(solution)/shard_map/ppermute | solution.py:302
  15.4 0.7 %collective-permute-done.refs_1_.refs_4_ = bf16[16,3968]{1,0:T(8,128)(2,1)S(1)} collective-permute-done((bf16[16,3968]{1,0:T(8,128)(2,1)S(1)}, bf16[16,3968]{1,0:T(8,128)(2,1)S(1)}, u32[]{:S(2)}, u32[]{:S(2)}) %collective-permute-start) | collective-permute-done | bytes 127008 | tf_op jit(solution)/shard_map/ppermute | solution.py:305
  16.1 1.9 %collective-permute-done.2.refs_3_.refs_6_ = bf16[16,3968]{1,0:T(8,128)(2,1)S(1)} collective-permute-done((bf16[16,3968]{1,0:T(8,128)(2,1)S(1)}, bf16[16,3968]{1,0:T(8,128)(2,1)S(1)}, u32[]{:S(2)}, u32[]{:S(2)}) %collective-permute-start.2) | collective-permute-done | bytes 127008 | tf_op jit(solution)/shard_map/ppermute | solution.py:305
  18.0 0.2 rank.1
  18.2 8.2 %energies.1 = f32[64,16]{1,0:T(8,128)S(1)} custom-call(s32[8,128]{1,0:T(8,128)S(1)} %get-tuple-element.10.refs_0_, bf16[64,64]{1,0:T(8,128)(2,1)S(1)} %get-tuple-element.11.refs_1_, bf16[64,128]{1,0:T(8,128)(2,1)S(1)} %get-tuple-element.12.refs_2_, bf16[16,3968]{1,0:T(8,128)(2,1)S(1)} %get-tuple-element.9.refs_0_.refs_3_.refs_7_, ...), custom_call_target="tpu_custom_call" | custom-call | tf_op jit(solution)/shard_map/energies/pallas_call | solution.py:273
  26.4 1.2 %collective-permute-start.10 = (f32[16,16]{1,0:T(8,128)S(1)}, f32[16,16]{1,0:T(8,128)S(1)}, u32[]{:S(2)}, u32[]{:S(2)}) collective-permute-start(f32[16,16]{1,0:T(8,128)S(1)} %get-tuple-element.13), channel_id=1, source_target_pairs={{0,1},{1,0},{2,3},{3,2},{4,5},{5,4},{6,7},{7,6},{8,9},{9,8},{10,11... | collective-permute-start | bytes 3080 | tf_op jit(solution)/shard_map/ppermute | solution.py:305
  27.6 2.6 %collective-permute-start.12 = (f32[16,16]{1,0:T(8,128)S(1)}, f32[16,16]{1,0:T(8,128)S(1)}, u32[]{:S(2)}, u32[]{:S(2)}) collective-permute-start(f32[16,16]{1,0:T(8,128)S(1)} %get-tuple-element.14), channel_id=1, source_target_pairs={{0,3},{1,2},{2,1},{3,0},{4,7},{5,6},{6,5},{7,4},{8,11},{9,10},{10,... | collective-permute-start | bytes 3080 | tf_op jit(solution)/shard_map/ppermute | solution.py:305
  30.2 0.3 collective-permute-start.11
  30.5 2.5 %collective-permute-done.12 = f32[16,16]{1,0:T(8,128)S(1)} collective-permute-done((f32[16,16]{1,0:T(8,128)S(1)}, f32[16,16]{1,0:T(8,128)S(1)}, u32[]{:S(2)}, u32[]{:S(2)}) %collective-permute-start.12) | collective-permute-done | bytes 1056 | tf_op jit(solution)/shard_map/ppermute | solution.py:305
  33.1 1.7 %collective-permute-done.11 = f32[16,16]{1,0:T(8,128)S(1)} collective-permute-done((f32[16,16]{1,0:T(8,128)S(1)}, f32[16,16]{1,0:T(8,128)S(1)}, u32[]{:S(2)}, u32[]{:S(2)}) %collective-permute-start.11) | collective-permute-done | bytes 1056 | tf_op jit(solution)/shard_map/ppermute | solution.py:305
  34.8 0.6 %fusion.1 = f32[16,16]{1,0:T(8,128)} fusion(f32[16,16]{1,0:T(8,128)S(1)} %collective-permute-done.12, f32[16,16]{1,0:T(8,128)S(1)} %collective-permute-done.11, f32[16,16]{1,0:T(8,128)S(1)} %collective-permute-done.10, f32[64,16]{1,0:T(8,128)S(1)} %energies.1), kind=kLoop, calls=%fused_computation.2 | loop fusion | flops 768 | bytes 5120 | tf_op jit(solution)/shard_map/add | solution.py:316
  (17 shorter events, 0.0 us)
Async XLA Ops:
  0.0 0.7 %copy-start.1 = (f32[16,16]{1,0:T(8,128)S(1)}, f32[16,16]{1,0:T(8,128)}, u32[]{:S(2)}) copy-start(f32[16,16]{1,0:T(8,128)} %refs_3_.1) | copy-start | bytes 3076
  0.0 0.7 %copy-start.2 = (s32[4,8]{1,0:T(4,128)S(1)}, s32[4,8]{1,0:T(4,128)}, u32[]{:S(2)}) copy-start(s32[4,8]{1,0:T(4,128)} %refs_4_.1) | copy-start | bytes 388
  0.0 0.7 %copy-start.3 = (s32[16]{0:T(128)S(1)}, s32[16]{0:T(128)}, u32[]{:S(2)}) copy-start(s32[16]{0:T(128)} %param.6) | copy-start | bytes 196
  0.0 0.7 %copy-start.4 = (f32[49]{0:T(128)S(1)}, f32[49]{0:T(128)}, u32[]{:S(2)}) copy-start(f32[49]{0:T(128)} %param.7) | copy-start | bytes 592
  0.7 0.9 %copy-start = (bf16[16,3675]{1,0:T(8,128)(2,1)S(1)}, bf16[16,3675]{1,0:T(8,128)(2,1)}, u32[]{:S(2)}) copy-start(bf16[16,3675]{1,0:T(8,128)(2,1)} %refs_0_.1) | copy-start | bytes 352804
  2.3 10.3 %collective-permute-start.1 = (bf16[16,3968]{1,0:T(8,128)(2,1)S(1)}, bf16[16,3968]{1,0:T(8,128)(2,1)S(1)}, u32[]{:S(2)}, u32[]{:S(2)}) collective-permute-start(bf16[16,3968]{1,0:T(8,128)(2,1)S(1)} %get-tuple-element.9.refs_0_.refs_3_.refs_7_), channel_id=1, source_target_pairs={{0,2},{1,3},{2,0},{3,1},{4,6},{5,7},{6,4},{7,5},{8,10},{9,11},{10,... | collective-permute-start | bytes 380936 | tf_op jit(solution)/shard_map/ppermute | solution.py:305
  6.4 6.9 %collective-permute-start.5 = (bf16[16,3968]{1,0:T(8,128)(2,1)S(1)}, bf16[16,3968]{1,0:T(8,128)(2,1)S(1)}, u32[]{:S(2)}, u32[]{:S(2)}) collective-permute-start(bf16[16,3968]{1,0:T(8,128)(2,1)S(1)} %get-tuple-element.9.refs_0_.refs_3_.refs_7_), channel_id=1, source_target_pairs={{0,24},{4,28},{8,16},{12,20},{16,8},{20,12},{24,0},{28,4},{1,25},{... | collective-permute-start | bytes 380936 | tf_op jit(solution)/shard_map/ppermute | solution.py:302
  8.9 6.0 %collective-permute-start.4 = (bf16[16,3968]{1,0:T(8,128)(2,1)S(1)}, bf16[16,3968]{1,0:T(8,128)(2,1)S(1)}, u32[]{:S(2)}, u32[]{:S(2)}) collective-permute-start(bf16[16,3968]{1,0:T(8,128)(2,1)S(1)} %get-tuple-element.9.refs_0_.refs_3_.refs_7_), channel_id=1, source_target_pairs={{0,16},{4,20},{8,24},{12,28},{16,0},{20,4},{24,8},{28,12},{1,17},{... | collective-permute-start | bytes 380936 | tf_op jit(solution)/shard_map/ppermute | solution.py:302
  9.4 5.6 %collective-permute-start.3 = (bf16[16,3968]{1,0:T(8,128)(2,1)S(1)}, bf16[16,3968]{1,0:T(8,128)(2,1)S(1)}, u32[]{:S(2)}, u32[]{:S(2)}) collective-permute-start(bf16[16,3968]{1,0:T(8,128)(2,1)S(1)} %get-tuple-element.9.refs_0_.refs_3_.refs_7_), channel_id=1, source_target_pairs={{0,8},{4,12},{8,0},{12,4},{16,24},{20,28},{24,16},{28,20},{1,9},{5... | collective-permute-start | bytes 380936 | tf_op jit(solution)/shard_map/ppermute | solution.py:302
  9.9 6.2 %collective-permute-start = (bf16[16,3968]{1,0:T(8,128)(2,1)S(1)}, bf16[16,3968]{1,0:T(8,128)(2,1)S(1)}, u32[]{:S(2)}, u32[]{:S(2)}) collective-permute-start(bf16[16,3968]{1,0:T(8,128)(2,1)S(1)} %get-tuple-element.9.refs_0_.refs_3_.refs_7_), channel_id=1, source_target_pairs={{0,1},{1,0},{2,3},{3,2},{4,5},{5,4},{6,7},{7,6},{8,9},{9,8},{10,11... | collective-permute-start | bytes 380936 | tf_op jit(solution)/shard_map/ppermute | solution.py:305
  12.6 5.3 %collective-permute-start.2 = (bf16[16,3968]{1,0:T(8,128)(2,1)S(1)}, bf16[16,3968]{1,0:T(8,128)(2,1)S(1)}, u32[]{:S(2)}, u32[]{:S(2)}) collective-permute-start(bf16[16,3968]{1,0:T(8,128)(2,1)S(1)} %collective-permute-done.1.refs_2_.refs_5_), channel_id=1, source_target_pairs={{0,1},{1,0},{2,3},{3,2},{4,5},{5,4},{6,7},{7,6},{8,9},{9,8},{10,11... | collective-permute-start | bytes 380936 | tf_op jit(solution)/shard_map/ppermute | solution.py:305
  13.3 4.9 %collective-permute-start.6 = (bf16[16,3968]{1,0:T(8,128)(2,1)S(1)}, bf16[16,3968]{1,0:T(8,128)(2,1)S(1)}, u32[]{:S(2)}, u32[]{:S(2)}) collective-permute-start(bf16[16,3968]{1,0:T(8,128)(2,1)S(1)} %get-tuple-element.9.refs_0_.refs_3_.refs_7_), channel_id=1, source_target_pairs={{0,4},{4,0},{8,12},{12,8},{16,20},{20,16},{24,28},{28,24},{1,5},{5... | collective-permute-start | bytes 380936 | tf_op jit(solution)/shard_map/ppermute | solution.py:302
  14.9 3.3 %collective-permute-start.9 = (bf16[16,3968]{1,0:T(8,128)(2,1)S(1)}, bf16[16,3968]{1,0:T(8,128)(2,1)S(1)}, u32[]{:S(2)}, u32[]{:S(2)}) collective-permute-start(bf16[16,3968]{1,0:T(8,128)(2,1)S(1)} %collective-permute-done.5.refs_10_), channel_id=1, source_target_pairs={{0,4},{4,0},{8,12},{12,8},{16,20},{20,16},{24,28},{28,24},{1,5},{5... | collective-permute-start | bytes 380936 | tf_op jit(solution)/shard_map/ppermute | solution.py:302
  15.0 3.2 %collective-permute-start.8 = (bf16[16,3968]{1,0:T(8,128)(2,1)S(1)}, bf16[16,3968]{1,0:T(8,128)(2,1)S(1)}, u32[]{:S(2)}, u32[]{:S(2)}) collective-permute-start(bf16[16,3968]{1,0:T(8,128)(2,1)S(1)} %collective-permute-done.4.refs_9_), channel_id=1, source_target_pairs={{0,4},{4,0},{8,12},{12,8},{16,20},{20,16},{24,28},{28,24},{1,5},{5... | collective-permute-start | bytes 380936 | tf_op jit(solution)/shard_map/ppermute | solution.py:302
  16.1 2.1 %collective-permute-start.7 = (bf16[16,3968]{1,0:T(8,128)(2,1)S(1)}, bf16[16,3968]{1,0:T(8,128)(2,1)S(1)}, u32[]{:S(2)}, u32[]{:S(2)}) collective-permute-start(bf16[16,3968]{1,0:T(8,128)(2,1)S(1)} %collective-permute-done.3.refs_8_), channel_id=1, source_target_pairs={{0,4},{4,0},{8,12},{12,8},{16,20},{20,16},{24,28},{28,24},{1,5},{5... | collective-permute-start | bytes 380936 | tf_op jit(solution)/shard_map/ppermute | solution.py:302
  26.4 4.1 %collective-permute-start.10 = (f32[16,16]{1,0:T(8,128)S(1)}, f32[16,16]{1,0:T(8,128)S(1)}, u32[]{:S(2)}, u32[]{:S(2)}) collective-permute-start(f32[16,16]{1,0:T(8,128)S(1)} %get-tuple-element.13), channel_id=1, source_target_pairs={{0,1},{1,0},{2,3},{3,2},{4,5},{5,4},{6,7},{7,6},{8,9},{9,8},{10,11... | collective-permute-start | bytes 3080 | tf_op jit(solution)/shard_map/ppermute | solution.py:305
  27.6 5.4 %collective-permute-start.12 = (f32[16,16]{1,0:T(8,128)S(1)}, f32[16,16]{1,0:T(8,128)S(1)}, u32[]{:S(2)}, u32[]{:S(2)}) collective-permute-start(f32[16,16]{1,0:T(8,128)S(1)} %get-tuple-element.14), channel_id=1, source_target_pairs={{0,3},{1,2},{2,1},{3,0},{4,7},{5,6},{6,5},{7,4},{8,11},{9,10},{10,... | collective-permute-start | bytes 3080 | tf_op jit(solution)/shard_map/ppermute | solution.py:305
  30.2 4.5 %collective-permute-start.11 = (f32[16,16]{1,0:T(8,128)S(1)}, f32[16,16]{1,0:T(8,128)S(1)}, u32[]{:S(2)}, u32[]{:S(2)}) collective-permute-start(f32[16,16]{1,0:T(8,128)S(1)} %get-tuple-element.15), channel_id=1, source_target_pairs={{0,2},{1,3},{2,0},{3,1},{4,6},{5,7},{6,4},{7,5},{8,10},{9,11},{10,... | collective-permute-start | bytes 3080 | tf_op jit(solution)/shard_map/ppermute | solution.py:305

commit v2 on v1

--- a/solution.py
+++ b/solution.py
@@ -22,8 +22,9 @@
 COUNT_AT = WIDE - TAIL
 PROBE_AT = COUNT_AT + 1
 OWNER_AT = STRIDE
-ROWS = (1024, 256)
-COLS = (1024, 256)
+ROWS = (896, 1024, 256)
+COLS = (896, 1024, 256)
+PREPARED = (2048, 2048, 256)
 SCALE = 2.0 * math.log2(math.e) / (2.0 * PV)
 NT = (((1,), (1,)), ((), ()))
 NN = (((1,), (0,)), ((), ()))
@@ -148,73 +149,93 @@
     return chosen, first.astype(jnp.int32)
 
 
-def spread(sorted_ref, chosen, first_ref, at, x_ref, room):
+def owners(chosen):
+    number = chosen.shape[0]
+    owner = jnp.sum(jnp.where(chosen > 0, iota((number, number), 1).astype(jnp.float32), 0.0), axis=1, keepdims=True)
+    return jnp.where(iota((number, LANES), 1) == OWNER_AT, owner, 0.0)
+
+
+def spread(sorted_ref, owner, first_ref, x_ref, room):
     number = sorted_ref.shape[0]
     lane = iota((number, LANES), 1)
-    owner = jnp.sum(jnp.where(chosen > 0, iota((number, number), 1).astype(jnp.float32), 0.0), axis=1, keepdims=True)
-    owner = jnp.where(lane == OWNER_AT, owner, 0.0)
     for p in range(P_SIZE):
         values = jnp.where(lane < STRIDE, sorted_ref[:, p * STRIDE : p * STRIDE + LANES], owner)
-        x_ref[pl.ds(first_ref[at, p], number), :] = values
-    total = first_ref[at, P_SIZE]
+        x_ref[pl.ds(first_ref[0, p], number), :] = values
+    total = first_ref[0, P_SIZE]
     x_ref[pl.ds(total, room), :] = jnp.zeros((room, LANES), jnp.float32)
     return total
 
 
 def cover(total, sizes, step, carry):
-    large, small = sizes
-    number = (total + large - small) // large
-    carry = lax.fori_loop(0, number, lambda k, c: step(pl.multiple_of(k * large, large), large, c), carry)
-    rest = (total - number * large + small - 1) // small
-    start = pl.multiple_of(number * large, large)
-    return lax.fori_loop(0, rest, lambda k, c: step(start, small, c), carry)
-
-
-def rank_kernel(*refs):
-    chosen_ref, first_ref = refs[-2:]
-    tail = jnp.concatenate([part[:, TAIL : TAIL + LANES] for part in refs[:-2]], axis=0)
-    chosen, first = order(tail.astype(jnp.float32))
-    chosen_ref[...] = chosen
-    first_ref[...] = first
-
-
-def rank(near):
-    images = sum(a.shape[0] for a in near)
+    tight, large, small = sizes
+    fits = total <= 2 * tight
+
+    def run(number, size, base, carry):
+        return lax.fori_loop(0, number, lambda k, c: step(pl.multiple_of(base + k * size, LANES), size, c), carry)
+
+    carry = run(jnp.where(fits, (total + tight - 1) // tight, 0), tight, 0, carry)
+    number = jnp.where(fits, 0, (total + large - small) // large)
+    carry = run(number, large, 0, carry)
+    rest = jnp.where(fits, 0, (total - number * large + small - 1) // small)
+    return run(rest, small, number * large, carry)
+
+
+def rank_rows_kernel(*refs):
+    which_ref, owner_ref, first_ref = refs[-3:]
+    tail = jnp.concatenate([part[:, TAIL : TAIL + LANES] for part in refs[:-3]], axis=0)
+    which_ref[...], first_ref[...] = order(tail.astype(jnp.float32))
+    owner_ref[...] = owners(which_ref[...])
+
+
+def rank_cols_kernel(met_ref, *refs):
+    which_ref, owner_ref, first_ref, probe_ref = refs[-4:]
+    met = met_ref[...]
+    tail = dot(met, jnp.concatenate([part[:, TAIL : TAIL + LANES] for part in refs[:-4]], axis=0))
+    chosen, first_ref[...] = order(tail)
+    which_ref[...] = dot(chosen, met).astype(jnp.bfloat16)
+    owner_ref[...] = owners(chosen)
+    both = (2 * NPROBE, LANES)
+    pick_probe = (iota(both, 1) == iota(both, 0) + PROBE_AT).astype(jnp.bfloat16)
+    probe_ref[...] = dot(pick_probe, tail.astype(jnp.bfloat16), NT).astype(jnp.bfloat16)
+
+
+def rank(kernel, number, given, extra, flops):
     return pl.pallas_call(
-        rank_kernel,
-        out_shape=(jax.ShapeDtypeStruct((images, images), jnp.bfloat16), jax.ShapeDtypeStruct((8, LANES), jnp.int32)),
-        in_specs=[VMEM] * len(near),
-        out_specs=(VMEM, VMEM),
+        kernel,
+        out_shape=(
+            jax.ShapeDtypeStruct((number, sum(a.shape[0] for a in given[-extra:])), jnp.bfloat16),
+            jax.ShapeDtypeStruct((number, LANES), jnp.float32),
+            jax.ShapeDtypeStruct((8, LANES), jnp.int32),
+        )
+        + ((jax.ShapeDtypeStruct((2 * NPROBE, number), jnp.bfloat16),) if extra < len(given) else ()),
+        in_specs=[VMEM] * len(given),
+        out_specs=(VMEM,) * (3 if extra == len(given) else 4),
         compiler_params=pltpu.CompilerParams(vmem_limit_bytes=8 * 2**20),
-        cost_estimate=pl.CostEstimate(flops=2 * 10**10, bytes_accessed=10**6, transcendentals=0),
+        cost_estimate=pl.CostEstimate(flops=flops, bytes_accessed=10**6, transcendentals=0),
         name="rank",
-    )(*near)
+    )(*given)
 
 
 def energies(counted, *refs):
     near_number, far_number = counted
-    row_first, row_order, met_ref = refs[:3]
-    near_parts = refs[3 : 3 + near_number]
-    far_parts = refs[3 + near_number : 3 + near_number + far_number]
-    (out_ref, row_sorted, col_sorted, row_x, col_f, col_x, col_u, product, first_v, first_s, sem) = refs[
-        3 + near_number + far_number :
+    row_given, col_given, row_which, row_owner, col_which, col_owner, probe_ref = refs[:7]
+    near_parts = refs[7 : 7 + near_number]
+    far_parts = refs[7 + near_number : 7 + near_number + far_number]
+    (out_ref, row_sorted, col_sorted, row_x, col_f, col_x, col_u, product, row_first, col_first, sem) = refs[
+        7 + near_number + far_number :
     ]
-    cols = met_ref.shape[0]
-    met = met_ref[...]
-    for target in (row_sorted, col_sorted):
-        target[:, PACKED:] = jnp.zeros((target.shape[0], LANES), jnp.float32)
-    tails = jnp.concatenate([part[:, TAIL : TAIL + LANES] for part in far_parts], axis=0)
-    col_tail = dot(met, tails)
-    col_order, col_first = order(col_tail)
-    first_v[...] = col_first
-    copy = pltpu.make_async_copy(first_v, first_s, sem)
-    copy.start()
-    row_sorted[:, 0:PACKED] = dot(row_order[...], jnp.concatenate([part[...] for part in near_parts], axis=0))
-    col_chosen = dot(col_order, met).astype(jnp.bfloat16)
-    col_sorted[:, 0:PACKED] = dot(col_chosen, jnp.concatenate([part[...] for part in far_parts], axis=0))
-    row_total = spread(row_sorted, row_order[...], row_first, 0, row_x, ROWS[0])
-    copy.wait()
-    col_total = spread(col_sorted, col_order, first_s, 0, col_f, COLS[0])
+    cols = col_owner.shape[0]
+    copies = [pltpu.make_async_copy(s, t, sem.at[k]) for k, (s, t) in enumerate(((col_given, col_first), (row_given, row_first)))]
+    for copy in copies:
+        copy.start()
+    product[...] = jnp.zeros_like(product)
+    col_sorted[...] = dot(col_which[...], jnp.concatenate([part[...] for part in far_parts], axis=0))
+    row_sorted[...] = dot(row_which[...], jnp.concatenate([part[...] for part in near_parts], axis=0))
+    copies[0].wait()
+    col_total = spread(col_sorted, col_owner[...], col_first, col_f, COLS[1])
+    copies[1].wait()
+    row_total = spread(row_sorted, row_owner[...], row_first, row_x, ROWS[1])
+    probes = probe_ref[...]
 
     line, lane = iota((NPROBE, LANES), 0), iota((NPROBE, LANES), 1)
     pick = (
@@ -222,10 +243,6 @@
         | ((line == 1) & (lane >= ALPHA_AT) & (lane < STRIDE))
         | ((line == 2) & (lane == OWNER_AT))
     ).astype(jnp.bfloat16)
-    both = (2 * NPROBE, LANES)
-    pick_probe = (iota(both, 1) == iota(both, 0) + PROBE_AT).astype(jnp.bfloat16)
-    probes = dot(pick_probe, col_tail.astype(jnp.bfloat16), NT).astype(jnp.bfloat16)
-
     def owned(picked, number, size):
         return (iota((number, size), 0).astype(jnp.float32) == picked[2:3]).astype(jnp.bfloat16)
 
@@ -238,8 +255,7 @@
         col_u[:, here] = (picked[1:2] * (mine[:NPROBE] + mine[NPROBE:])).astype(jnp.bfloat16)
         return unused
 
-    cover(col_total, COLS, prepare, 0)
-    product[...] = jnp.zeros_like(product)
+    cover(col_total, PREPARED, prepare, 0)
 
     def one_row(start, size, unused):
         x_rows = row_x[pl.ds(start, size), :].astype(jnp.bfloat16)
@@ -265,31 +281,32 @@
     out_ref[...] = product[...].T
 
 
-def local_terms(met, ranked, near, far):
-    row_order, row_first = ranked
-    rows, cols = row_order.shape[0], met.shape[0]
-    row_room = rows * P_SIZE + rows + ROWS[0]
-    col_room = (cols * P_SIZE + cols) // COLS[0] * COLS[0] + 2 * COLS[0]
+def local_terms(rows_rank, cols_rank, near, far):
+    row_which, row_owner, row_first = rows_rank
+    col_which, col_owner, col_first, probes = cols_rank
+    rows, cols = row_owner.shape[0], col_owner.shape[0]
+    row_room = rows * P_SIZE + rows + ROWS[1]
+    col_room = (cols * P_SIZE + cols) // COLS[1] * COLS[1] + COLS[1] + PREPARED[1]
     return pl.pallas_call(
         functools.partial(energies, (len(near), len(far))),
         out_shape=jax.ShapeDtypeStruct((rows, NPROBE), jnp.float32),
-        in_specs=[SMEM] + [VMEM] * (2 + len(near) + len(far)),
+        in_specs=[VMEM] * (7 + len(near) + len(far)),
         out_specs=VMEM,
         scratch_shapes=[
-            pltpu.VMEM((rows, PACKED + LANES), jnp.float32),
-            pltpu.VMEM((cols, PACKED + LANES), jnp.float32),
+            pltpu.VMEM((rows, PACKED), jnp.float32),
+            pltpu.VMEM((cols, PACKED), jnp.float32),
             pltpu.VMEM((row_room, LANES), jnp.float32),
             pltpu.VMEM((col_room, LANES), jnp.float32),
             pltpu.VMEM((col_room, LANES), jnp.bfloat16),
             pltpu.VMEM((NPROBE, col_room), jnp.bfloat16),
             pltpu.VMEM((NPROBE, rows), jnp.float32),
-            pltpu.VMEM((8, LANES), jnp.int32),
             pltpu.SMEM((8, LANES), jnp.int32),
-            pltpu.SemaphoreType.DMA,
+            pltpu.SMEM((8, LANES), jnp.int32),
+            pltpu.SemaphoreType.DMA((2,)),
         ],
         compiler_params=pltpu.CompilerParams(vmem_limit_bytes=40 * 2**20),
         name="energies",
-    )(row_first, row_order, met, *near, *far)
+    )(row_first, col_first, row_which, row_owner, col_which, col_owner, probes, *near, *far)
 
 
 def shards(patches, counts, weights, probes, plan):
@@ -310,9 +327,11 @@
     for apart in range(1, subs):
         low = apart & -apart
         near.append(across(near[apart - low], low))
-    terms = local_terms(met, rank(near), near, far)
+    rows_rank = rank(rank_rows_kernel, subs * images, near, subs, 20 * 10**9)
+    cols_rank = rank(rank_cols_kernel, met.shape[0], [met, *far], groups, 2 * 10**9)
+    terms = local_terms(rows_rank, cols_rank, near, far)
     total = terms[:images]
-    for apart in range(1, subs):
+    for apart in range(subs - 1, 0, -1):
         total = total + across(terms[apart * images : (apart + 1) * images], apart)
     return total
 

time: 35.6 us -> 34.5 us (0.969)
  Pallas kernels: 9.06 us -> 8.21 us
  waiting for transfers between devices: 9.71 us -> 9.07 us
    pallas_call x1, Pallas kernels: 8.17 us -> 6.96 us  [local_terms(): pl.pallas_call(functools.partial(energies, (len(near), len(far))), out_sh...]
    ppermute x6, waiting for transfers between devices: 8 us -> 7.37 us  [across(): return lax.ppermute(array, 'narrow', [(i, i ^ apart) for i in range(subs)])]
  transfers between devices with their start and end apart: 13 -> 13, of which waited for: 7 -> 8; matrix products, arithmetic and copies ran while one was open for 0% -> 0% of each run, Pallas kernels for 1% -> 1%
where the time goes in v2:
time: 34.5 us; the launch traced here: 34.3 us
  starting transfers between devices  14.7 us (43%)
  waiting for transfers between devices  9.07 us (26%)
  Pallas kernels  8.21 us (24%)
  local copies, waits for them, and re-layouts  1.6 us (5%)
  other arithmetic  0.6 us (2%)
    ppermute x6, starting transfers between devices, across(): return lax.ppermute(array, 'narrow', [(i, i ^ apart) for i in range(subs)])  10.8 us
    ppermute x6, waiting for transfers between devices, across(): return lax.ppermute(array, 'narrow', [(i, i ^ apart) for i in range(subs)])  7.37 us
    pallas_call x1, Pallas kernels, local_terms(): pl.pallas_call(functools.partial(energies, (len(near), len(far))), out_sh...  6.96 us
    ppermute x7, starting transfers between devices, swap(): return lax.ppermute(array, 'group', [(i, i ^ apart) for i in range(groups)])  3.9 us
    ppermute x7, waiting for transfers between devices, swap(): return lax.ppermute(array, 'group', [(i, i ^ apart) for i in range(groups)])  1.7 us
    unnamed x10, local copies, waits for them, and re-layouts  1.6 us
  transfers between devices with their start and end apart: 13, of which 8 were waited for; matrix products, arithmetic and copies ran while one was open for 0% of the time, Pallas kernels for 1%

profile of v2, /device:TPU:0, one launch (start us, length us, event | category | flops | bytes accessed | tf_op | source)
XLA Modules:
  0.0 34.3 jit_solution(4995048740312109021)
XLA Ops:
  0.0 0.7 %copy-done.1 = f32[16,16]{1,0:T(8,128)S(1)} copy-done((f32[16,16]{1,0:T(8,128)S(1)}, f32[16,16]{1,0:T(8,128)}, u32[]{:S(2)}) %copy-start.1) | copy-done | bytes 1048
  0.7 0.9 %copy-done = bf16[16,3675]{1,0:T(8,128)(2,1)S(1)} copy-done((bf16[16,3675]{1,0:T(8,128)(2,1)S(1)}, bf16[16,3675]{1,0:T(8,128)(2,1)}, u32[]{:S(2)}) %copy-start) | copy-done | bytes 117624
  1.6 0.7 %pack.1 = (bf16[16,3968]{1,0:T(8,128)(2,1)S(1)}, bf16[64,128]{1,0:T(8,128)(2,1)S(1)}) custom-call(s32[1]{0:T(128)} %bitcast.mine_ref, bf16[16,3675]{1,0:T(8,128)(2,1)S(1)} %copy-done, s32[1,16]{1,0:T(1,128)S(1)} %bitcast.3, f32[1,49]{1,0:T(1,128)S(1)} %bitcast.4, f32[16,16]{1,0:T(8,128)S(1)} %copy-done.1, s32[4,8]{1,0:T(4,128)S(1)} %copy-done.2), custom_call_target="tpu_custom_call" | custom-call | tf_op jit(solution)/shard_map/pack/pallas_call | solution.py:122
  2.3 4.1 %collective-permute-start.1 = (bf16[16,3968]{1,0:T(8,128)(2,1)S(1)}, bf16[16,3968]{1,0:T(8,128)(2,1)S(1)}, u32[]{:S(2)}, u32[]{:S(2)}) collective-permute-start(bf16[16,3968]{1,0:T(8,128)(2,1)S(1)} %get-tuple-element.14.refs_0_.refs_7_.refs_11_), channel_id=1, source_target_pairs={{0,2},{1,3},{2,0},{3,1},{4,6},{5,7},{6,4},{7,5},{8,10},{9,11},{10,... | collective-permute-start | bytes 380936 | tf_op jit(solution)/shard_map/ppermute | solution.py:322
  6.4 2.4 %collective-permute-start.5 = (bf16[16,3968]{1,0:T(8,128)(2,1)S(1)}, bf16[16,3968]{1,0:T(8,128)(2,1)S(1)}, u32[]{:S(2)}, u32[]{:S(2)}) collective-permute-start(bf16[16,3968]{1,0:T(8,128)(2,1)S(1)} %get-tuple-element.14.refs_0_.refs_7_.refs_11_), channel_id=1, source_target_pairs={{0,24},{4,28},{8,16},{12,20},{16,8},{20,12},{24,0},{28,4},{1,25},{... | collective-permute-start | bytes 380936 | tf_op jit(solution)/shard_map/ppermute | solution.py:319
  8.9 0.5 %collective-permute-start.4 = (bf16[16,3968]{1,0:T(8,128)(2,1)S(1)}, bf16[16,3968]{1,0:T(8,128)(2,1)S(1)}, u32[]{:S(2)}, u32[]{:S(2)}) collective-permute-start(bf16[16,3968]{1,0:T(8,128)(2,1)S(1)} %get-tuple-element.14.refs_0_.refs_7_.refs_11_), channel_id=1, source_target_pairs={{0,16},{4,20},{8,24},{12,28},{16,0},{20,4},{24,8},{28,12},{1,17},{... | collective-permute-start | bytes 380936 | tf_op jit(solution)/shard_map/ppermute | solution.py:319
  9.4 0.5 %collective-permute-start.3 = (bf16[16,3968]{1,0:T(8,128)(2,1)S(1)}, bf16[16,3968]{1,0:T(8,128)(2,1)S(1)}, u32[]{:S(2)}, u32[]{:S(2)}) collective-permute-start(bf16[16,3968]{1,0:T(8,128)(2,1)S(1)} %get-tuple-element.14.refs_0_.refs_7_.refs_11_), channel_id=1, source_target_pairs={{0,8},{4,12},{8,0},{12,4},{16,24},{20,28},{24,16},{28,20},{1,9},{5... | collective-permute-start | bytes 380936 | tf_op jit(solution)/shard_map/ppermute | solution.py:319
  9.9 1.6 %collective-permute-start = (bf16[16,3968]{1,0:T(8,128)(2,1)S(1)}, bf16[16,3968]{1,0:T(8,128)(2,1)S(1)}, u32[]{:S(2)}, u32[]{:S(2)}) collective-permute-start(bf16[16,3968]{1,0:T(8,128)(2,1)S(1)} %get-tuple-element.14.refs_0_.refs_7_.refs_11_), channel_id=1, source_target_pairs={{0,1},{1,0},{2,3},{3,2},{4,5},{5,4},{6,7},{7,6},{8,9},{9,8},{10,11... | collective-permute-start | bytes 380936 | tf_op jit(solution)/shard_map/ppermute | solution.py:322
  11.5 1.2 %collective-permute-done.1.refs_2_.refs_9_ = bf16[16,3968]{1,0:T(8,128)(2,1)S(1)} collective-permute-done((bf16[16,3968]{1,0:T(8,128)(2,1)S(1)}, bf16[16,3968]{1,0:T(8,128)(2,1)S(1)}, u32[]{:S(2)}, u32[]{:S(2)}) %collective-permute-start.1) | collective-permute-done | bytes 127008 | tf_op jit(solution)/shard_map/ppermute | solution.py:322
  12.6 0.7 %collective-permute-start.2 = (bf16[16,3968]{1,0:T(8,128)(2,1)S(1)}, bf16[16,3968]{1,0:T(8,128)(2,1)S(1)}, u32[]{:S(2)}, u32[]{:S(2)}) collective-permute-start(bf16[16,3968]{1,0:T(8,128)(2,1)S(1)} %collective-permute-done.1.refs_2_.refs_9_), channel_id=1, source_target_pairs={{0,1},{1,0},{2,3},{3,2},{4,5},{5,4},{6,7},{7,6},{8,9},{9,8},{10,11... | collective-permute-start | bytes 380936 | tf_op jit(solution)/shard_map/ppermute | solution.py:322
  13.3 1.6 %collective-permute-done.4.refs_2_.refs_13_ = bf16[16,3968]{1,0:T(8,128)(2,1)S(1)} collective-permute-done((bf16[16,3968]{1,0:T(8,128)(2,1)S(1)}, bf16[16,3968]{1,0:T(8,128)(2,1)S(1)}, u32[]{:S(2)}, u32[]{:S(2)}) %collective-permute-start.4) | collective-permute-done | bytes 127008 | tf_op jit(solution)/shard_map/ppermute | solution.py:319
  14.9 0.1 collective-permute-done.3.refs_1_.refs_12_
  15.0 0.4 %collective-permute-start.8 = (bf16[16,3968]{1,0:T(8,128)(2,1)S(1)}, bf16[16,3968]{1,0:T(8,128)(2,1)S(1)}, u32[]{:S(2)}, u32[]{:S(2)}) collective-permute-start(bf16[16,3968]{1,0:T(8,128)(2,1)S(1)} %collective-permute-done.4.refs_2_.refs_13_), channel_id=1, source_target_pairs={{0,4},{4,0},{8,12},{12,8},{16,20},{20,16},{24,28},{28,24},{1,5},{5... | collective-permute-start | bytes 380936 | tf_op jit(solution)/shard_map/ppermute | solution.py:319
  15.4 0.7 %collective-permute-done.refs_1_.refs_8_ = bf16[16,3968]{1,0:T(8,128)(2,1)S(1)} collective-permute-done((bf16[16,3968]{1,0:T(8,128)(2,1)S(1)}, bf16[16,3968]{1,0:T(8,128)(2,1)S(1)}, u32[]{:S(2)}, u32[]{:S(2)}) %collective-permute-start) | collective-permute-done | bytes 127008 | tf_op jit(solution)/shard_map/ppermute | solution.py:322
  16.1 1.9 %collective-permute-done.2.refs_3_.refs_10_ = bf16[16,3968]{1,0:T(8,128)(2,1)S(1)} collective-permute-done((bf16[16,3968]{1,0:T(8,128)(2,1)S(1)}, bf16[16,3968]{1,0:T(8,128)(2,1)S(1)}, u32[]{:S(2)}, u32[]{:S(2)}) %collective-permute-start.2) | collective-permute-done | bytes 127008 | tf_op jit(solution)/shard_map/ppermute | solution.py:322
  18.0 0.2 rank.2
  18.2 0.4 %rank.3 = (bf16[64,128]{1,0:T(8,128)(2,1)S(1)}, f32[64,128]{1,0:T(8,128)S(1)}, s32[8,128]{1,0:T(8,128)S(1)}, bf16[32,64]{1,0:T(8,128)(2,1)S(1)}) custom-call(bf16[64,128]{1,0:T(8,128)(2,1)S(1)} %get-tuple-element.16.met_ref, bf16[16,3968]{1,0:T(8,128)(2,1)S(1)} %get-tuple-element.14.refs_0_.refs_7_.refs_11_, ...), custom_call_target="tpu_custom_call" | custom-call | flops 2000000000 | bytes 1000000 | tf_op jit(solution)/shard_map/rank/pallas_call | solution.py:203
  18.6 7.0 %energies.1 = f32[64,16]{1,0:T(8,128)S(1)} custom-call(s32[8,128]{1,0:T(8,128)S(1)} %get-tuple-element.15.refs_0_, s32[8,128]{1,0:T(8,128)S(1)} %get-tuple-element.17.refs_1_, bf16[64,64]{1,0:T(8,128)(2,1)S(1)} %get-tuple-element.18.refs_2_, f32[64,128]{1,0:T(8,128)S(1)} %get-tuple-element.19.refs_3_, bf16[64,128]{1,0:T(8,128)(2,1)S(1)} %get-tuple-element.20.refs_4_, ...), custom_call_target="tpu_custom_call" | custom-call | tf_op jit(solution)/shard_map/energies/pallas_call | solution.py:290
  25.6 3.5 %collective-permute-start.10 = (f32[16,16]{1,0:T(8,128)S(1)}, f32[16,16]{1,0:T(8,128)S(1)}, u32[]{:S(2)}, u32[]{:S(2)}) collective-permute-start(f32[16,16]{1,0:T(8,128)S(1)} %get-tuple-element.23), channel_id=1, source_target_pairs={{0,3},{1,2},{2,1},{3,0},{4,7},{5,6},{6,5},{7,4},{8,11},{9,10},{10,... | collective-permute-start | bytes 3080 | tf_op jit(solution)/shard_map/ppermute | solution.py:322
  29.1 0.9 %collective-permute-start.11 = (f32[16,16]{1,0:T(8,128)S(1)}, f32[16,16]{1,0:T(8,128)S(1)}, u32[]{:S(2)}, u32[]{:S(2)}) collective-permute-start(f32[16,16]{1,0:T(8,128)S(1)} %get-tuple-element.25), channel_id=1, source_target_pairs={{0,2},{1,3},{2,0},{3,1},{4,6},{5,7},{6,4},{7,5},{8,10},{9,11},{10,... | collective-permute-start | bytes 3080 | tf_op jit(solution)/shard_map/ppermute | solution.py:322
  30.0 1.1 %collective-permute-done.10 = f32[16,16]{1,0:T(8,128)S(1)} collective-permute-done((f32[16,16]{1,0:T(8,128)S(1)}, f32[16,16]{1,0:T(8,128)S(1)}, u32[]{:S(2)}, u32[]{:S(2)}) %collective-permute-start.10) | collective-permute-done | bytes 1056 | tf_op jit(solution)/shard_map/ppermute | solution.py:322
  31.1 1.7 %collective-permute-done.12 = f32[16,16]{1,0:T(8,128)S(1)} collective-permute-done((f32[16,16]{1,0:T(8,128)S(1)}, f32[16,16]{1,0:T(8,128)S(1)}, u32[]{:S(2)}, u32[]{:S(2)}) %collective-permute-start.12) | collective-permute-done | bytes 1056 | tf_op jit(solution)/shard_map/ppermute | solution.py:322
  32.8 0.9 %collective-permute-done.11 = f32[16,16]{1,0:T(8,128)S(1)} collective-permute-done((f32[16,16]{1,0:T(8,128)S(1)}, f32[16,16]{1,0:T(8,128)S(1)}, u32[]{:S(2)}, u32[]{:S(2)}) %collective-permute-start.11) | collective-permute-done | bytes 1056 | tf_op jit(solution)/shard_map/ppermute | solution.py:322
  33.7 0.6 %fusion.1 = f32[16,16]{1,0:T(8,128)} fusion(f32[16,16]{1,0:T(8,128)S(1)} %collective-permute-done.12, f32[16,16]{1,0:T(8,128)S(1)} %collective-permute-done.11, f32[16,16]{1,0:T(8,128)S(1)} %collective-permute-done.10, f32[64,16]{1,0:T(8,128)S(1)} %energies.1), kind=kLoop, calls=%fused_computation.2 | loop fusion | flops 768 | bytes 5120 | tf_op jit(solution)/shard_map/add | solution.py:335
  (18 shorter events, 0.0 us)
Async XLA Ops:
  0.0 0.7 %copy-start.1 = (f32[16,16]{1,0:T(8,128)S(1)}, f32[16,16]{1,0:T(8,128)}, u32[]{:S(2)}) copy-start(f32[16,16]{1,0:T(8,128)} %refs_3_.1) | copy-start | bytes 3076
  0.0 0.7 %copy-start.2 = (s32[4,8]{1,0:T(4,128)S(1)}, s32[4,8]{1,0:T(4,128)}, u32[]{:S(2)}) copy-start(s32[4,8]{1,0:T(4,128)} %refs_4_.1) | copy-start | bytes 388
  0.0 0.7 %copy-start.3 = (s32[16]{0:T(128)S(1)}, s32[16]{0:T(128)}, u32[]{:S(2)}) copy-start(s32[16]{0:T(128)} %param.6) | copy-start | bytes 196
  0.0 0.7 %copy-start.4 = (f32[49]{0:T(128)S(1)}, f32[49]{0:T(128)}, u32[]{:S(2)}) copy-start(f32[49]{0:T(128)} %param.7) | copy-start | bytes 592
  0.7 0.9 %copy-start = (bf16[16,3675]{1,0:T(8,128)(2,1)S(1)}, bf16[16,3675]{1,0:T(8,128)(2,1)}, u32[]{:S(2)}) copy-start(bf16[16,3675]{1,0:T(8,128)(2,1)} %refs_0_.1) | copy-start | bytes 352804
  2.3 10.3 %collective-permute-start.1 = (bf16[16,3968]{1,0:T(8,128)(2,1)S(1)}, bf16[16,3968]{1,0:T(8,128)(2,1)S(1)}, u32[]{:S(2)}, u32[]{:S(2)}) collective-permute-start(bf16[16,3968]{1,0:T(8,128)(2,1)S(1)} %get-tuple-element.14.refs_0_.refs_7_.refs_11_), channel_id=1, source_target_pairs={{0,2},{1,3},{2,0},{3,1},{4,6},{5,7},{6,4},{7,5},{8,10},{9,11},{10,... | collective-permute-start | bytes 380936 | tf_op jit(solution)/shard_map/ppermute | solution.py:322
  6.4 6.9 %collective-permute-start.5 = (bf16[16,3968]{1,0:T(8,128)(2,1)S(1)}, bf16[16,3968]{1,0:T(8,128)(2,1)S(1)}, u32[]{:S(2)}, u32[]{:S(2)}) collective-permute-start(bf16[16,3968]{1,0:T(8,128)(2,1)S(1)} %get-tuple-element.14.refs_0_.refs_7_.refs_11_), channel_id=1, source_target_pairs={{0,24},{4,28},{8,16},{12,20},{16,8},{20,12},{24,0},{28,4},{1,25},{... | collective-permute-start | bytes 380936 | tf_op jit(solution)/shard_map/ppermute | solution.py:319
  8.9 6.0 %collective-permute-start.4 = (bf16[16,3968]{1,0:T(8,128)(2,1)S(1)}, bf16[16,3968]{1,0:T(8,128)(2,1)S(1)}, u32[]{:S(2)}, u32[]{:S(2)}) collective-permute-start(bf16[16,3968]{1,0:T(8,128)(2,1)S(1)} %get-tuple-element.14.refs_0_.refs_7_.refs_11_), channel_id=1, source_target_pairs={{0,16},{4,20},{8,24},{12,28},{16,0},{20,4},{24,8},{28,12},{1,17},{... | collective-permute-start | bytes 380936 | tf_op jit(solution)/shard_map/ppermute | solution.py:319
  9.4 5.6 %collective-permute-start.3 = (bf16[16,3968]{1,0:T(8,128)(2,1)S(1)}, bf16[16,3968]{1,0:T(8,128)(2,1)S(1)}, u32[]{:S(2)}, u32[]{:S(2)}) collective-permute-start(bf16[16,3968]{1,0:T(8,128)(2,1)S(1)} %get-tuple-element.14.refs_0_.refs_7_.refs_11_), channel_id=1, source_target_pairs={{0,8},{4,12},{8,0},{12,4},{16,24},{20,28},{24,16},{28,20},{1,9},{5... | collective-permute-start | bytes 380936 | tf_op jit(solution)/shard_map/ppermute | solution.py:319
  9.9 6.2 %collective-permute-start = (bf16[16,3968]{1,0:T(8,128)(2,1)S(1)}, bf16[16,3968]{1,0:T(8,128)(2,1)S(1)}, u32[]{:S(2)}, u32[]{:S(2)}) collective-permute-start(bf16[16,3968]{1,0:T(8,128)(2,1)S(1)} %get-tuple-element.14.refs_0_.refs_7_.refs_11_), channel_id=1, source_target_pairs={{0,1},{1,0},{2,3},{3,2},{4,5},{5,4},{6,7},{7,6},{8,9},{9,8},{10,11... | collective-permute-start | bytes 380936 | tf_op jit(solution)/shard_map/ppermute | solution.py:322
  12.6 5.3 %collective-permute-start.2 = (bf16[16,3968]{1,0:T(8,128)(2,1)S(1)}, bf16[16,3968]{1,0:T(8,128)(2,1)S(1)}, u32[]{:S(2)}, u32[]{:S(2)}) collective-permute-start(bf16[16,3968]{1,0:T(8,128)(2,1)S(1)} %collective-permute-done.1.refs_2_.refs_9_), channel_id=1, source_target_pairs={{0,1},{1,0},{2,3},{3,2},{4,5},{5,4},{6,7},{7,6},{8,9},{9,8},{10,11... | collective-permute-start | bytes 380936 | tf_op jit(solution)/shard_map/ppermute | solution.py:322
  13.3 4.9 %collective-permute-start.6 = (bf16[16,3968]{1,0:T(8,128)(2,1)S(1)}, bf16[16,3968]{1,0:T(8,128)(2,1)S(1)}, u32[]{:S(2)}, u32[]{:S(2)}) collective-permute-start(bf16[16,3968]{1,0:T(8,128)(2,1)S(1)} %get-tuple-element.14.refs_0_.refs_7_.refs_11_), channel_id=1, source_target_pairs={{0,4},{4,0},{8,12},{12,8},{16,20},{20,16},{24,28},{28,24},{1,5},{5... | collective-permute-start | bytes 380936 | tf_op jit(solution)/shard_map/ppermute | solution.py:319
  14.9 3.3 %collective-permute-start.9 = (bf16[16,3968]{1,0:T(8,128)(2,1)S(1)}, bf16[16,3968]{1,0:T(8,128)(2,1)S(1)}, u32[]{:S(2)}, u32[]{:S(2)}) collective-permute-start(bf16[16,3968]{1,0:T(8,128)(2,1)S(1)} %collective-permute-done.5.refs_3_.refs_14_), channel_id=1, source_target_pairs={{0,4},{4,0},{8,12},{12,8},{16,20},{20,16},{24,28},{28,24},{1,5},{5... | collective-permute-start | bytes 380936 | tf_op jit(solution)/shard_map/ppermute | solution.py:319
  15.0 3.2 %collective-permute-start.8 = (bf16[16,3968]{1,0:T(8,128)(2,1)S(1)}, bf16[16,3968]{1,0:T(8,128)(2,1)S(1)}, u32[]{:S(2)}, u32[]{:S(2)}) collective-permute-start(bf16[16,3968]{1,0:T(8,128)(2,1)S(1)} %collective-permute-done.4.refs_2_.refs_13_), channel_id=1, source_target_pairs={{0,4},{4,0},{8,12},{12,8},{16,20},{20,16},{24,28},{28,24},{1,5},{5... | collective-permute-start | bytes 380936 | tf_op jit(solution)/shard_map/ppermute | solution.py:319
  16.1 2.1 %collective-permute-start.7 = (bf16[16,3968]{1,0:T(8,128)(2,1)S(1)}, bf16[16,3968]{1,0:T(8,128)(2,1)S(1)}, u32[]{:S(2)}, u32[]{:S(2)}) collective-permute-start(bf16[16,3968]{1,0:T(8,128)(2,1)S(1)} %collective-permute-done.3.refs_1_.refs_12_), channel_id=1, source_target_pairs={{0,4},{4,0},{8,12},{12,8},{16,20},{20,16},{24,28},{28,24},{1,5},{5... | collective-permute-start | bytes 380936 | tf_op jit(solution)/shard_map/ppermute | solution.py:319
  25.6 5.5 %collective-permute-start.10 = (f32[16,16]{1,0:T(8,128)S(1)}, f32[16,16]{1,0:T(8,128)S(1)}, u32[]{:S(2)}, u32[]{:S(2)}) collective-permute-start(f32[16,16]{1,0:T(8,128)S(1)} %get-tuple-element.23), channel_id=1, source_target_pairs={{0,3},{1,2},{2,1},{3,0},{4,7},{5,6},{6,5},{7,4},{8,11},{9,10},{10,... | collective-permute-start | bytes 3080 | tf_op jit(solution)/shard_map/ppermute | solution.py:322
  29.1 3.7 %collective-permute-start.12 = (f32[16,16]{1,0:T(8,128)S(1)}, f32[16,16]{1,0:T(8,128)S(1)}, u32[]{:S(2)}, u32[]{:S(2)}) collective-permute-start(f32[16,16]{1,0:T(8,128)S(1)} %get-tuple-element.24), channel_id=1, source_target_pairs={{0,1},{1,0},{2,3},{3,2},{4,5},{5,4},{6,7},{7,6},{8,9},{9,8},{10,11... | collective-permute-start | bytes 3080 | tf_op jit(solution)/shard_map/ppermute | solution.py:322
  29.1 4.5 %collective-permute-start.11 = (f32[16,16]{1,0:T(8,128)S(1)}, f32[16,16]{1,0:T(8,128)S(1)}, u32[]{:S(2)}, u32[]{:S(2)}) collective-permute-start(f32[16,16]{1,0:T(8,128)S(1)} %get-tuple-element.25), channel_id=1, source_target_pairs={{0,2},{1,3},{2,0},{3,1},{4,6},{5,7},{6,4},{7,5},{8,10},{9,11},{10,... | collective-permute-start | bytes 3080 | tf_op jit(solution)/shard_map/ppermute | solution.py:322

commit v3 on v2

--- a/solution.py
+++ b/solution.py
@@ -22,15 +22,15 @@
 COUNT_AT = WIDE - TAIL
 PROBE_AT = COUNT_AT + 1
 OWNER_AT = STRIDE
-ROWS = (896, 1024, 256)
-COLS = (896, 1024, 256)
-PREPARED = (2048, 2048, 256)
+ROWS = ((1792, 1), (2048, 1), (1024, None))
+COLS = ((896, 2), (1024, None))
+PREPARED = ((2048, None),)
+FILL = 256
 SCALE = 2.0 * math.log2(math.e) / (2.0 * PV)
 NT = (((1,), (1,)), ((), ()))
 NN = (((1,), (0,)), ((), ()))
 VMEM = pl.BlockSpec(memory_space=pltpu.VMEM)
 SMEM = pl.BlockSpec(memory_space=pltpu.SMEM)
-HBM = pl.BlockSpec(memory_space=pltpu.HBM)
 
 
 def dot(a, b, dims=NN):
@@ -49,13 +49,7 @@
 
 
 def pack_kernel(mine_ref, *refs):
-    sources, (out_ref, met_ref), targets, sem = refs[:5], refs[5:7], refs[7:12], refs[12]
-    copies = [pltpu.make_async_copy(s, t, sem.at[k]) for k, (s, t) in enumerate(zip(sources, targets))]
-    for copy in copies:
-        copy.start()
-    for copy in copies:
-        copy.wait()
-    patches_ref, counts_ref, weights_ref, probes_ref, plan_ref = targets
+    patches_ref, counts_ref, weights_ref, probes_ref, plan_ref, out_ref, met_ref = refs
     images, wide = patches_ref.shape
     cols, far = met_ref.shape
     plan = plan_ref[...]
@@ -125,9 +119,8 @@
             jax.ShapeDtypeStruct((images, PACKED), jnp.bfloat16),
             jax.ShapeDtypeStruct((images * plan.shape[0], images * plan.shape[1]), jnp.bfloat16),
         ),
-        in_specs=[SMEM] + [HBM] * len(given),
+        in_specs=[SMEM] + [VMEM] * len(given),
         out_specs=(VMEM, VMEM),
-        scratch_shapes=[pltpu.VMEM(a.shape, a.dtype) for a in given] + [pltpu.SemaphoreType.DMA((len(given),))],
         compiler_params=pltpu.CompilerParams(vmem_limit_bytes=8 * 2**20),
         name="pack",
     )(mine, *given)
@@ -155,29 +148,38 @@
     return jnp.where(iota((number, LANES), 1) == OWNER_AT, owner, 0.0)
 
 
-def spread(sorted_ref, owner, first_ref, x_ref, room):
+def spread(sorted_ref, owner, first_ref, x_ref, options):
     number = sorted_ref.shape[0]
     lane = iota((number, LANES), 1)
     for p in range(P_SIZE):
         values = jnp.where(lane < STRIDE, sorted_ref[:, p * STRIDE : p * STRIDE + LANES], owner)
         x_ref[pl.ds(first_ref[0, p], number), :] = values
     total = first_ref[0, P_SIZE]
-    x_ref[pl.ds(total, room), :] = jnp.zeros((room, LANES), jnp.float32)
-    return total
-
-
-def cover(total, sizes, step, carry):
-    tight, large, small = sizes
-    fits = total <= 2 * tight
-
-    def run(number, size, base, carry):
-        return lax.fori_loop(0, number, lambda k, c: step(pl.multiple_of(base + k * size, LANES), size, c), carry)
-
-    carry = run(jnp.where(fits, (total + tight - 1) // tight, 0), tight, 0, carry)
-    number = jnp.where(fits, 0, (total + large - small) // large)
-    carry = run(number, large, 0, carry)
-    rest = jnp.where(fits, 0, (total - number * large + small - 1) // small)
-    return run(rest, small, number * large, carry)
+    counts = choose(total, options)
+    end = sum(count * size for count, (size, unused) in zip(counts, options))
+
+    def clear(step, unused):
+        x_ref[pl.ds(total + step * FILL, FILL), :] = jnp.zeros((FILL, LANES), jnp.float32)
+        return unused
+
+    lax.fori_loop(0, (end - total + FILL - 1) // FILL, clear, 0)
+    return total, counts
+
+
+def choose(total, options):
+    counts, left = [], 1
+    for size, most in options:
+        need = (total + size - 1) // size
+        fits = left if most is None else jnp.where(need <= most, left, 0)
+        counts.append(fits * need)
+        left = left - fits
+    return counts
+
+
+def cover(counts, options, step, carry):
+    for count, (size, unused) in zip(counts, options):
+        carry = lax.fori_loop(0, count, lambda k, c, size=size: step(pl.multiple_of(k * size, LANES), size, c), carry)
+    return carry
 
 
 def rank_rows_kernel(*refs):
@@ -232,9 +234,9 @@
     col_sorted[...] = dot(col_which[...], jnp.concatenate([part[...] for part in far_parts], axis=0))
     row_sorted[...] = dot(row_which[...], jnp.concatenate([part[...] for part in near_parts], axis=0))
     copies[0].wait()
-    col_total = spread(col_sorted, col_owner[...], col_first, col_f, COLS[1])
+    col_total, col_counts = spread(col_sorted, col_owner[...], col_first, col_f, COLS)
     copies[1].wait()
-    row_total = spread(row_sorted, row_owner[...], row_first, row_x, ROWS[1])
+    row_total, row_counts = spread(row_sorted, row_owner[...], row_first, row_x, ROWS)
     probes = probe_ref[...]
 
     line, lane = iota((NPROBE, LANES), 0), iota((NPROBE, LANES), 1)
@@ -255,7 +257,7 @@
         col_u[:, here] = (picked[1:2] * (mine[:NPROBE] + mine[NPROBE:])).astype(jnp.bfloat16)
         return unused
 
-    cover(col_total, PREPARED, prepare, 0)
+    cover(choose(col_total, PREPARED), PREPARED, prepare, 0)
 
     def one_row(start, size, unused):
         x_rows = row_x[pl.ds(start, size), :].astype(jnp.bfloat16)
@@ -271,13 +273,13 @@
             energy = jnp.exp2((inner + picked[0:1]) * SCALE).astype(jnp.bfloat16)
             return total + dot(col_u[:, here], energy)
 
-        total = cover(col_total, COLS, one_col, jnp.zeros((NPROBE, size), jnp.float32))
+        total = cover(col_counts, COLS, one_col, jnp.zeros((NPROBE, size), jnp.float32))
         weighted = jnp.concatenate(parts(total * picked[1:2]), axis=0).astype(jnp.bfloat16)
         sums = dot(weighted, owned(picked, product.shape[1], size), NT)
         product[...] += sums[0:NPROBE] + sums[NPROBE : 2 * NPROBE] + sums[2 * NPROBE :]
         return unused
 
-    cover(row_total, ROWS, one_row, 0)
+    cover(row_counts, ROWS, one_row, 0)
     out_ref[...] = product[...].T
 
 
@@ -285,8 +287,8 @@
     row_which, row_owner, row_first = rows_rank
     col_which, col_owner, col_first, probes = cols_rank
     rows, cols = row_owner.shape[0], col_owner.shape[0]
-    row_room = rows * P_SIZE + rows + ROWS[1]
-    col_room = (cols * P_SIZE + cols) // COLS[1] * COLS[1] + COLS[1] + PREPARED[1]
+    row_room = rows * P_SIZE + ROWS[1][0] + FILL
+    col_room = (cols * P_SIZE // PREPARED[0][0] + 1) * PREPARED[0][0] + FILL
     return pl.pallas_call(
         functools.partial(energies, (len(near), len(far))),
         out_shape=jax.ShapeDtypeStruct((rows, NPROBE), jnp.float32),
@@ -321,7 +323,7 @@
     def across(array, apart):
         return lax.ppermute(array, "narrow", [(i, i ^ apart) for i in range(subs)])
 
-    even = [packed] + [swap(packed, apart) for apart in range(2, groups, 2)]
+    even = [packed] + [swap(packed, apart) for apart in range(groups - 2, 0, -2)][::-1]
     far = even + [swap(array, 1) for array in even]
     near = [packed]
     for apart in range(1, subs):

time: 34.5 us -> 33.7 us (0.977)
  Pallas kernels: 8.21 us -> 7.28 us
    pallas_call x1, Pallas kernels: 6.96 us -> 6.22 us  [local_terms(): pl.pallas_call(functools.partial(energies, (len(near), len(far))), out_sh...]
where the time goes in v3:
time: 33.7 us; the launch traced here: 33.3 us
  starting transfers between devices  14.7 us (44%)
  waiting for transfers between devices  9.08 us (27%)
  Pallas kernels  7.28 us (22%)
  local copies, waits for them, and re-layouts  1.6 us (5%)
  other arithmetic  0.6 us (2%)
    ppermute x6, starting transfers between devices, across(): return lax.ppermute(array, 'narrow', [(i, i ^ apart) for i in range(subs)])  10.8 us
    ppermute x6, waiting for transfers between devices, across(): return lax.ppermute(array, 'narrow', [(i, i ^ apart) for i in range(subs)])  7.37 us
    pallas_call x1, Pallas kernels, local_terms(): pl.pallas_call(functools.partial(energies, (len(near), len(far))), out_sh...  6.22 us
    ppermute x7, starting transfers between devices, swap(): return lax.ppermute(array, 'group', [(i, i ^ apart) for i in range(groups)])  3.89 us
    ppermute x7, waiting for transfers between devices, swap(): return lax.ppermute(array, 'group', [(i, i ^ apart) for i in range(groups)])  1.71 us
    unnamed x10, local copies, waits for them, and re-layouts  1.6 us
  transfers between devices with their start and end apart: 13, of which 8 were waited for; matrix products, arithmetic and copies ran while one was open for 0% of the time, Pallas kernels for 1%

profile of v3, /device:TPU:0, one launch (start us, length us, event | category | flops | bytes accessed | tf_op | source)
XLA Modules:
  0.0 33.3 jit_solution(16496141991725608645)
XLA Ops:
  0.0 0.7 %copy-done.1 = f32[16,16]{1,0:T(8,128)S(1)} copy-done((f32[16,16]{1,0:T(8,128)S(1)}, f32[16,16]{1,0:T(8,128)}, u32[]{:S(2)}) %copy-start.1) | copy-done | bytes 1048
  0.7 0.9 %copy-done = bf16[16,3675]{1,0:T(8,128)(2,1)S(1)} copy-done((bf16[16,3675]{1,0:T(8,128)(2,1)S(1)}, bf16[16,3675]{1,0:T(8,128)(2,1)}, u32[]{:S(2)}) %copy-start) | copy-done | bytes 117624
  1.6 0.5 %pack.1 = (bf16[16,3968]{1,0:T(8,128)(2,1)S(1)}, bf16[64,128]{1,0:T(8,128)(2,1)S(1)}) custom-call(s32[1]{0:T(128)} %bitcast.mine_ref, bf16[16,3675]{1,0:T(8,128)(2,1)S(1)} %copy-done, s32[1,16]{1,0:T(1,128)S(1)} %bitcast.3, f32[1,49]{1,0:T(1,128)S(1)} %bitcast.4, f32[16,16]{1,0:T(8,128)S(1)} %copy-done.1, s32[4,8]{1,0:T(4,128)S(1)} %copy-done.2), custom_call_target="tpu_custom_call" | custom-call | tf_op jit(solution)/shard_map/pack/pallas_call | solution.py:116
  2.1 4.1 %collective-permute-start.1 = (bf16[16,3968]{1,0:T(8,128)(2,1)S(1)}, bf16[16,3968]{1,0:T(8,128)(2,1)S(1)}, u32[]{:S(2)}, u32[]{:S(2)}) collective-permute-start(bf16[16,3968]{1,0:T(8,128)(2,1)S(1)} %get-tuple-element.14.refs_0_.refs_7_.refs_11_), channel_id=1, source_target_pairs={{0,2},{1,3},{2,0},{3,1},{4,6},{5,7},{6,4},{7,5},{8,10},{9,11},{10,... | collective-permute-start | bytes 380936 | tf_op jit(solution)/shard_map/ppermute | solution.py:324
  6.2 2.4 %collective-permute-start.5 = (bf16[16,3968]{1,0:T(8,128)(2,1)S(1)}, bf16[16,3968]{1,0:T(8,128)(2,1)S(1)}, u32[]{:S(2)}, u32[]{:S(2)}) collective-permute-start(bf16[16,3968]{1,0:T(8,128)(2,1)S(1)} %get-tuple-element.14.refs_0_.refs_7_.refs_11_), channel_id=1, source_target_pairs={{0,24},{4,28},{8,16},{12,20},{16,8},{20,12},{24,0},{28,4},{1,25},{... | collective-permute-start | bytes 380936 | tf_op jit(solution)/shard_map/ppermute | solution.py:321
  8.7 0.5 %collective-permute-start.4 = (bf16[16,3968]{1,0:T(8,128)(2,1)S(1)}, bf16[16,3968]{1,0:T(8,128)(2,1)S(1)}, u32[]{:S(2)}, u32[]{:S(2)}) collective-permute-start(bf16[16,3968]{1,0:T(8,128)(2,1)S(1)} %get-tuple-element.14.refs_0_.refs_7_.refs_11_), channel_id=1, source_target_pairs={{0,16},{4,20},{8,24},{12,28},{16,0},{20,4},{24,8},{28,12},{1,17},{... | collective-permute-start | bytes 380936 | tf_op jit(solution)/shard_map/ppermute | solution.py:321
  9.2 0.5 %collective-permute-start.3 = (bf16[16,3968]{1,0:T(8,128)(2,1)S(1)}, bf16[16,3968]{1,0:T(8,128)(2,1)S(1)}, u32[]{:S(2)}, u32[]{:S(2)}) collective-permute-start(bf16[16,3968]{1,0:T(8,128)(2,1)S(1)} %get-tuple-element.14.refs_0_.refs_7_.refs_11_), channel_id=1, source_target_pairs={{0,8},{4,12},{8,0},{12,4},{16,24},{20,28},{24,16},{28,20},{1,9},{5... | collective-permute-start | bytes 380936 | tf_op jit(solution)/shard_map/ppermute | solution.py:321
  9.7 1.6 %collective-permute-start = (bf16[16,3968]{1,0:T(8,128)(2,1)S(1)}, bf16[16,3968]{1,0:T(8,128)(2,1)S(1)}, u32[]{:S(2)}, u32[]{:S(2)}) collective-permute-start(bf16[16,3968]{1,0:T(8,128)(2,1)S(1)} %get-tuple-element.14.refs_0_.refs_7_.refs_11_), channel_id=1, source_target_pairs={{0,1},{1,0},{2,3},{3,2},{4,5},{5,4},{6,7},{7,6},{8,9},{9,8},{10,11... | collective-permute-start | bytes 380936 | tf_op jit(solution)/shard_map/ppermute | solution.py:324
  11.3 1.2 %collective-permute-done.1.refs_2_.refs_9_ = bf16[16,3968]{1,0:T(8,128)(2,1)S(1)} collective-permute-done((bf16[16,3968]{1,0:T(8,128)(2,1)S(1)}, bf16[16,3968]{1,0:T(8,128)(2,1)S(1)}, u32[]{:S(2)}, u32[]{:S(2)}) %collective-permute-start.1) | collective-permute-done | bytes 127008 | tf_op jit(solution)/shard_map/ppermute | solution.py:324
  12.4 0.7 %collective-permute-start.2 = (bf16[16,3968]{1,0:T(8,128)(2,1)S(1)}, bf16[16,3968]{1,0:T(8,128)(2,1)S(1)}, u32[]{:S(2)}, u32[]{:S(2)}) collective-permute-start(bf16[16,3968]{1,0:T(8,128)(2,1)S(1)} %collective-permute-done.1.refs_2_.refs_9_), channel_id=1, source_target_pairs={{0,1},{1,0},{2,3},{3,2},{4,5},{5,4},{6,7},{7,6},{8,9},{9,8},{10,11... | collective-permute-start | bytes 380936 | tf_op jit(solution)/shard_map/ppermute | solution.py:324
  13.1 1.6 %collective-permute-done.4.refs_2_.refs_13_ = bf16[16,3968]{1,0:T(8,128)(2,1)S(1)} collective-permute-done((bf16[16,3968]{1,0:T(8,128)(2,1)S(1)}, bf16[16,3968]{1,0:T(8,128)(2,1)S(1)}, u32[]{:S(2)}, u32[]{:S(2)}) %collective-permute-start.4) | collective-permute-done | bytes 127008 | tf_op jit(solution)/shard_map/ppermute | solution.py:321
  14.7 0.1 collective-permute-done.3.refs_1_.refs_12_
  14.8 0.4 %collective-permute-start.8 = (bf16[16,3968]{1,0:T(8,128)(2,1)S(1)}, bf16[16,3968]{1,0:T(8,128)(2,1)S(1)}, u32[]{:S(2)}, u32[]{:S(2)}) collective-permute-start(bf16[16,3968]{1,0:T(8,128)(2,1)S(1)} %collective-permute-done.4.refs_2_.refs_13_), channel_id=1, source_target_pairs={{0,4},{4,0},{8,12},{12,8},{16,20},{20,16},{24,28},{28,24},{1,5},{5... | collective-permute-start | bytes 380936 | tf_op jit(solution)/shard_map/ppermute | solution.py:321
  15.2 0.7 %collective-permute-done.refs_1_.refs_8_ = bf16[16,3968]{1,0:T(8,128)(2,1)S(1)} collective-permute-done((bf16[16,3968]{1,0:T(8,128)(2,1)S(1)}, bf16[16,3968]{1,0:T(8,128)(2,1)S(1)}, u32[]{:S(2)}, u32[]{:S(2)}) %collective-permute-start) | collective-permute-done | bytes 127008 | tf_op jit(solution)/shard_map/ppermute | solution.py:324
  15.9 1.9 %collective-permute-done.2.refs_3_.refs_10_ = bf16[16,3968]{1,0:T(8,128)(2,1)S(1)} collective-permute-done((bf16[16,3968]{1,0:T(8,128)(2,1)S(1)}, bf16[16,3968]{1,0:T(8,128)(2,1)S(1)}, u32[]{:S(2)}, u32[]{:S(2)}) %collective-permute-start.2) | collective-permute-done | bytes 127008 | tf_op jit(solution)/shard_map/ppermute | solution.py:324
  17.8 0.2 rank.2
  18.0 0.4 %rank.3 = (bf16[64,128]{1,0:T(8,128)(2,1)S(1)}, f32[64,128]{1,0:T(8,128)S(1)}, s32[8,128]{1,0:T(8,128)S(1)}, bf16[32,64]{1,0:T(8,128)(2,1)S(1)}) custom-call(bf16[64,128]{1,0:T(8,128)(2,1)S(1)} %get-tuple-element.16.met_ref, bf16[16,3968]{1,0:T(8,128)(2,1)S(1)} %get-tuple-element.14.refs_0_.refs_7_.refs_11_, ...), custom_call_target="tpu_custom_call" | custom-call | flops 2000000000 | bytes 1000000 | tf_op jit(solution)/shard_map/rank/pallas_call | solution.py:205
  18.4 6.2 %energies.1 = f32[64,16]{1,0:T(8,128)S(1)} custom-call(s32[8,128]{1,0:T(8,128)S(1)} %get-tuple-element.15.refs_0_, s32[8,128]{1,0:T(8,128)S(1)} %get-tuple-element.17.refs_1_, bf16[64,64]{1,0:T(8,128)(2,1)S(1)} %get-tuple-element.18.refs_2_, f32[64,128]{1,0:T(8,128)S(1)} %get-tuple-element.19.refs_3_, bf16[64,128]{1,0:T(8,128)(2,1)S(1)} %get-tuple-element.20.refs_4_, ...), custom_call_target="tpu_custom_call" | custom-call | tf_op jit(solution)/shard_map/energies/pallas_call | solution.py:292
  24.6 3.5 %collective-permute-start.10 = (f32[16,16]{1,0:T(8,128)S(1)}, f32[16,16]{1,0:T(8,128)S(1)}, u32[]{:S(2)}, u32[]{:S(2)}) collective-permute-start(f32[16,16]{1,0:T(8,128)S(1)} %get-tuple-element.23), channel_id=1, source_target_pairs={{0,3},{1,2},{2,1},{3,0},{4,7},{5,6},{6,5},{7,4},{8,11},{9,10},{10,... | collective-permute-start | bytes 3080 | tf_op jit(solution)/shard_map/ppermute | solution.py:324
  28.2 0.9 %collective-permute-start.11 = (f32[16,16]{1,0:T(8,128)S(1)}, f32[16,16]{1,0:T(8,128)S(1)}, u32[]{:S(2)}, u32[]{:S(2)}) collective-permute-start(f32[16,16]{1,0:T(8,128)S(1)} %get-tuple-element.25), channel_id=1, source_target_pairs={{0,2},{1,3},{2,0},{3,1},{4,6},{5,7},{6,4},{7,5},{8,10},{9,11},{10,... | collective-permute-start | bytes 3080 | tf_op jit(solution)/shard_map/ppermute | solution.py:324
  29.1 1.1 %collective-permute-done.10 = f32[16,16]{1,0:T(8,128)S(1)} collective-permute-done((f32[16,16]{1,0:T(8,128)S(1)}, f32[16,16]{1,0:T(8,128)S(1)}, u32[]{:S(2)}, u32[]{:S(2)}) %collective-permute-start.10) | collective-permute-done | bytes 1056 | tf_op jit(solution)/shard_map/ppermute | solution.py:324
  30.1 1.7 %collective-permute-done.12 = f32[16,16]{1,0:T(8,128)S(1)} collective-permute-done((f32[16,16]{1,0:T(8,128)S(1)}, f32[16,16]{1,0:T(8,128)S(1)}, u32[]{:S(2)}, u32[]{:S(2)}) %collective-permute-start.12) | collective-permute-done | bytes 1056 | tf_op jit(solution)/shard_map/ppermute | solution.py:324
  31.8 0.9 %collective-permute-done.11 = f32[16,16]{1,0:T(8,128)S(1)} collective-permute-done((f32[16,16]{1,0:T(8,128)S(1)}, f32[16,16]{1,0:T(8,128)S(1)}, u32[]{:S(2)}, u32[]{:S(2)}) %collective-permute-start.11) | collective-permute-done | bytes 1056 | tf_op jit(solution)/shard_map/ppermute | solution.py:324
  32.7 0.6 %fusion.1 = f32[16,16]{1,0:T(8,128)} fusion(f32[16,16]{1,0:T(8,128)S(1)} %collective-permute-done.12, f32[16,16]{1,0:T(8,128)S(1)} %collective-permute-done.11, f32[16,16]{1,0:T(8,128)S(1)} %collective-permute-done.10, f32[64,16]{1,0:T(8,128)S(1)} %energies.1), kind=kLoop, calls=%fused_computation.2 | loop fusion | flops 768 | bytes 5120 | tf_op jit(solution)/shard_map/add | solution.py:337
  (18 shorter events, 0.0 us)
Async XLA Ops:
  0.0 0.7 %copy-start.1 = (f32[16,16]{1,0:T(8,128)S(1)}, f32[16,16]{1,0:T(8,128)}, u32[]{:S(2)}) copy-start(f32[16,16]{1,0:T(8,128)} %refs_3_.1) | copy-start | bytes 3076
  0.0 0.7 %copy-start.2 = (s32[4,8]{1,0:T(4,128)S(1)}, s32[4,8]{1,0:T(4,128)}, u32[]{:S(2)}) copy-start(s32[4,8]{1,0:T(4,128)} %refs_4_.1) | copy-start | bytes 388
  0.0 0.7 %copy-start.3 = (s32[16]{0:T(128)S(1)}, s32[16]{0:T(128)}, u32[]{:S(2)}) copy-start(s32[16]{0:T(128)} %param.6) | copy-start | bytes 196
  0.0 0.7 %copy-start.4 = (f32[49]{0:T(128)S(1)}, f32[49]{0:T(128)}, u32[]{:S(2)}) copy-start(f32[49]{0:T(128)} %param.7) | copy-start | bytes 592
  0.7 0.9 %copy-start = (bf16[16,3675]{1,0:T(8,128)(2,1)S(1)}, bf16[16,3675]{1,0:T(8,128)(2,1)}, u32[]{:S(2)}) copy-start(bf16[16,3675]{1,0:T(8,128)(2,1)} %refs_0_.1) | copy-start | bytes 352804
  2.1 10.3 %collective-permute-start.1 = (bf16[16,3968]{1,0:T(8,128)(2,1)S(1)}, bf16[16,3968]{1,0:T(8,128)(2,1)S(1)}, u32[]{:S(2)}, u32[]{:S(2)}) collective-permute-start(bf16[16,3968]{1,0:T(8,128)(2,1)S(1)} %get-tuple-element.14.refs_0_.refs_7_.refs_11_), channel_id=1, source_target_pairs={{0,2},{1,3},{2,0},{3,1},{4,6},{5,7},{6,4},{7,5},{8,10},{9,11},{10,... | collective-permute-start | bytes 380936 | tf_op jit(solution)/shard_map/ppermute | solution.py:324
  6.2 6.9 %collective-permute-start.5 = (bf16[16,3968]{1,0:T(8,128)(2,1)S(1)}, bf16[16,3968]{1,0:T(8,128)(2,1)S(1)}, u32[]{:S(2)}, u32[]{:S(2)}) collective-permute-start(bf16[16,3968]{1,0:T(8,128)(2,1)S(1)} %get-tuple-element.14.refs_0_.refs_7_.refs_11_), channel_id=1, source_target_pairs={{0,24},{4,28},{8,16},{12,20},{16,8},{20,12},{24,0},{28,4},{1,25},{... | collective-permute-start | bytes 380936 | tf_op jit(solution)/shard_map/ppermute | solution.py:321
  8.7 6.0 %collective-permute-start.4 = (bf16[16,3968]{1,0:T(8,128)(2,1)S(1)}, bf16[16,3968]{1,0:T(8,128)(2,1)S(1)}, u32[]{:S(2)}, u32[]{:S(2)}) collective-permute-start(bf16[16,3968]{1,0:T(8,128)(2,1)S(1)} %get-tuple-element.14.refs_0_.refs_7_.refs_11_), channel_id=1, source_target_pairs={{0,16},{4,20},{8,24},{12,28},{16,0},{20,4},{24,8},{28,12},{1,17},{... | collective-permute-start | bytes 380936 | tf_op jit(solution)/shard_map/ppermute | solution.py:321
  9.2 5.6 %collective-permute-start.3 = (bf16[16,3968]{1,0:T(8,128)(2,1)S(1)}, bf16[16,3968]{1,0:T(8,128)(2,1)S(1)}, u32[]{:S(2)}, u32[]{:S(2)}) collective-permute-start(bf16[16,3968]{1,0:T(8,128)(2,1)S(1)} %get-tuple-element.14.refs_0_.refs_7_.refs_11_), channel_id=1, source_target_pairs={{0,8},{4,12},{8,0},{12,4},{16,24},{20,28},{24,16},{28,20},{1,9},{5... | collective-permute-start | bytes 380936 | tf_op jit(solution)/shard_map/ppermute | solution.py:321
  9.7 6.2 %collective-permute-start = (bf16[16,3968]{1,0:T(8,128)(2,1)S(1)}, bf16[16,3968]{1,0:T(8,128)(2,1)S(1)}, u32[]{:S(2)}, u32[]{:S(2)}) collective-permute-start(bf16[16,3968]{1,0:T(8,128)(2,1)S(1)} %get-tuple-element.14.refs_0_.refs_7_.refs_11_), channel_id=1, source_target_pairs={{0,1},{1,0},{2,3},{3,2},{4,5},{5,4},{6,7},{7,6},{8,9},{9,8},{10,11... | collective-permute-start | bytes 380936 | tf_op jit(solution)/shard_map/ppermute | solution.py:324
  12.4 5.3 %collective-permute-start.2 = (bf16[16,3968]{1,0:T(8,128)(2,1)S(1)}, bf16[16,3968]{1,0:T(8,128)(2,1)S(1)}, u32[]{:S(2)}, u32[]{:S(2)}) collective-permute-start(bf16[16,3968]{1,0:T(8,128)(2,1)S(1)} %collective-permute-done.1.refs_2_.refs_9_), channel_id=1, source_target_pairs={{0,1},{1,0},{2,3},{3,2},{4,5},{5,4},{6,7},{7,6},{8,9},{9,8},{10,11... | collective-permute-start | bytes 380936 | tf_op jit(solution)/shard_map/ppermute | solution.py:324
  13.1 4.9 %collective-permute-start.6 = (bf16[16,3968]{1,0:T(8,128)(2,1)S(1)}, bf16[16,3968]{1,0:T(8,128)(2,1)S(1)}, u32[]{:S(2)}, u32[]{:S(2)}) collective-permute-start(bf16[16,3968]{1,0:T(8,128)(2,1)S(1)} %get-tuple-element.14.refs_0_.refs_7_.refs_11_), channel_id=1, source_target_pairs={{0,4},{4,0},{8,12},{12,8},{16,20},{20,16},{24,28},{28,24},{1,5},{5... | collective-permute-start | bytes 380936 | tf_op jit(solution)/shard_map/ppermute | solution.py:321
  14.7 3.3 %collective-permute-start.9 = (bf16[16,3968]{1,0:T(8,128)(2,1)S(1)}, bf16[16,3968]{1,0:T(8,128)(2,1)S(1)}, u32[]{:S(2)}, u32[]{:S(2)}) collective-permute-start(bf16[16,3968]{1,0:T(8,128)(2,1)S(1)} %collective-permute-done.5.refs_3_.refs_14_), channel_id=1, source_target_pairs={{0,4},{4,0},{8,12},{12,8},{16,20},{20,16},{24,28},{28,24},{1,5},{5... | collective-permute-start | bytes 380936 | tf_op jit(solution)/shard_map/ppermute | solution.py:321
  14.8 3.2 %collective-permute-start.8 = (bf16[16,3968]{1,0:T(8,128)(2,1)S(1)}, bf16[16,3968]{1,0:T(8,128)(2,1)S(1)}, u32[]{:S(2)}, u32[]{:S(2)}) collective-permute-start(bf16[16,3968]{1,0:T(8,128)(2,1)S(1)} %collective-permute-done.4.refs_2_.refs_13_), channel_id=1, source_target_pairs={{0,4},{4,0},{8,12},{12,8},{16,20},{20,16},{24,28},{28,24},{1,5},{5... | collective-permute-start | bytes 380936 | tf_op jit(solution)/shard_map/ppermute | solution.py:321
  15.9 2.1 %collective-permute-start.7 = (bf16[16,3968]{1,0:T(8,128)(2,1)S(1)}, bf16[16,3968]{1,0:T(8,128)(2,1)S(1)}, u32[]{:S(2)}, u32[]{:S(2)}) collective-permute-start(bf16[16,3968]{1,0:T(8,128)(2,1)S(1)} %collective-permute-done.3.refs_1_.refs_12_), channel_id=1, source_target_pairs={{0,4},{4,0},{8,12},{12,8},{16,20},{20,16},{24,28},{28,24},{1,5},{5... | collective-permute-start | bytes 380936 | tf_op jit(solution)/shard_map/ppermute | solution.py:321
  24.6 5.5 %collective-permute-start.10 = (f32[16,16]{1,0:T(8,128)S(1)}, f32[16,16]{1,0:T(8,128)S(1)}, u32[]{:S(2)}, u32[]{:S(2)}) collective-permute-start(f32[16,16]{1,0:T(8,128)S(1)} %get-tuple-element.23), channel_id=1, source_target_pairs={{0,3},{1,2},{2,1},{3,0},{4,7},{5,6},{6,5},{7,4},{8,11},{9,10},{10,... | collective-permute-start | bytes 3080 | tf_op jit(solution)/shard_map/ppermute | solution.py:324
  28.2 3.7 %collective-permute-start.12 = (f32[16,16]{1,0:T(8,128)S(1)}, f32[16,16]{1,0:T(8,128)S(1)}, u32[]{:S(2)}, u32[]{:S(2)}) collective-permute-start(f32[16,16]{1,0:T(8,128)S(1)} %get-tuple-element.24), channel_id=1, source_target_pairs={{0,1},{1,0},{2,3},{3,2},{4,5},{5,4},{6,7},{7,6},{8,9},{9,8},{10,11... | collective-permute-start | bytes 3080 | tf_op jit(solution)/shard_map/ppermute | solution.py:324
  28.2 4.5 %collective-permute-start.11 = (f32[16,16]{1,0:T(8,128)S(1)}, f32[16,16]{1,0:T(8,128)S(1)}, u32[]{:S(2)}, u32[]{:S(2)}) collective-permute-start(f32[16,16]{1,0:T(8,128)S(1)} %get-tuple-element.25), channel_id=1, source_target_pairs={{0,2},{1,3},{2,0},{3,1},{4,6},{5,7},{6,4},{7,5},{8,10},{9,11},{10,... | collective-permute-start | bytes 3080 | tf_op jit(solution)/shard_map/ppermute | solution.py:324

commit v4 on v3

--- a/solution.py
+++ b/solution.py
@@ -152,7 +152,7 @@
     number = sorted_ref.shape[0]
     lane = iota((number, LANES), 1)
     for p in range(P_SIZE):
-        values = jnp.where(lane < STRIDE, sorted_ref[:, p * STRIDE : p * STRIDE + LANES], owner)
+        values = jnp.where(lane < STRIDE, sorted_ref[:, p * STRIDE : p * STRIDE + LANES].astype(jnp.float32), owner)
         x_ref[pl.ds(first_ref[0, p], number), :] = values
     total = first_ref[0, P_SIZE]
     counts = choose(total, options)
@@ -231,8 +231,8 @@
     for copy in copies:
         copy.start()
     product[...] = jnp.zeros_like(product)
-    col_sorted[...] = dot(col_which[...], jnp.concatenate([part[...] for part in far_parts], axis=0))
-    row_sorted[...] = dot(row_which[...], jnp.concatenate([part[...] for part in near_parts], axis=0))
+    col_sorted[...] = dot(col_which[...], jnp.concatenate([part[...] for part in far_parts], axis=0)).astype(jnp.bfloat16)
+    row_sorted[...] = dot(row_which[...], jnp.concatenate([part[...] for part in near_parts], axis=0)).astype(jnp.bfloat16)
     copies[0].wait()
     col_total, col_counts = spread(col_sorted, col_owner[...], col_first, col_f, COLS)
     copies[1].wait()
@@ -295,8 +295,8 @@
         in_specs=[VMEM] * (7 + len(near) + len(far)),
         out_specs=VMEM,
         scratch_shapes=[
-            pltpu.VMEM((rows, PACKED), jnp.float32),
-            pltpu.VMEM((cols, PACKED), jnp.float32),
+            pltpu.VMEM((rows, PACKED), jnp.bfloat16),
+            pltpu.VMEM((cols, PACKED), jnp.bfloat16),
             pltpu.VMEM((row_room, LANES), jnp.float32),
             pltpu.VMEM((col_room, LANES), jnp.float32),
             pltpu.VMEM((col_room, LANES), jnp.bfloat16),

time: 33.7 us -> 32.8 us (0.973); the launches traced: 33.3 us -> 32.8 us
  Pallas kernels: 7.28 us -> 6.41 us
    pallas_call x1, Pallas kernels: 6.22 us -> 5.36 us  [local_terms(): pl.pallas_call(functools.partial(energies, (len(near), len(far))), out_sh...]
where the time goes in v4:
time: 32.8 us
  starting transfers between devices  14.8 us (45%)
  waiting for transfers between devices  9.35 us (29%)
  Pallas kernels  6.41 us (20%)
  local copies, waits for them, and re-layouts  1.6 us (5%)
  other arithmetic  0.6 us (2%)
    ppermute x6, starting transfers between devices, across(): return lax.ppermute(array, 'narrow', [(i, i ^ apart) for i in range(subs)])  10.9 us
    ppermute x6, waiting for transfers between devices, across(): return lax.ppermute(array, 'narrow', [(i, i ^ apart) for i in range(subs)])  7.64 us
    pallas_call x1, Pallas kernels, local_terms(): pl.pallas_call(functools.partial(energies, (len(near), len(far))), out_sh...  5.36 us
    ppermute x7, starting transfers between devices, swap(): return lax.ppermute(array, 'group', [(i, i ^ apart) for i in range(groups)])  3.89 us
    ppermute x7, waiting for transfers between devices, swap(): return lax.ppermute(array, 'group', [(i, i ^ apart) for i in range(groups)])  1.71 us
    unnamed x10, local copies, waits for them, and re-layouts  1.6 us
  transfers between devices with their start and end apart: 13, of which 8 were waited for; matrix products, arithmetic and copies ran while one was open for 0% of the time, Pallas kernels for 1%

profile of v4, /device:TPU:0, one launch (start us, length us, event | category | flops | bytes accessed | tf_op | source)
XLA Modules:
  0.0 32.8 jit_solution(18311861636860224797)
XLA Ops:
  0.0 0.7 %copy-done.1 = f32[16,16]{1,0:T(8,128)S(1)} copy-done((f32[16,16]{1,0:T(8,128)S(1)}, f32[16,16]{1,0:T(8,128)}, u32[]{:S(2)}) %copy-start.1) | copy-done | bytes 1048
  0.7 0.9 %copy-done = bf16[16,3675]{1,0:T(8,128)(2,1)S(1)} copy-done((bf16[16,3675]{1,0:T(8,128)(2,1)S(1)}, bf16[16,3675]{1,0:T(8,128)(2,1)}, u32[]{:S(2)}) %copy-start) | copy-done | bytes 117624
  1.6 0.5 %pack.1 = (bf16[16,3968]{1,0:T(8,128)(2,1)S(1)}, bf16[64,128]{1,0:T(8,128)(2,1)S(1)}) custom-call(s32[1]{0:T(128)} %bitcast.mine_ref, bf16[16,3675]{1,0:T(8,128)(2,1)S(1)} %copy-done, s32[1,16]{1,0:T(1,128)S(1)} %bitcast.3, f32[1,49]{1,0:T(1,128)S(1)} %bitcast.4, f32[16,16]{1,0:T(8,128)S(1)} %copy-done.1, s32[4,8]{1,0:T(4,128)S(1)} %copy-done.2), custom_call_target="tpu_custom_call" | custom-call | tf_op jit(solution)/shard_map/pack/pallas_call | solution.py:116
  2.1 4.1 %collective-permute-start.1 = (bf16[16,3968]{1,0:T(8,128)(2,1)S(1)}, bf16[16,3968]{1,0:T(8,128)(2,1)S(1)}, u32[]{:S(2)}, u32[]{:S(2)}) collective-permute-start(bf16[16,3968]{1,0:T(8,128)(2,1)S(1)} %get-tuple-element.14.refs_0_.refs_7_.refs_11_), channel_id=1, source_target_pairs={{0,2},{1,3},{2,0},{3,1},{4,6},{5,7},{6,4},{7,5},{8,10},{9,11},{10,... | collective-permute-start | bytes 380936 | tf_op jit(solution)/shard_map/ppermute | solution.py:324
  6.2 2.4 %collective-permute-start.5 = (bf16[16,3968]{1,0:T(8,128)(2,1)S(1)}, bf16[16,3968]{1,0:T(8,128)(2,1)S(1)}, u32[]{:S(2)}, u32[]{:S(2)}) collective-permute-start(bf16[16,3968]{1,0:T(8,128)(2,1)S(1)} %get-tuple-element.14.refs_0_.refs_7_.refs_11_), channel_id=1, source_target_pairs={{0,24},{4,28},{8,16},{12,20},{16,8},{20,12},{24,0},{28,4},{1,25},{... | collective-permute-start | bytes 380936 | tf_op jit(solution)/shard_map/ppermute | solution.py:321
  8.7 0.5 %collective-permute-start.4 = (bf16[16,3968]{1,0:T(8,128)(2,1)S(1)}, bf16[16,3968]{1,0:T(8,128)(2,1)S(1)}, u32[]{:S(2)}, u32[]{:S(2)}) collective-permute-start(bf16[16,3968]{1,0:T(8,128)(2,1)S(1)} %get-tuple-element.14.refs_0_.refs_7_.refs_11_), channel_id=1, source_target_pairs={{0,16},{4,20},{8,24},{12,28},{16,0},{20,4},{24,8},{28,12},{1,17},{... | collective-permute-start | bytes 380936 | tf_op jit(solution)/shard_map/ppermute | solution.py:321
  9.2 0.5 %collective-permute-start.3 = (bf16[16,3968]{1,0:T(8,128)(2,1)S(1)}, bf16[16,3968]{1,0:T(8,128)(2,1)S(1)}, u32[]{:S(2)}, u32[]{:S(2)}) collective-permute-start(bf16[16,3968]{1,0:T(8,128)(2,1)S(1)} %get-tuple-element.14.refs_0_.refs_7_.refs_11_), channel_id=1, source_target_pairs={{0,8},{4,12},{8,0},{12,4},{16,24},{20,28},{24,16},{28,20},{1,9},{5... | collective-permute-start | bytes 380936 | tf_op jit(solution)/shard_map/ppermute | solution.py:321
  9.7 1.6 %collective-permute-start = (bf16[16,3968]{1,0:T(8,128)(2,1)S(1)}, bf16[16,3968]{1,0:T(8,128)(2,1)S(1)}, u32[]{:S(2)}, u32[]{:S(2)}) collective-permute-start(bf16[16,3968]{1,0:T(8,128)(2,1)S(1)} %get-tuple-element.14.refs_0_.refs_7_.refs_11_), channel_id=1, source_target_pairs={{0,1},{1,0},{2,3},{3,2},{4,5},{5,4},{6,7},{7,6},{8,9},{9,8},{10,11... | collective-permute-start | bytes 380936 | tf_op jit(solution)/shard_map/ppermute | solution.py:324
  11.3 1.2 %collective-permute-done.1.refs_2_.refs_9_ = bf16[16,3968]{1,0:T(8,128)(2,1)S(1)} collective-permute-done((bf16[16,3968]{1,0:T(8,128)(2,1)S(1)}, bf16[16,3968]{1,0:T(8,128)(2,1)S(1)}, u32[]{:S(2)}, u32[]{:S(2)}) %collective-permute-start.1) | collective-permute-done | bytes 127008 | tf_op jit(solution)/shard_map/ppermute | solution.py:324
  12.4 0.7 %collective-permute-start.2 = (bf16[16,3968]{1,0:T(8,128)(2,1)S(1)}, bf16[16,3968]{1,0:T(8,128)(2,1)S(1)}, u32[]{:S(2)}, u32[]{:S(2)}) collective-permute-start(bf16[16,3968]{1,0:T(8,128)(2,1)S(1)} %collective-permute-done.1.refs_2_.refs_9_), channel_id=1, source_target_pairs={{0,1},{1,0},{2,3},{3,2},{4,5},{5,4},{6,7},{7,6},{8,9},{9,8},{10,11... | collective-permute-start | bytes 380936 | tf_op jit(solution)/shard_map/ppermute | solution.py:324
  13.1 1.6 %collective-permute-done.4.refs_2_.refs_13_ = bf16[16,3968]{1,0:T(8,128)(2,1)S(1)} collective-permute-done((bf16[16,3968]{1,0:T(8,128)(2,1)S(1)}, bf16[16,3968]{1,0:T(8,128)(2,1)S(1)}, u32[]{:S(2)}, u32[]{:S(2)}) %collective-permute-start.4) | collective-permute-done | bytes 127008 | tf_op jit(solution)/shard_map/ppermute | solution.py:321
  14.7 0.1 collective-permute-done.3.refs_1_.refs_12_
  14.8 0.4 %collective-permute-start.8 = (bf16[16,3968]{1,0:T(8,128)(2,1)S(1)}, bf16[16,3968]{1,0:T(8,128)(2,1)S(1)}, u32[]{:S(2)}, u32[]{:S(2)}) collective-permute-start(bf16[16,3968]{1,0:T(8,128)(2,1)S(1)} %collective-permute-done.4.refs_2_.refs_13_), channel_id=1, source_target_pairs={{0,4},{4,0},{8,12},{12,8},{16,20},{20,16},{24,28},{28,24},{1,5},{5... | collective-permute-start | bytes 380936 | tf_op jit(solution)/shard_map/ppermute | solution.py:321
  15.2 0.7 %collective-permute-done.refs_1_.refs_8_ = bf16[16,3968]{1,0:T(8,128)(2,1)S(1)} collective-permute-done((bf16[16,3968]{1,0:T(8,128)(2,1)S(1)}, bf16[16,3968]{1,0:T(8,128)(2,1)S(1)}, u32[]{:S(2)}, u32[]{:S(2)}) %collective-permute-start) | collective-permute-done | bytes 127008 | tf_op jit(solution)/shard_map/ppermute | solution.py:324
  15.9 1.9 %collective-permute-done.2.refs_3_.refs_10_ = bf16[16,3968]{1,0:T(8,128)(2,1)S(1)} collective-permute-done((bf16[16,3968]{1,0:T(8,128)(2,1)S(1)}, bf16[16,3968]{1,0:T(8,128)(2,1)S(1)}, u32[]{:S(2)}, u32[]{:S(2)}) %collective-permute-start.2) | collective-permute-done | bytes 127008 | tf_op jit(solution)/shard_map/ppermute | solution.py:324
  17.8 0.2 rank.2
  18.0 0.4 %rank.3 = (bf16[64,128]{1,0:T(8,128)(2,1)S(1)}, f32[64,128]{1,0:T(8,128)S(1)}, s32[8,128]{1,0:T(8,128)S(1)}, bf16[32,64]{1,0:T(8,128)(2,1)S(1)}) custom-call(bf16[64,128]{1,0:T(8,128)(2,1)S(1)} %get-tuple-element.16.met_ref, bf16[16,3968]{1,0:T(8,128)(2,1)S(1)} %get-tuple-element.14.refs_0_.refs_7_.refs_11_, ...), custom_call_target="tpu_custom_call" | custom-call | flops 2000000000 | bytes 1000000 | tf_op jit(solution)/shard_map/rank/pallas_call | solution.py:205
  18.4 5.4 %energies.1 = f32[64,16]{1,0:T(8,128)S(1)} custom-call(s32[8,128]{1,0:T(8,128)S(1)} %get-tuple-element.15.refs_0_, s32[8,128]{1,0:T(8,128)S(1)} %get-tuple-element.17.refs_1_, bf16[64,64]{1,0:T(8,128)(2,1)S(1)} %get-tuple-element.18.refs_2_, f32[64,128]{1,0:T(8,128)S(1)} %get-tuple-element.19.refs_3_, bf16[64,128]{1,0:T(8,128)(2,1)S(1)} %get-tuple-element.20.refs_4_, ...), custom_call_target="tpu_custom_call" | custom-call | tf_op jit(solution)/shard_map/energies/pallas_call | solution.py:292
  23.8 3.9 %collective-permute-start.10 = (f32[16,16]{1,0:T(8,128)S(1)}, f32[16,16]{1,0:T(8,128)S(1)}, u32[]{:S(2)}, u32[]{:S(2)}) collective-permute-start(f32[16,16]{1,0:T(8,128)S(1)} %get-tuple-element.23), channel_id=1, source_target_pairs={{0,3},{1,2},{2,1},{3,0},{4,7},{5,6},{6,5},{7,4},{8,11},{9,10},{10,... | collective-permute-start | bytes 3080 | tf_op jit(solution)/shard_map/ppermute | solution.py:324
  27.7 0.6 %collective-permute-start.11 = (f32[16,16]{1,0:T(8,128)S(1)}, f32[16,16]{1,0:T(8,128)S(1)}, u32[]{:S(2)}, u32[]{:S(2)}) collective-permute-start(f32[16,16]{1,0:T(8,128)S(1)} %get-tuple-element.25), channel_id=1, source_target_pairs={{0,2},{1,3},{2,0},{3,1},{4,6},{5,7},{6,4},{7,5},{8,10},{9,11},{10,... | collective-permute-start | bytes 3080 | tf_op jit(solution)/shard_map/ppermute | solution.py:324
  28.3 1.0 %collective-permute-done.10 = f32[16,16]{1,0:T(8,128)S(1)} collective-permute-done((f32[16,16]{1,0:T(8,128)S(1)}, f32[16,16]{1,0:T(8,128)S(1)}, u32[]{:S(2)}, u32[]{:S(2)}) %collective-permute-start.10) | collective-permute-done | bytes 1056 | tf_op jit(solution)/shard_map/ppermute | solution.py:324
  29.3 2.0 %collective-permute-done.12 = f32[16,16]{1,0:T(8,128)S(1)} collective-permute-done((f32[16,16]{1,0:T(8,128)S(1)}, f32[16,16]{1,0:T(8,128)S(1)}, u32[]{:S(2)}, u32[]{:S(2)}) %collective-permute-start.12) | collective-permute-done | bytes 1056 | tf_op jit(solution)/shard_map/ppermute | solution.py:324
  31.3 0.9 %collective-permute-done.11 = f32[16,16]{1,0:T(8,128)S(1)} collective-permute-done((f32[16,16]{1,0:T(8,128)S(1)}, f32[16,16]{1,0:T(8,128)S(1)}, u32[]{:S(2)}, u32[]{:S(2)}) %collective-permute-start.11) | collective-permute-done | bytes 1056 | tf_op jit(solution)/shard_map/ppermute | solution.py:324
  32.2 0.6 %fusion.1 = f32[16,16]{1,0:T(8,128)} fusion(f32[16,16]{1,0:T(8,128)S(1)} %collective-permute-done.12, f32[16,16]{1,0:T(8,128)S(1)} %collective-permute-done.11, f32[16,16]{1,0:T(8,128)S(1)} %collective-permute-done.10, f32[64,16]{1,0:T(8,128)S(1)} %energies.1), kind=kLoop, calls=%fused_computation.2 | loop fusion | flops 768 | bytes 5120 | tf_op jit(solution)/shard_map/add | solution.py:337
  (18 shorter events, 0.0 us)
Async XLA Ops:
  0.0 0.7 %copy-start.1 = (f32[16,16]{1,0:T(8,128)S(1)}, f32[16,16]{1,0:T(8,128)}, u32[]{:S(2)}) copy-start(f32[16,16]{1,0:T(8,128)} %refs_3_.1) | copy-start | bytes 3076
  0.0 0.7 %copy-start.2 = (s32[4,8]{1,0:T(4,128)S(1)}, s32[4,8]{1,0:T(4,128)}, u32[]{:S(2)}) copy-start(s32[4,8]{1,0:T(4,128)} %refs_4_.1) | copy-start | bytes 388
  0.0 0.7 %copy-start.3 = (s32[16]{0:T(128)S(1)}, s32[16]{0:T(128)}, u32[]{:S(2)}) copy-start(s32[16]{0:T(128)} %param.6) | copy-start | bytes 196
  0.0 0.7 %copy-start.4 = (f32[49]{0:T(128)S(1)}, f32[49]{0:T(128)}, u32[]{:S(2)}) copy-start(f32[49]{0:T(128)} %param.7) | copy-start | bytes 592
  0.7 0.9 %copy-start = (bf16[16,3675]{1,0:T(8,128)(2,1)S(1)}, bf16[16,3675]{1,0:T(8,128)(2,1)}, u32[]{:S(2)}) copy-start(bf16[16,3675]{1,0:T(8,128)(2,1)} %refs_0_.1) | copy-start | bytes 352804
  2.1 10.3 %collective-permute-start.1 = (bf16[16,3968]{1,0:T(8,128)(2,1)S(1)}, bf16[16,3968]{1,0:T(8,128)(2,1)S(1)}, u32[]{:S(2)}, u32[]{:S(2)}) collective-permute-start(bf16[16,3968]{1,0:T(8,128)(2,1)S(1)} %get-tuple-element.14.refs_0_.refs_7_.refs_11_), channel_id=1, source_target_pairs={{0,2},{1,3},{2,0},{3,1},{4,6},{5,7},{6,4},{7,5},{8,10},{9,11},{10,... | collective-permute-start | bytes 380936 | tf_op jit(solution)/shard_map/ppermute | solution.py:324
  6.2 6.9 %collective-permute-start.5 = (bf16[16,3968]{1,0:T(8,128)(2,1)S(1)}, bf16[16,3968]{1,0:T(8,128)(2,1)S(1)}, u32[]{:S(2)}, u32[]{:S(2)}) collective-permute-start(bf16[16,3968]{1,0:T(8,128)(2,1)S(1)} %get-tuple-element.14.refs_0_.refs_7_.refs_11_), channel_id=1, source_target_pairs={{0,24},{4,28},{8,16},{12,20},{16,8},{20,12},{24,0},{28,4},{1,25},{... | collective-permute-start | bytes 380936 | tf_op jit(solution)/shard_map/ppermute | solution.py:321
  8.7 6.0 %collective-permute-start.4 = (bf16[16,3968]{1,0:T(8,128)(2,1)S(1)}, bf16[16,3968]{1,0:T(8,128)(2,1)S(1)}, u32[]{:S(2)}, u32[]{:S(2)}) collective-permute-start(bf16[16,3968]{1,0:T(8,128)(2,1)S(1)} %get-tuple-element.14.refs_0_.refs_7_.refs_11_), channel_id=1, source_target_pairs={{0,16},{4,20},{8,24},{12,28},{16,0},{20,4},{24,8},{28,12},{1,17},{... | collective-permute-start | bytes 380936 | tf_op jit(solution)/shard_map/ppermute | solution.py:321
  9.2 5.6 %collective-permute-start.3 = (bf16[16,3968]{1,0:T(8,128)(2,1)S(1)}, bf16[16,3968]{1,0:T(8,128)(2,1)S(1)}, u32[]{:S(2)}, u32[]{:S(2)}) collective-permute-start(bf16[16,3968]{1,0:T(8,128)(2,1)S(1)} %get-tuple-element.14.refs_0_.refs_7_.refs_11_), channel_id=1, source_target_pairs={{0,8},{4,12},{8,0},{12,4},{16,24},{20,28},{24,16},{28,20},{1,9},{5... | collective-permute-start | bytes 380936 | tf_op jit(solution)/shard_map/ppermute | solution.py:321
  9.7 6.2 %collective-permute-start = (bf16[16,3968]{1,0:T(8,128)(2,1)S(1)}, bf16[16,3968]{1,0:T(8,128)(2,1)S(1)}, u32[]{:S(2)}, u32[]{:S(2)}) collective-permute-start(bf16[16,3968]{1,0:T(8,128)(2,1)S(1)} %get-tuple-element.14.refs_0_.refs_7_.refs_11_), channel_id=1, source_target_pairs={{0,1},{1,0},{2,3},{3,2},{4,5},{5,4},{6,7},{7,6},{8,9},{9,8},{10,11... | collective-permute-start | bytes 380936 | tf_op jit(solution)/shard_map/ppermute | solution.py:324
  12.4 5.3 %collective-permute-start.2 = (bf16[16,3968]{1,0:T(8,128)(2,1)S(1)}, bf16[16,3968]{1,0:T(8,128)(2,1)S(1)}, u32[]{:S(2)}, u32[]{:S(2)}) collective-permute-start(bf16[16,3968]{1,0:T(8,128)(2,1)S(1)} %collective-permute-done.1.refs_2_.refs_9_), channel_id=1, source_target_pairs={{0,1},{1,0},{2,3},{3,2},{4,5},{5,4},{6,7},{7,6},{8,9},{9,8},{10,11... | collective-permute-start | bytes 380936 | tf_op jit(solution)/shard_map/ppermute | solution.py:324
  13.1 4.9 %collective-permute-start.6 = (bf16[16,3968]{1,0:T(8,128)(2,1)S(1)}, bf16[16,3968]{1,0:T(8,128)(2,1)S(1)}, u32[]{:S(2)}, u32[]{:S(2)}) collective-permute-start(bf16[16,3968]{1,0:T(8,128)(2,1)S(1)} %get-tuple-element.14.refs_0_.refs_7_.refs_11_), channel_id=1, source_target_pairs={{0,4},{4,0},{8,12},{12,8},{16,20},{20,16},{24,28},{28,24},{1,5},{5... | collective-permute-start | bytes 380936 | tf_op jit(solution)/shard_map/ppermute | solution.py:321
  14.7 3.3 %collective-permute-start.9 = (bf16[16,3968]{1,0:T(8,128)(2,1)S(1)}, bf16[16,3968]{1,0:T(8,128)(2,1)S(1)}, u32[]{:S(2)}, u32[]{:S(2)}) collective-permute-start(bf16[16,3968]{1,0:T(8,128)(2,1)S(1)} %collective-permute-done.5.refs_3_.refs_14_), channel_id=1, source_target_pairs={{0,4},{4,0},{8,12},{12,8},{16,20},{20,16},{24,28},{28,24},{1,5},{5... | collective-permute-start | bytes 380936 | tf_op jit(solution)/shard_map/ppermute | solution.py:321
  14.8 3.2 %collective-permute-start.8 = (bf16[16,3968]{1,0:T(8,128)(2,1)S(1)}, bf16[16,3968]{1,0:T(8,128)(2,1)S(1)}, u32[]{:S(2)}, u32[]{:S(2)}) collective-permute-start(bf16[16,3968]{1,0:T(8,128)(2,1)S(1)} %collective-permute-done.4.refs_2_.refs_13_), channel_id=1, source_target_pairs={{0,4},{4,0},{8,12},{12,8},{16,20},{20,16},{24,28},{28,24},{1,5},{5... | collective-permute-start | bytes 380936 | tf_op jit(solution)/shard_map/ppermute | solution.py:321
  15.9 2.1 %collective-permute-start.7 = (bf16[16,3968]{1,0:T(8,128)(2,1)S(1)}, bf16[16,3968]{1,0:T(8,128)(2,1)S(1)}, u32[]{:S(2)}, u32[]{:S(2)}) collective-permute-start(bf16[16,3968]{1,0:T(8,128)(2,1)S(1)} %collective-permute-done.3.refs_1_.refs_12_), channel_id=1, source_target_pairs={{0,4},{4,0},{8,12},{12,8},{16,20},{20,16},{24,28},{28,24},{1,5},{5... | collective-permute-start | bytes 380936 | tf_op jit(solution)/shard_map/ppermute | solution.py:321
  23.8 5.5 %collective-permute-start.10 = (f32[16,16]{1,0:T(8,128)S(1)}, f32[16,16]{1,0:T(8,128)S(1)}, u32[]{:S(2)}, u32[]{:S(2)}) collective-permute-start(f32[16,16]{1,0:T(8,128)S(1)} %get-tuple-element.23), channel_id=1, source_target_pairs={{0,3},{1,2},{2,1},{3,0},{4,7},{5,6},{6,5},{7,4},{8,11},{9,10},{10,... | collective-permute-start | bytes 3080 | tf_op jit(solution)/shard_map/ppermute | solution.py:324
  27.7 3.7 %collective-permute-start.12 = (f32[16,16]{1,0:T(8,128)S(1)}, f32[16,16]{1,0:T(8,128)S(1)}, u32[]{:S(2)}, u32[]{:S(2)}) collective-permute-start(f32[16,16]{1,0:T(8,128)S(1)} %get-tuple-element.24), channel_id=1, source_target_pairs={{0,1},{1,0},{2,3},{3,2},{4,5},{5,4},{6,7},{7,6},{8,9},{9,8},{10,11... | collective-permute-start | bytes 3080 | tf_op jit(solution)/shard_map/ppermute | solution.py:324
  27.7 4.5 %collective-permute-start.11 = (f32[16,16]{1,0:T(8,128)S(1)}, f32[16,16]{1,0:T(8,128)S(1)}, u32[]{:S(2)}, u32[]{:S(2)}) collective-permute-start(f32[16,16]{1,0:T(8,128)S(1)} %get-tuple-element.25), channel_id=1, source_target_pairs={{0,2},{1,3},{2,0},{3,1},{4,6},{5,7},{6,4},{7,5},{8,10},{9,11},{10,... | collective-permute-start | bytes 3080 | tf_op jit(solution)/shard_map/ppermute | solution.py:324

commit v5 on v4

--- a/solution.py
+++ b/solution.py
@@ -16,11 +16,24 @@
 ALPHA_AT = PV + 3
 FEATURES = 5
 STRIDE = PV + FEATURES
-WIDE = P_SIZE * STRIDE
-PACKED = (WIDE + 1 + 2 * NPROBE + LANES - 1) // LANES * LANES
-TAIL = WIDE // LANES * LANES
-COUNT_AT = WIDE - TAIL
+TILES = (P_SIZE * STRIDE + 1 + 2 * NPROBE + LANES - 1) // LANES
+PACKED = TILES * LANES
+TAIL = PACKED - LANES
+COUNT_AT = STRIDE
 PROBE_AT = COUNT_AT + 1
+
+
+def layout():
+    rest, left = LANES - STRIDE, 2 * (LANES - STRIDE) - STRIDE
+    pairs = TILES // 2
+    places = [[(tile, 0, 0, STRIDE)] for tile in range(TILES)]
+    places += [[(2 * k, STRIDE, 0, rest), (2 * k + 1, STRIDE, rest, STRIDE - rest)] for k in range(pairs)]
+    each = STRIDE // left
+    for j in range(P_SIZE - len(places)):
+        places.append([(2 * (each * j + i) + 1, LANES - left, left * i, left) for i in range(each)])
+    return places
+
+
 OWNER_AT = STRIDE
 ROWS = ((1792, 1), (2048, 1), (1024, None))
 COLS = ((896, 2), (1024, None))
@@ -86,26 +99,27 @@
     alphas = [part.astype(jnp.bfloat16) for part in parts(alpha)[:2]]
     tiles = [None] * (PACKED // LANES)
 
-    def put(values, start):
-        tile, shift = divmod(start, LANES)
-        moved = pltpu.roll(values, shift, 1) if shift else values
-        first = jnp.where(lane >= shift, moved, jnp.bfloat16(0)) if shift else moved
-        tiles[tile] = first if tiles[tile] is None else tiles[tile] + first
-        if shift and tile + 1 < len(tiles):
-            tiles[tile + 1] = jnp.where(lane < shift, moved, jnp.bfloat16(0))
-
+    def put(values, places):
+        for tile, there, here, lanes in places:
+            shift = (there - here) % LANES
+            moved = pltpu.roll(values, shift, 1) if shift else values
+            if lanes < LANES:
+                moved = jnp.where((lane >= there) & (lane < there + lanes), moved, jnp.bfloat16(0))
+            tiles[tile] = moved if tiles[tile] is None else tiles[tile] + moved
+
+    places = layout()
     for p in range(P_SIZE):
         values = patches[p]
         for step, part in enumerate(norms):
             values = jnp.where(lane == NORM_AT + step, part[p * images : (p + 1) * images], values)
         for step, part in enumerate(alphas):
             values = jnp.where(lane == ALPHA_AT + step, pltpu.roll(part, (ALPHA_AT + step - p) % LANES, 1), values)
-        put(values, p * STRIDE)
+        put(values, places[p])
     probe_hi, probe_low, unused = parts(probes_ref[...])
     rest = jnp.concatenate(
         [count, probe_hi, probe_low, jnp.zeros((images, LANES - 1 - 2 * NPROBE), jnp.float32)], axis=1
     )
-    put(rest.astype(jnp.bfloat16), WIDE)
+    put(rest.astype(jnp.bfloat16), [(TILES - 1, COUNT_AT, 0, LANES - STRIDE)])
     for tile, values in enumerate(tiles):
         out_ref[:, tile * LANES : (tile + 1) * LANES] = values
 
@@ -151,8 +165,14 @@
 def spread(sorted_ref, owner, first_ref, x_ref, options):
     number = sorted_ref.shape[0]
     lane = iota((number, LANES), 1)
-    for p in range(P_SIZE):
-        values = jnp.where(lane < STRIDE, sorted_ref[:, p * STRIDE : p * STRIDE + LANES].astype(jnp.float32), owner)
+    for p, places in enumerate(layout()):
+        values = None
+        for tile, there, here, lanes in places:
+            moved = sorted_ref[:, tile * LANES : (tile + 1) * LANES]
+            if there != here:
+                moved = pltpu.roll(moved, (here - there) % LANES, 1)
+            values = moved if values is None else jnp.where(lane < here, values, moved)
+        values = jnp.where(lane < STRIDE, values.astype(jnp.float32), owner)
         x_ref[pl.ds(first_ref[0, p], number), :] = values
     total = first_ref[0, P_SIZE]
     counts = choose(total, options)
@@ -183,35 +203,30 @@
 
 
 def rank_rows_kernel(*refs):
-    which_ref, owner_ref, first_ref = refs[-3:]
-    tail = jnp.concatenate([part[:, TAIL : TAIL + LANES] for part in refs[:-3]], axis=0)
-    which_ref[...], first_ref[...] = order(tail.astype(jnp.float32))
-    owner_ref[...] = owners(which_ref[...])
+    chosen_ref, first_ref = refs[-2:]
+    tail = jnp.concatenate([part[:, TAIL : TAIL + LANES] for part in refs[:-2]], axis=0)
+    chosen_ref[...], first_ref[...] = order(tail.astype(jnp.float32))
 
 
 def rank_cols_kernel(met_ref, *refs):
-    which_ref, owner_ref, first_ref, probe_ref = refs[-4:]
+    chosen_ref, first_ref, which_ref, tail_ref = refs[-4:]
     met = met_ref[...]
     tail = dot(met, jnp.concatenate([part[:, TAIL : TAIL + LANES] for part in refs[:-4]], axis=0))
-    chosen, first_ref[...] = order(tail)
-    which_ref[...] = dot(chosen, met).astype(jnp.bfloat16)
-    owner_ref[...] = owners(chosen)
-    both = (2 * NPROBE, LANES)
-    pick_probe = (iota(both, 1) == iota(both, 0) + PROBE_AT).astype(jnp.bfloat16)
-    probe_ref[...] = dot(pick_probe, tail.astype(jnp.bfloat16), NT).astype(jnp.bfloat16)
-
-
-def rank(kernel, number, given, extra, flops):
+    tail_ref[...] = tail.astype(jnp.bfloat16)
+    chosen_ref[...], first_ref[...] = order(tail)
+    which_ref[...] = dot(chosen_ref[...], met).astype(jnp.bfloat16)
+
+
+def rank(kernel, given, number, more, flops):
+    shapes = (
+        jax.ShapeDtypeStruct((number, number), jnp.bfloat16),
+        jax.ShapeDtypeStruct((8, LANES), jnp.int32),
+    ) + tuple(jax.ShapeDtypeStruct(shape, jnp.bfloat16) for shape in more)
     return pl.pallas_call(
         kernel,
-        out_shape=(
-            jax.ShapeDtypeStruct((number, sum(a.shape[0] for a in given[-extra:])), jnp.bfloat16),
-            jax.ShapeDtypeStruct((number, LANES), jnp.float32),
-            jax.ShapeDtypeStruct((8, LANES), jnp.int32),
-        )
-        + ((jax.ShapeDtypeStruct((2 * NPROBE, number), jnp.bfloat16),) if extra < len(given) else ()),
+        out_shape=shapes,
         in_specs=[VMEM] * len(given),
-        out_specs=(VMEM,) * (3 if extra == len(given) else 4),
+        out_specs=(VMEM,) * len(shapes),
         compiler_params=pltpu.CompilerParams(vmem_limit_bytes=8 * 2**20),
         cost_estimate=pl.CostEstimate(flops=flops, bytes_accessed=10**6, transcendentals=0),
         name="rank",
@@ -220,24 +235,27 @@
 
 def energies(counted, *refs):
     near_number, far_number = counted
-    row_given, col_given, row_which, row_owner, col_which, col_owner, probe_ref = refs[:7]
-    near_parts = refs[7 : 7 + near_number]
-    far_parts = refs[7 + near_number : 7 + near_number + far_number]
+    row_given, col_given, row_order, col_order, col_which, tail_ref = refs[:6]
+    near_parts = refs[6 : 6 + near_number]
+    far_parts = refs[6 + near_number : 6 + near_number + far_number]
     (out_ref, row_sorted, col_sorted, row_x, col_f, col_x, col_u, product, row_first, col_first, sem) = refs[
-        7 + near_number + far_number :
+        6 + near_number + far_number :
     ]
-    cols = col_owner.shape[0]
+    cols = col_order.shape[0]
     copies = [pltpu.make_async_copy(s, t, sem.at[k]) for k, (s, t) in enumerate(((col_given, col_first), (row_given, row_first)))]
     for copy in copies:
         copy.start()
     product[...] = jnp.zeros_like(product)
     col_sorted[...] = dot(col_which[...], jnp.concatenate([part[...] for part in far_parts], axis=0)).astype(jnp.bfloat16)
-    row_sorted[...] = dot(row_which[...], jnp.concatenate([part[...] for part in near_parts], axis=0)).astype(jnp.bfloat16)
+    row_sorted[...] = dot(row_order[...], jnp.concatenate([part[...] for part in near_parts], axis=0)).astype(jnp.bfloat16)
+    both = (2 * NPROBE, LANES)
+    pick_probe = (iota(both, 1) == iota(both, 0) + PROBE_AT).astype(jnp.bfloat16)
+    probes = dot(pick_probe, tail_ref[...], NT).astype(jnp.bfloat16)
+    col_owner, row_owner = owners(col_order[...]), owners(row_order[...])
     copies[0].wait()
-    col_total, col_counts = spread(col_sorted, col_owner[...], col_first, col_f, COLS)
+    col_total, col_counts = spread(col_sorted, col_owner, col_first, col_f, COLS)
     copies[1].wait()
-    row_total, row_counts = spread(row_sorted, row_owner[...], row_first, row_x, ROWS)
-    probes = probe_ref[...]
+    row_total, row_counts = spread(row_sorted, row_owner, row_first, row_x, ROWS)
 
     line, lane = iota((NPROBE, LANES), 0), iota((NPROBE, LANES), 1)
     pick = (
@@ -284,15 +302,15 @@
 
 
 def local_terms(rows_rank, cols_rank, near, far):
-    row_which, row_owner, row_first = rows_rank
-    col_which, col_owner, col_first, probes = cols_rank
-    rows, cols = row_owner.shape[0], col_owner.shape[0]
+    row_order, row_first = rows_rank
+    col_order, col_first, col_which, col_tail = cols_rank
+    rows, cols = row_order.shape[0], col_order.shape[0]
     row_room = rows * P_SIZE + ROWS[1][0] + FILL
     col_room = (cols * P_SIZE // PREPARED[0][0] + 1) * PREPARED[0][0] + FILL
     return pl.pallas_call(
         functools.partial(energies, (len(near), len(far))),
         out_shape=jax.ShapeDtypeStruct((rows, NPROBE), jnp.float32),
-        in_specs=[VMEM] * (7 + len(near) + len(far)),
+        in_specs=[VMEM] * (6 + len(near) + len(far)),
         out_specs=VMEM,
         scratch_shapes=[
             pltpu.VMEM((rows, PACKED), jnp.bfloat16),
@@ -308,7 +326,7 @@
         ],
         compiler_params=pltpu.CompilerParams(vmem_limit_bytes=40 * 2**20),
         name="energies",
-    )(row_first, col_first, row_which, row_owner, col_which, col_owner, probes, *near, *far)
+    )(row_first, col_first, row_order, col_order, col_which, col_tail, *near, *far)
 
 
 def shards(patches, counts, weights, probes, plan):
@@ -329,8 +347,9 @@
     for apart in range(1, subs):
         low = apart & -apart
         near.append(across(near[apart - low], low))
-    rows_rank = rank(rank_rows_kernel, subs * images, near, subs, 20 * 10**9)
-    cols_rank = rank(rank_cols_kernel, met.shape[0], [met, *far], groups, 2 * 10**9)
+    rows_rank = rank(rank_rows_kernel, near, subs * images, (), 20 * 10**9)
+    cols = met.shape[0]
+    cols_rank = rank(rank_cols_kernel, [met, *far], cols, (met.shape, (cols, LANES)), 2 * 10**9)
     terms = local_terms(rows_rank, cols_rank, near, far)
     total = terms[:images]
     for apart in range(subs - 1, 0, -1):

time: 32.8 us -> 32.4 us (0.988)
  no operation moved by 1% of the time
where the time goes in v5:
time: 32.4 us; the launch traced here: 32.2 us
  starting transfers between devices  14.7 us (45%)
  waiting for transfers between devices  9.06 us (28%)
  Pallas kernels  6.18 us (19%)
  local copies, waits for them, and re-layouts  1.6 us (5%)
  other arithmetic  0.6 us (2%)
    ppermute x6, starting transfers between devices, across(): return lax.ppermute(array, 'narrow', [(i, i ^ apart) for i in range(subs)])  10.8 us
    ppermute x6, waiting for transfers between devices, across(): return lax.ppermute(array, 'narrow', [(i, i ^ apart) for i in range(subs)])  7.36 us
    pallas_call x1, Pallas kernels, local_terms(): pl.pallas_call(functools.partial(energies, (len(near), len(far))), out_sh...  5.12 us
    ppermute x7, starting transfers between devices, swap(): return lax.ppermute(array, 'group', [(i, i ^ apart) for i in range(groups)])  3.9 us
    ppermute x7, waiting for transfers between devices, swap(): return lax.ppermute(array, 'group', [(i, i ^ apart) for i in range(groups)])  1.7 us
    unnamed x10, local copies, waits for them, and re-layouts  1.6 us
  transfers between devices with their start and end apart: 13, of which 8 were waited for; matrix products, arithmetic and copies ran while one was open for 0% of the time, Pallas kernels for 1%

profile of v5, /device:TPU:0, one launch (start us, length us, event | category | flops | bytes accessed | tf_op | source)
XLA Modules:
  0.0 32.2 jit_solution(646344628209312263)
XLA Ops:
  0.0 0.7 %copy-done.1 = f32[16,16]{1,0:T(8,128)S(1)} copy-done((f32[16,16]{1,0:T(8,128)S(1)}, f32[16,16]{1,0:T(8,128)}, u32[]{:S(2)}) %copy-start.1) | copy-done | bytes 1048
  0.7 0.9 %copy-done = bf16[16,3675]{1,0:T(8,128)(2,1)S(1)} copy-done((bf16[16,3675]{1,0:T(8,128)(2,1)S(1)}, bf16[16,3675]{1,0:T(8,128)(2,1)}, u32[]{:S(2)}) %copy-start) | copy-done | bytes 117624
  1.6 0.5 %pack.1 = (bf16[16,3968]{1,0:T(8,128)(2,1)S(1)}, bf16[64,128]{1,0:T(8,128)(2,1)S(1)}) custom-call(s32[1]{0:T(128)} %bitcast.mine_ref, bf16[16,3675]{1,0:T(8,128)(2,1)S(1)} %copy-done, s32[1,16]{1,0:T(1,128)S(1)} %bitcast.3, f32[1,49]{1,0:T(1,128)S(1)} %bitcast.4, f32[16,16]{1,0:T(8,128)S(1)} %copy-done.1, s32[4,8]{1,0:T(4,128)S(1)} %copy-done.2), custom_call_target="tpu_custom_call" | custom-call | tf_op jit(solution)/shard_map/pack/pallas_call | solution.py:130
  2.1 4.1 %collective-permute-start.1 = (bf16[16,3968]{1,0:T(8,128)(2,1)S(1)}, bf16[16,3968]{1,0:T(8,128)(2,1)S(1)}, u32[]{:S(2)}, u32[]{:S(2)}) collective-permute-start(bf16[16,3968]{1,0:T(8,128)(2,1)S(1)} %get-tuple-element.13.refs_0_.refs_6_.refs_10_), channel_id=1, source_target_pairs={{0,2},{1,3},{2,0},{3,1},{4,6},{5,7},{6,4},{7,5},{8,10},{9,11},{10,... | collective-permute-start | bytes 380936 | tf_op jit(solution)/shard_map/ppermute | solution.py:342
  6.2 2.4 %collective-permute-start.5 = (bf16[16,3968]{1,0:T(8,128)(2,1)S(1)}, bf16[16,3968]{1,0:T(8,128)(2,1)S(1)}, u32[]{:S(2)}, u32[]{:S(2)}) collective-permute-start(bf16[16,3968]{1,0:T(8,128)(2,1)S(1)} %get-tuple-element.13.refs_0_.refs_6_.refs_10_), channel_id=1, source_target_pairs={{0,24},{4,28},{8,16},{12,20},{16,8},{20,12},{24,0},{28,4},{1,25},{... | collective-permute-start | bytes 380936 | tf_op jit(solution)/shard_map/ppermute | solution.py:339
  8.7 0.5 %collective-permute-start.4 = (bf16[16,3968]{1,0:T(8,128)(2,1)S(1)}, bf16[16,3968]{1,0:T(8,128)(2,1)S(1)}, u32[]{:S(2)}, u32[]{:S(2)}) collective-permute-start(bf16[16,3968]{1,0:T(8,128)(2,1)S(1)} %get-tuple-element.13.refs_0_.refs_6_.refs_10_), channel_id=1, source_target_pairs={{0,16},{4,20},{8,24},{12,28},{16,0},{20,4},{24,8},{28,12},{1,17},{... | collective-permute-start | bytes 380936 | tf_op jit(solution)/shard_map/ppermute | solution.py:339
  9.2 0.5 %collective-permute-start.3 = (bf16[16,3968]{1,0:T(8,128)(2,1)S(1)}, bf16[16,3968]{1,0:T(8,128)(2,1)S(1)}, u32[]{:S(2)}, u32[]{:S(2)}) collective-permute-start(bf16[16,3968]{1,0:T(8,128)(2,1)S(1)} %get-tuple-element.13.refs_0_.refs_6_.refs_10_), channel_id=1, source_target_pairs={{0,8},{4,12},{8,0},{12,4},{16,24},{20,28},{24,16},{28,20},{1,9},{5... | collective-permute-start | bytes 380936 | tf_op jit(solution)/shard_map/ppermute | solution.py:339
  9.7 1.6 %collective-permute-start = (bf16[16,3968]{1,0:T(8,128)(2,1)S(1)}, bf16[16,3968]{1,0:T(8,128)(2,1)S(1)}, u32[]{:S(2)}, u32[]{:S(2)}) collective-permute-start(bf16[16,3968]{1,0:T(8,128)(2,1)S(1)} %get-tuple-element.13.refs_0_.refs_6_.refs_10_), channel_id=1, source_target_pairs={{0,1},{1,0},{2,3},{3,2},{4,5},{5,4},{6,7},{7,6},{8,9},{9,8},{10,11... | collective-permute-start | bytes 380936 | tf_op jit(solution)/shard_map/ppermute | solution.py:342
  11.3 1.2 %collective-permute-done.1.refs_2_.refs_8_ = bf16[16,3968]{1,0:T(8,128)(2,1)S(1)} collective-permute-done((bf16[16,3968]{1,0:T(8,128)(2,1)S(1)}, bf16[16,3968]{1,0:T(8,128)(2,1)S(1)}, u32[]{:S(2)}, u32[]{:S(2)}) %collective-permute-start.1) | collective-permute-done | bytes 127008 | tf_op jit(solution)/shard_map/ppermute | solution.py:342
  12.5 0.7 %collective-permute-start.2 = (bf16[16,3968]{1,0:T(8,128)(2,1)S(1)}, bf16[16,3968]{1,0:T(8,128)(2,1)S(1)}, u32[]{:S(2)}, u32[]{:S(2)}) collective-permute-start(bf16[16,3968]{1,0:T(8,128)(2,1)S(1)} %collective-permute-done.1.refs_2_.refs_8_), channel_id=1, source_target_pairs={{0,1},{1,0},{2,3},{3,2},{4,5},{5,4},{6,7},{7,6},{8,9},{9,8},{10,11... | collective-permute-start | bytes 380936 | tf_op jit(solution)/shard_map/ppermute | solution.py:342
  13.1 1.6 %collective-permute-done.4.refs_2_.refs_12_ = bf16[16,3968]{1,0:T(8,128)(2,1)S(1)} collective-permute-done((bf16[16,3968]{1,0:T(8,128)(2,1)S(1)}, bf16[16,3968]{1,0:T(8,128)(2,1)S(1)}, u32[]{:S(2)}, u32[]{:S(2)}) %collective-permute-start.4) | collective-permute-done | bytes 127008 | tf_op jit(solution)/shard_map/ppermute | solution.py:339
  14.7 0.1 collective-permute-done.3.refs_1_.refs_11_
  14.8 0.4 %collective-permute-start.8 = (bf16[16,3968]{1,0:T(8,128)(2,1)S(1)}, bf16[16,3968]{1,0:T(8,128)(2,1)S(1)}, u32[]{:S(2)}, u32[]{:S(2)}) collective-permute-start(bf16[16,3968]{1,0:T(8,128)(2,1)S(1)} %collective-permute-done.4.refs_2_.refs_12_), channel_id=1, source_target_pairs={{0,4},{4,0},{8,12},{12,8},{16,20},{20,16},{24,28},{28,24},{1,5},{5... | collective-permute-start | bytes 380936 | tf_op jit(solution)/shard_map/ppermute | solution.py:339
  15.2 0.7 %collective-permute-done.refs_1_.refs_7_ = bf16[16,3968]{1,0:T(8,128)(2,1)S(1)} collective-permute-done((bf16[16,3968]{1,0:T(8,128)(2,1)S(1)}, bf16[16,3968]{1,0:T(8,128)(2,1)S(1)}, u32[]{:S(2)}, u32[]{:S(2)}) %collective-permute-start) | collective-permute-done | bytes 127008 | tf_op jit(solution)/shard_map/ppermute | solution.py:342
  15.9 1.9 %collective-permute-done.2.refs_3_.refs_9_ = bf16[16,3968]{1,0:T(8,128)(2,1)S(1)} collective-permute-done((bf16[16,3968]{1,0:T(8,128)(2,1)S(1)}, bf16[16,3968]{1,0:T(8,128)(2,1)S(1)}, u32[]{:S(2)}, u32[]{:S(2)}) %collective-permute-start.2) | collective-permute-done | bytes 127008 | tf_op jit(solution)/shard_map/ppermute | solution.py:342
  17.8 0.2 rank.2
  18.0 0.4 %rank.3 = (bf16[64,64]{1,0:T(8,128)(2,1)S(1)}, s32[8,128]{1,0:T(8,128)S(1)}, bf16[64,128]{1,0:T(8,128)(2,1)S(1)}, bf16[64,128]{1,0:T(8,128)(2,1)S(1)}) custom-call(bf16[64,128]{1,0:T(8,128)(2,1)S(1)} %get-tuple-element.15.met_ref, bf16[16,3968]{1,0:T(8,128)(2,1)S(1)} %get-tuple-element.13.refs_0_.refs_6_.refs_10_, ...), custom_call_target="tpu_custom_call" | custom-call | flops 2000000000 | bytes 1000000 | tf_op jit(solution)/shard_map/rank/pallas_call | solution.py:225
  18.4 5.1 %energies.1 = f32[64,16]{1,0:T(8,128)S(1)} custom-call(s32[8,128]{1,0:T(8,128)S(1)} %get-tuple-element.14.refs_0_, s32[8,128]{1,0:T(8,128)S(1)} %get-tuple-element.16.refs_1_, bf16[64,64]{1,0:T(8,128)(2,1)S(1)} %get-tuple-element.17.refs_2_, bf16[64,64]{1,0:T(8,128)(2,1)S(1)} %get-tuple-element.18.refs_3_, bf16[64,128]{1,0:T(8,128)(2,1)S(1)} %get-tuple-element.19.refs_4_, ...), custom_call_target="tpu_custom_call" | custom-call | tf_op jit(solution)/shard_map/energies/pallas_call | solution.py:310
  23.5 3.5 %collective-permute-start.10 = (f32[16,16]{1,0:T(8,128)S(1)}, f32[16,16]{1,0:T(8,128)S(1)}, u32[]{:S(2)}, u32[]{:S(2)}) collective-permute-start(f32[16,16]{1,0:T(8,128)S(1)} %get-tuple-element.21), channel_id=1, source_target_pairs={{0,3},{1,2},{2,1},{3,0},{4,7},{5,6},{6,5},{7,4},{8,11},{9,10},{10,... | collective-permute-start | bytes 3080 | tf_op jit(solution)/shard_map/ppermute | solution.py:342
  27.1 0.9 %collective-permute-start.11 = (f32[16,16]{1,0:T(8,128)S(1)}, f32[16,16]{1,0:T(8,128)S(1)}, u32[]{:S(2)}, u32[]{:S(2)}) collective-permute-start(f32[16,16]{1,0:T(8,128)S(1)} %get-tuple-element.23), channel_id=1, source_target_pairs={{0,2},{1,3},{2,0},{3,1},{4,6},{5,7},{6,4},{7,5},{8,10},{9,11},{10,... | collective-permute-start | bytes 3080 | tf_op jit(solution)/shard_map/ppermute | solution.py:342
  28.0 1.1 %collective-permute-done.10 = f32[16,16]{1,0:T(8,128)S(1)} collective-permute-done((f32[16,16]{1,0:T(8,128)S(1)}, f32[16,16]{1,0:T(8,128)S(1)}, u32[]{:S(2)}, u32[]{:S(2)}) %collective-permute-start.10) | collective-permute-done | bytes 1056 | tf_op jit(solution)/shard_map/ppermute | solution.py:342
  29.0 1.7 %collective-permute-done.12 = f32[16,16]{1,0:T(8,128)S(1)} collective-permute-done((f32[16,16]{1,0:T(8,128)S(1)}, f32[16,16]{1,0:T(8,128)S(1)}, u32[]{:S(2)}, u32[]{:S(2)}) %collective-permute-start.12) | collective-permute-done | bytes 1056 | tf_op jit(solution)/shard_map/ppermute | solution.py:342
  30.7 0.9 %collective-permute-done.11 = f32[16,16]{1,0:T(8,128)S(1)} collective-permute-done((f32[16,16]{1,0:T(8,128)S(1)}, f32[16,16]{1,0:T(8,128)S(1)}, u32[]{:S(2)}, u32[]{:S(2)}) %collective-permute-start.11) | collective-permute-done | bytes 1056 | tf_op jit(solution)/shard_map/ppermute | solution.py:342
  31.6 0.6 %fusion.1 = f32[16,16]{1,0:T(8,128)} fusion(f32[16,16]{1,0:T(8,128)S(1)} %collective-permute-done.12, f32[16,16]{1,0:T(8,128)S(1)} %collective-permute-done.11, f32[16,16]{1,0:T(8,128)S(1)} %collective-permute-done.10, f32[64,16]{1,0:T(8,128)S(1)} %energies.1), kind=kLoop, calls=%fused_computation.2 | loop fusion | flops 768 | bytes 5120 | tf_op jit(solution)/shard_map/add | solution.py:356
  (18 shorter events, 0.0 us)
Async XLA Ops:
  0.0 0.7 %copy-start.1 = (f32[16,16]{1,0:T(8,128)S(1)}, f32[16,16]{1,0:T(8,128)}, u32[]{:S(2)}) copy-start(f32[16,16]{1,0:T(8,128)} %refs_3_.1) | copy-start | bytes 3076
  0.0 0.7 %copy-start.2 = (s32[4,8]{1,0:T(4,128)S(1)}, s32[4,8]{1,0:T(4,128)}, u32[]{:S(2)}) copy-start(s32[4,8]{1,0:T(4,128)} %refs_4_.1) | copy-start | bytes 388
  0.0 0.7 %copy-start.3 = (s32[16]{0:T(128)S(1)}, s32[16]{0:T(128)}, u32[]{:S(2)}) copy-start(s32[16]{0:T(128)} %param.6) | copy-start | bytes 196
  0.0 0.7 %copy-start.4 = (f32[49]{0:T(128)S(1)}, f32[49]{0:T(128)}, u32[]{:S(2)}) copy-start(f32[49]{0:T(128)} %param.7) | copy-start | bytes 592
  0.7 0.9 %copy-start = (bf16[16,3675]{1,0:T(8,128)(2,1)S(1)}, bf16[16,3675]{1,0:T(8,128)(2,1)}, u32[]{:S(2)}) copy-start(bf16[16,3675]{1,0:T(8,128)(2,1)} %refs_0_.1) | copy-start | bytes 352804
  2.1 10.3 %collective-permute-start.1 = (bf16[16,3968]{1,0:T(8,128)(2,1)S(1)}, bf16[16,3968]{1,0:T(8,128)(2,1)S(1)}, u32[]{:S(2)}, u32[]{:S(2)}) collective-permute-start(bf16[16,3968]{1,0:T(8,128)(2,1)S(1)} %get-tuple-element.13.refs_0_.refs_6_.refs_10_), channel_id=1, source_target_pairs={{0,2},{1,3},{2,0},{3,1},{4,6},{5,7},{6,4},{7,5},{8,10},{9,11},{10,... | collective-permute-start | bytes 380936 | tf_op jit(solution)/shard_map/ppermute | solution.py:342
  6.2 6.9 %collective-permute-start.5 = (bf16[16,3968]{1,0:T(8,128)(2,1)S(1)}, bf16[16,3968]{1,0:T(8,128)(2,1)S(1)}, u32[]{:S(2)}, u32[]{:S(2)}) collective-permute-start(bf16[16,3968]{1,0:T(8,128)(2,1)S(1)} %get-tuple-element.13.refs_0_.refs_6_.refs_10_), channel_id=1, source_target_pairs={{0,24},{4,28},{8,16},{12,20},{16,8},{20,12},{24,0},{28,4},{1,25},{... | collective-permute-start | bytes 380936 | tf_op jit(solution)/shard_map/ppermute | solution.py:339
  8.7 6.0 %collective-permute-start.4 = (bf16[16,3968]{1,0:T(8,128)(2,1)S(1)}, bf16[16,3968]{1,0:T(8,128)(2,1)S(1)}, u32[]{:S(2)}, u32[]{:S(2)}) collective-permute-start(bf16[16,3968]{1,0:T(8,128)(2,1)S(1)} %get-tuple-element.13.refs_0_.refs_6_.refs_10_), channel_id=1, source_target_pairs={{0,16},{4,20},{8,24},{12,28},{16,0},{20,4},{24,8},{28,12},{1,17},{... | collective-permute-start | bytes 380936 | tf_op jit(solution)/shard_map/ppermute | solution.py:339
  9.2 5.6 %collective-permute-start.3 = (bf16[16,3968]{1,0:T(8,128)(2,1)S(1)}, bf16[16,3968]{1,0:T(8,128)(2,1)S(1)}, u32[]{:S(2)}, u32[]{:S(2)}) collective-permute-start(bf16[16,3968]{1,0:T(8,128)(2,1)S(1)} %get-tuple-element.13.refs_0_.refs_6_.refs_10_), channel_id=1, source_target_pairs={{0,8},{4,12},{8,0},{12,4},{16,24},{20,28},{24,16},{28,20},{1,9},{5... | collective-permute-start | bytes 380936 | tf_op jit(solution)/shard_map/ppermute | solution.py:339
  9.7 6.2 %collective-permute-start = (bf16[16,3968]{1,0:T(8,128)(2,1)S(1)}, bf16[16,3968]{1,0:T(8,128)(2,1)S(1)}, u32[]{:S(2)}, u32[]{:S(2)}) collective-permute-start(bf16[16,3968]{1,0:T(8,128)(2,1)S(1)} %get-tuple-element.13.refs_0_.refs_6_.refs_10_), channel_id=1, source_target_pairs={{0,1},{1,0},{2,3},{3,2},{4,5},{5,4},{6,7},{7,6},{8,9},{9,8},{10,11... | collective-permute-start | bytes 380936 | tf_op jit(solution)/shard_map/ppermute | solution.py:342
  12.5 5.3 %collective-permute-start.2 = (bf16[16,3968]{1,0:T(8,128)(2,1)S(1)}, bf16[16,3968]{1,0:T(8,128)(2,1)S(1)}, u32[]{:S(2)}, u32[]{:S(2)}) collective-permute-start(bf16[16,3968]{1,0:T(8,128)(2,1)S(1)} %collective-permute-done.1.refs_2_.refs_8_), channel_id=1, source_target_pairs={{0,1},{1,0},{2,3},{3,2},{4,5},{5,4},{6,7},{7,6},{8,9},{9,8},{10,11... | collective-permute-start | bytes 380936 | tf_op jit(solution)/shard_map/ppermute | solution.py:342
  13.1 4.9 %collective-permute-start.6 = (bf16[16,3968]{1,0:T(8,128)(2,1)S(1)}, bf16[16,3968]{1,0:T(8,128)(2,1)S(1)}, u32[]{:S(2)}, u32[]{:S(2)}) collective-permute-start(bf16[16,3968]{1,0:T(8,128)(2,1)S(1)} %get-tuple-element.13.refs_0_.refs_6_.refs_10_), channel_id=1, source_target_pairs={{0,4},{4,0},{8,12},{12,8},{16,20},{20,16},{24,28},{28,24},{1,5},{5... | collective-permute-start | bytes 380936 | tf_op jit(solution)/shard_map/ppermute | solution.py:339
  14.7 3.3 %collective-permute-start.9 = (bf16[16,3968]{1,0:T(8,128)(2,1)S(1)}, bf16[16,3968]{1,0:T(8,128)(2,1)S(1)}, u32[]{:S(2)}, u32[]{:S(2)}) collective-permute-start(bf16[16,3968]{1,0:T(8,128)(2,1)S(1)} %collective-permute-done.5.refs_3_.refs_13_), channel_id=1, source_target_pairs={{0,4},{4,0},{8,12},{12,8},{16,20},{20,16},{24,28},{28,24},{1,5},{5... | collective-permute-start | bytes 380936 | tf_op jit(solution)/shard_map/ppermute | solution.py:339
  14.8 3.2 %collective-permute-start.8 = (bf16[16,3968]{1,0:T(8,128)(2,1)S(1)}, bf16[16,3968]{1,0:T(8,128)(2,1)S(1)}, u32[]{:S(2)}, u32[]{:S(2)}) collective-permute-start(bf16[16,3968]{1,0:T(8,128)(2,1)S(1)} %collective-permute-done.4.refs_2_.refs_12_), channel_id=1, source_target_pairs={{0,4},{4,0},{8,12},{12,8},{16,20},{20,16},{24,28},{28,24},{1,5},{5... | collective-permute-start | bytes 380936 | tf_op jit(solution)/shard_map/ppermute | solution.py:339
  15.9 2.1 %collective-permute-start.7 = (bf16[16,3968]{1,0:T(8,128)(2,1)S(1)}, bf16[16,3968]{1,0:T(8,128)(2,1)S(1)}, u32[]{:S(2)}, u32[]{:S(2)}) collective-permute-start(bf16[16,3968]{1,0:T(8,128)(2,1)S(1)} %collective-permute-done.3.refs_1_.refs_11_), channel_id=1, source_target_pairs={{0,4},{4,0},{8,12},{12,8},{16,20},{20,16},{24,28},{28,24},{1,5},{5... | collective-permute-start | bytes 380936 | tf_op jit(solution)/shard_map/ppermute | solution.py:339
  23.5 5.5 %collective-permute-start.10 = (f32[16,16]{1,0:T(8,128)S(1)}, f32[16,16]{1,0:T(8,128)S(1)}, u32[]{:S(2)}, u32[]{:S(2)}) collective-permute-start(f32[16,16]{1,0:T(8,128)S(1)} %get-tuple-element.21), channel_id=1, source_target_pairs={{0,3},{1,2},{2,1},{3,0},{4,7},{5,6},{6,5},{7,4},{8,11},{9,10},{10,... | collective-permute-start | bytes 3080 | tf_op jit(solution)/shard_map/ppermute | solution.py:342
  27.0 3.7 %collective-permute-start.12 = (f32[16,16]{1,0:T(8,128)S(1)}, f32[16,16]{1,0:T(8,128)S(1)}, u32[]{:S(2)}, u32[]{:S(2)}) collective-permute-start(f32[16,16]{1,0:T(8,128)S(1)} %get-tuple-element.22), channel_id=1, source_target_pairs={{0,1},{1,0},{2,3},{3,2},{4,5},{5,4},{6,7},{7,6},{8,9},{9,8},{10,11... | collective-permute-start | bytes 3080 | tf_op jit(solution)/shard_map/ppermute | solution.py:342
  27.1 4.5 %collective-permute-start.11 = (f32[16,16]{1,0:T(8,128)S(1)}, f32[16,16]{1,0:T(8,128)S(1)}, u32[]{:S(2)}, u32[]{:S(2)}) collective-permute-start(f32[16,16]{1,0:T(8,128)S(1)} %get-tuple-element.23), channel_id=1, source_target_pairs={{0,2},{1,3},{2,0},{3,1},{4,6},{5,7},{6,4},{7,5},{8,10},{9,11},{10,... | collective-permute-start | bytes 3080 | tf_op jit(solution)/shard_map/ppermute | solution.py:342

commit v6 on v5

--- a/solution.py
+++ b/solution.py
@@ -35,7 +35,7 @@
 
 
 OWNER_AT = STRIDE
-ROWS = ((1792, 1), (2048, 1), (1024, None))
+ROWS = ((1664, 1), (1792, 1), (2048, 1), (1024, None))
 COLS = ((896, 2), (1024, None))
 PREPARED = ((2048, None),)
 FILL = 256
@@ -305,7 +305,7 @@
     row_order, row_first = rows_rank
     col_order, col_first, col_which, col_tail = cols_rank
     rows, cols = row_order.shape[0], col_order.shape[0]
-    row_room = rows * P_SIZE + ROWS[1][0] + FILL
+    row_room = rows * P_SIZE + ROWS[2][0] + FILL
     col_room = (cols * P_SIZE // PREPARED[0][0] + 1) * PREPARED[0][0] + FILL
     return pl.pallas_call(
         functools.partial(energies, (len(near), len(far))),

time: 32.4 us -> 32.3 us (level)
  no operation moved by 1% of the time
where the time goes in v6:
time: 32.3 us; the launch traced here: 32.1 us
  starting transfers between devices  14.7 us (46%)
  waiting for transfers between devices  9.09 us (28%)
  Pallas kernels  6.02 us (19%)
  local copies, waits for them, and re-layouts  1.6 us (5%)
  other arithmetic  0.6 us (2%)
    ppermute x6, starting transfers between devices, across(): return lax.ppermute(array, 'narrow', [(i, i ^ apart) for i in range(subs)])  10.8 us
    ppermute x6, waiting for transfers between devices, across(): return lax.ppermute(array, 'narrow', [(i, i ^ apart) for i in range(subs)])  7.39 us
    pallas_call x1, Pallas kernels, local_terms(): pl.pallas_call(functools.partial(energies, (len(near), len(far))), out_sh...  4.96 us
    ppermute x7, starting transfers between devices, swap(): return lax.ppermute(array, 'group', [(i, i ^ apart) for i in range(groups)])  3.9 us
    ppermute x7, waiting for transfers between devices, swap(): return lax.ppermute(array, 'group', [(i, i ^ apart) for i in range(groups)])  1.7 us
    unnamed x10, local copies, waits for them, and re-layouts  1.6 us
  transfers between devices with their start and end apart: 13, of which 8 were waited for; matrix products, arithmetic and copies ran while one was open for 0% of the time, Pallas kernels for 1%

profile of v6, /device:TPU:0, one launch (start us, length us, event | category | flops | bytes accessed | tf_op | source)
XLA Modules:
  0.0 32.1 jit_solution(4469874430565633927)
XLA Ops:
  0.0 0.7 %copy-done.1 = f32[16,16]{1,0:T(8,128)S(1)} copy-done((f32[16,16]{1,0:T(8,128)S(1)}, f32[16,16]{1,0:T(8,128)}, u32[]{:S(2)}) %copy-start.1) | copy-done | bytes 1048
  0.7 0.9 %copy-done = bf16[16,3675]{1,0:T(8,128)(2,1)S(1)} copy-done((bf16[16,3675]{1,0:T(8,128)(2,1)S(1)}, bf16[16,3675]{1,0:T(8,128)(2,1)}, u32[]{:S(2)}) %copy-start) | copy-done | bytes 117624
  1.6 0.5 %pack.1 = (bf16[16,3968]{1,0:T(8,128)(2,1)S(1)}, bf16[64,128]{1,0:T(8,128)(2,1)S(1)}) custom-call(s32[1]{0:T(128)} %bitcast.mine_ref, bf16[16,3675]{1,0:T(8,128)(2,1)S(1)} %copy-done, s32[1,16]{1,0:T(1,128)S(1)} %bitcast.3, f32[1,49]{1,0:T(1,128)S(1)} %bitcast.4, f32[16,16]{1,0:T(8,128)S(1)} %copy-done.1, s32[4,8]{1,0:T(4,128)S(1)} %copy-done.2), custom_call_target="tpu_custom_call" | custom-call | tf_op jit(solution)/shard_map/pack/pallas_call | solution.py:130
  2.1 4.1 %collective-permute-start.1 = (bf16[16,3968]{1,0:T(8,128)(2,1)S(1)}, bf16[16,3968]{1,0:T(8,128)(2,1)S(1)}, u32[]{:S(2)}, u32[]{:S(2)}) collective-permute-start(bf16[16,3968]{1,0:T(8,128)(2,1)S(1)} %get-tuple-element.13.refs_0_.refs_6_.refs_10_), channel_id=1, source_target_pairs={{0,2},{1,3},{2,0},{3,1},{4,6},{5,7},{6,4},{7,5},{8,10},{9,11},{10,... | collective-permute-start | bytes 380936 | tf_op jit(solution)/shard_map/ppermute | solution.py:342
  6.2 2.4 %collective-permute-start.5 = (bf16[16,3968]{1,0:T(8,128)(2,1)S(1)}, bf16[16,3968]{1,0:T(8,128)(2,1)S(1)}, u32[]{:S(2)}, u32[]{:S(2)}) collective-permute-start(bf16[16,3968]{1,0:T(8,128)(2,1)S(1)} %get-tuple-element.13.refs_0_.refs_6_.refs_10_), channel_id=1, source_target_pairs={{0,24},{4,28},{8,16},{12,20},{16,8},{20,12},{24,0},{28,4},{1,25},{... | collective-permute-start | bytes 380936 | tf_op jit(solution)/shard_map/ppermute | solution.py:339
  8.7 0.5 %collective-permute-start.4 = (bf16[16,3968]{1,0:T(8,128)(2,1)S(1)}, bf16[16,3968]{1,0:T(8,128)(2,1)S(1)}, u32[]{:S(2)}, u32[]{:S(2)}) collective-permute-start(bf16[16,3968]{1,0:T(8,128)(2,1)S(1)} %get-tuple-element.13.refs_0_.refs_6_.refs_10_), channel_id=1, source_target_pairs={{0,16},{4,20},{8,24},{12,28},{16,0},{20,4},{24,8},{28,12},{1,17},{... | collective-permute-start | bytes 380936 | tf_op jit(solution)/shard_map/ppermute | solution.py:339
  9.2 0.5 %collective-permute-start.3 = (bf16[16,3968]{1,0:T(8,128)(2,1)S(1)}, bf16[16,3968]{1,0:T(8,128)(2,1)S(1)}, u32[]{:S(2)}, u32[]{:S(2)}) collective-permute-start(bf16[16,3968]{1,0:T(8,128)(2,1)S(1)} %get-tuple-element.13.refs_0_.refs_6_.refs_10_), channel_id=1, source_target_pairs={{0,8},{4,12},{8,0},{12,4},{16,24},{20,28},{24,16},{28,20},{1,9},{5... | collective-permute-start | bytes 380936 | tf_op jit(solution)/shard_map/ppermute | solution.py:339
  9.7 1.6 %collective-permute-start = (bf16[16,3968]{1,0:T(8,128)(2,1)S(1)}, bf16[16,3968]{1,0:T(8,128)(2,1)S(1)}, u32[]{:S(2)}, u32[]{:S(2)}) collective-permute-start(bf16[16,3968]{1,0:T(8,128)(2,1)S(1)} %get-tuple-element.13.refs_0_.refs_6_.refs_10_), channel_id=1, source_target_pairs={{0,1},{1,0},{2,3},{3,2},{4,5},{5,4},{6,7},{7,6},{8,9},{9,8},{10,11... | collective-permute-start | bytes 380936 | tf_op jit(solution)/shard_map/ppermute | solution.py:342
  11.3 1.2 %collective-permute-done.1.refs_2_.refs_8_ = bf16[16,3968]{1,0:T(8,128)(2,1)S(1)} collective-permute-done((bf16[16,3968]{1,0:T(8,128)(2,1)S(1)}, bf16[16,3968]{1,0:T(8,128)(2,1)S(1)}, u32[]{:S(2)}, u32[]{:S(2)}) %collective-permute-start.1) | collective-permute-done | bytes 127008 | tf_op jit(solution)/shard_map/ppermute | solution.py:342
  12.5 0.7 %collective-permute-start.2 = (bf16[16,3968]{1,0:T(8,128)(2,1)S(1)}, bf16[16,3968]{1,0:T(8,128)(2,1)S(1)}, u32[]{:S(2)}, u32[]{:S(2)}) collective-permute-start(bf16[16,3968]{1,0:T(8,128)(2,1)S(1)} %collective-permute-done.1.refs_2_.refs_8_), channel_id=1, source_target_pairs={{0,1},{1,0},{2,3},{3,2},{4,5},{5,4},{6,7},{7,6},{8,9},{9,8},{10,11... | collective-permute-start | bytes 380936 | tf_op jit(solution)/shard_map/ppermute | solution.py:342
  13.1 1.6 %collective-permute-done.4.refs_2_.refs_12_ = bf16[16,3968]{1,0:T(8,128)(2,1)S(1)} collective-permute-done((bf16[16,3968]{1,0:T(8,128)(2,1)S(1)}, bf16[16,3968]{1,0:T(8,128)(2,1)S(1)}, u32[]{:S(2)}, u32[]{:S(2)}) %collective-permute-start.4) | collective-permute-done | bytes 127008 | tf_op jit(solution)/shard_map/ppermute | solution.py:339
  14.7 0.1 collective-permute-done.3.refs_1_.refs_11_
  14.8 0.4 %collective-permute-start.8 = (bf16[16,3968]{1,0:T(8,128)(2,1)S(1)}, bf16[16,3968]{1,0:T(8,128)(2,1)S(1)}, u32[]{:S(2)}, u32[]{:S(2)}) collective-permute-start(bf16[16,3968]{1,0:T(8,128)(2,1)S(1)} %collective-permute-done.4.refs_2_.refs_12_), channel_id=1, source_target_pairs={{0,4},{4,0},{8,12},{12,8},{16,20},{20,16},{24,28},{28,24},{1,5},{5... | collective-permute-start | bytes 380936 | tf_op jit(solution)/shard_map/ppermute | solution.py:339
  15.2 0.7 %collective-permute-done.refs_1_.refs_7_ = bf16[16,3968]{1,0:T(8,128)(2,1)S(1)} collective-permute-done((bf16[16,3968]{1,0:T(8,128)(2,1)S(1)}, bf16[16,3968]{1,0:T(8,128)(2,1)S(1)}, u32[]{:S(2)}, u32[]{:S(2)}) %collective-permute-start) | collective-permute-done | bytes 127008 | tf_op jit(solution)/shard_map/ppermute | solution.py:342
  15.9 1.9 %collective-permute-done.2.refs_3_.refs_9_ = bf16[16,3968]{1,0:T(8,128)(2,1)S(1)} collective-permute-done((bf16[16,3968]{1,0:T(8,128)(2,1)S(1)}, bf16[16,3968]{1,0:T(8,128)(2,1)S(1)}, u32[]{:S(2)}, u32[]{:S(2)}) %collective-permute-start.2) | collective-permute-done | bytes 127008 | tf_op jit(solution)/shard_map/ppermute | solution.py:342
  17.8 0.2 rank.2
  18.0 0.4 %rank.3 = (bf16[64,64]{1,0:T(8,128)(2,1)S(1)}, s32[8,128]{1,0:T(8,128)S(1)}, bf16[64,128]{1,0:T(8,128)(2,1)S(1)}, bf16[64,128]{1,0:T(8,128)(2,1)S(1)}) custom-call(bf16[64,128]{1,0:T(8,128)(2,1)S(1)} %get-tuple-element.15.met_ref, bf16[16,3968]{1,0:T(8,128)(2,1)S(1)} %get-tuple-element.13.refs_0_.refs_6_.refs_10_, ...), custom_call_target="tpu_custom_call" | custom-call | flops 2000000000 | bytes 1000000 | tf_op jit(solution)/shard_map/rank/pallas_call | solution.py:225
  18.4 5.0 %energies.1 = f32[64,16]{1,0:T(8,128)S(1)} custom-call(s32[8,128]{1,0:T(8,128)S(1)} %get-tuple-element.14.refs_0_, s32[8,128]{1,0:T(8,128)S(1)} %get-tuple-element.16.refs_1_, bf16[64,64]{1,0:T(8,128)(2,1)S(1)} %get-tuple-element.17.refs_2_, bf16[64,64]{1,0:T(8,128)(2,1)S(1)} %get-tuple-element.18.refs_3_, bf16[64,128]{1,0:T(8,128)(2,1)S(1)} %get-tuple-element.19.refs_4_, ...), custom_call_target="tpu_custom_call" | custom-call | tf_op jit(solution)/shard_map/energies/pallas_call | solution.py:310
  23.4 3.6 %collective-permute-start.10 = (f32[16,16]{1,0:T(8,128)S(1)}, f32[16,16]{1,0:T(8,128)S(1)}, u32[]{:S(2)}, u32[]{:S(2)}) collective-permute-start(f32[16,16]{1,0:T(8,128)S(1)} %get-tuple-element.21), channel_id=1, source_target_pairs={{0,3},{1,2},{2,1},{3,0},{4,7},{5,6},{6,5},{7,4},{8,11},{9,10},{10,... | collective-permute-start | bytes 3080 | tf_op jit(solution)/shard_map/ppermute | solution.py:342
  26.9 0.9 %collective-permute-start.11 = (f32[16,16]{1,0:T(8,128)S(1)}, f32[16,16]{1,0:T(8,128)S(1)}, u32[]{:S(2)}, u32[]{:S(2)}) collective-permute-start(f32[16,16]{1,0:T(8,128)S(1)} %get-tuple-element.23), channel_id=1, source_target_pairs={{0,2},{1,3},{2,0},{3,1},{4,6},{5,7},{6,4},{7,5},{8,10},{9,11},{10,... | collective-permute-start | bytes 3080 | tf_op jit(solution)/shard_map/ppermute | solution.py:342
  27.8 1.1 %collective-permute-done.10 = f32[16,16]{1,0:T(8,128)S(1)} collective-permute-done((f32[16,16]{1,0:T(8,128)S(1)}, f32[16,16]{1,0:T(8,128)S(1)}, u32[]{:S(2)}, u32[]{:S(2)}) %collective-permute-start.10) | collective-permute-done | bytes 1056 | tf_op jit(solution)/shard_map/ppermute | solution.py:342
  28.9 1.7 %collective-permute-done.12 = f32[16,16]{1,0:T(8,128)S(1)} collective-permute-done((f32[16,16]{1,0:T(8,128)S(1)}, f32[16,16]{1,0:T(8,128)S(1)}, u32[]{:S(2)}, u32[]{:S(2)}) %collective-permute-start.12) | collective-permute-done | bytes 1056 | tf_op jit(solution)/shard_map/ppermute | solution.py:342
  30.6 0.9 %collective-permute-done.11 = f32[16,16]{1,0:T(8,128)S(1)} collective-permute-done((f32[16,16]{1,0:T(8,128)S(1)}, f32[16,16]{1,0:T(8,128)S(1)}, u32[]{:S(2)}, u32[]{:S(2)}) %collective-permute-start.11) | collective-permute-done | bytes 1056 | tf_op jit(solution)/shard_map/ppermute | solution.py:342
  31.5 0.6 %fusion.1 = f32[16,16]{1,0:T(8,128)} fusion(f32[16,16]{1,0:T(8,128)S(1)} %collective-permute-done.12, f32[16,16]{1,0:T(8,128)S(1)} %collective-permute-done.11, f32[16,16]{1,0:T(8,128)S(1)} %collective-permute-done.10, f32[64,16]{1,0:T(8,128)S(1)} %energies.1), kind=kLoop, calls=%fused_computation.2 | loop fusion | flops 768 | bytes 5120 | tf_op jit(solution)/shard_map/add | solution.py:356
  (18 shorter events, 0.0 us)
Async XLA Ops:
  0.0 0.7 %copy-start.1 = (f32[16,16]{1,0:T(8,128)S(1)}, f32[16,16]{1,0:T(8,128)}, u32[]{:S(2)}) copy-start(f32[16,16]{1,0:T(8,128)} %refs_3_.1) | copy-start | bytes 3076
  0.0 0.7 %copy-start.2 = (s32[4,8]{1,0:T(4,128)S(1)}, s32[4,8]{1,0:T(4,128)}, u32[]{:S(2)}) copy-start(s32[4,8]{1,0:T(4,128)} %refs_4_.1) | copy-start | bytes 388
  0.0 0.7 %copy-start.3 = (s32[16]{0:T(128)S(1)}, s32[16]{0:T(128)}, u32[]{:S(2)}) copy-start(s32[16]{0:T(128)} %param.6) | copy-start | bytes 196
  0.0 0.7 %copy-start.4 = (f32[49]{0:T(128)S(1)}, f32[49]{0:T(128)}, u32[]{:S(2)}) copy-start(f32[49]{0:T(128)} %param.7) | copy-start | bytes 592
  0.7 0.9 %copy-start = (bf16[16,3675]{1,0:T(8,128)(2,1)S(1)}, bf16[16,3675]{1,0:T(8,128)(2,1)}, u32[]{:S(2)}) copy-start(bf16[16,3675]{1,0:T(8,128)(2,1)} %refs_0_.1) | copy-start | bytes 352804
  2.1 10.3 %collective-permute-start.1 = (bf16[16,3968]{1,0:T(8,128)(2,1)S(1)}, bf16[16,3968]{1,0:T(8,128)(2,1)S(1)}, u32[]{:S(2)}, u32[]{:S(2)}) collective-permute-start(bf16[16,3968]{1,0:T(8,128)(2,1)S(1)} %get-tuple-element.13.refs_0_.refs_6_.refs_10_), channel_id=1, source_target_pairs={{0,2},{1,3},{2,0},{3,1},{4,6},{5,7},{6,4},{7,5},{8,10},{9,11},{10,... | collective-permute-start | bytes 380936 | tf_op jit(solution)/shard_map/ppermute | solution.py:342
  6.2 6.9 %collective-permute-start.5 = (bf16[16,3968]{1,0:T(8,128)(2,1)S(1)}, bf16[16,3968]{1,0:T(8,128)(2,1)S(1)}, u32[]{:S(2)}, u32[]{:S(2)}) collective-permute-start(bf16[16,3968]{1,0:T(8,128)(2,1)S(1)} %get-tuple-element.13.refs_0_.refs_6_.refs_10_), channel_id=1, source_target_pairs={{0,24},{4,28},{8,16},{12,20},{16,8},{20,12},{24,0},{28,4},{1,25},{... | collective-permute-start | bytes 380936 | tf_op jit(solution)/shard_map/ppermute | solution.py:339
  8.7 6.0 %collective-permute-start.4 = (bf16[16,3968]{1,0:T(8,128)(2,1)S(1)}, bf16[16,3968]{1,0:T(8,128)(2,1)S(1)}, u32[]{:S(2)}, u32[]{:S(2)}) collective-permute-start(bf16[16,3968]{1,0:T(8,128)(2,1)S(1)} %get-tuple-element.13.refs_0_.refs_6_.refs_10_), channel_id=1, source_target_pairs={{0,16},{4,20},{8,24},{12,28},{16,0},{20,4},{24,8},{28,12},{1,17},{... | collective-permute-start | bytes 380936 | tf_op jit(solution)/shard_map/ppermute | solution.py:339
  9.2 5.6 %collective-permute-start.3 = (bf16[16,3968]{1,0:T(8,128)(2,1)S(1)}, bf16[16,3968]{1,0:T(8,128)(2,1)S(1)}, u32[]{:S(2)}, u32[]{:S(2)}) collective-permute-start(bf16[16,3968]{1,0:T(8,128)(2,1)S(1)} %get-tuple-element.13.refs_0_.refs_6_.refs_10_), channel_id=1, source_target_pairs={{0,8},{4,12},{8,0},{12,4},{16,24},{20,28},{24,16},{28,20},{1,9},{5... | collective-permute-start | bytes 380936 | tf_op jit(solution)/shard_map/ppermute | solution.py:339
  9.7 6.2 %collective-permute-start = (bf16[16,3968]{1,0:T(8,128)(2,1)S(1)}, bf16[16,3968]{1,0:T(8,128)(2,1)S(1)}, u32[]{:S(2)}, u32[]{:S(2)}) collective-permute-start(bf16[16,3968]{1,0:T(8,128)(2,1)S(1)} %get-tuple-element.13.refs_0_.refs_6_.refs_10_), channel_id=1, source_target_pairs={{0,1},{1,0},{2,3},{3,2},{4,5},{5,4},{6,7},{7,6},{8,9},{9,8},{10,11... | collective-permute-start | bytes 380936 | tf_op jit(solution)/shard_map/ppermute | solution.py:342
  12.5 5.3 %collective-permute-start.2 = (bf16[16,3968]{1,0:T(8,128)(2,1)S(1)}, bf16[16,3968]{1,0:T(8,128)(2,1)S(1)}, u32[]{:S(2)}, u32[]{:S(2)}) collective-permute-start(bf16[16,3968]{1,0:T(8,128)(2,1)S(1)} %collective-permute-done.1.refs_2_.refs_8_), channel_id=1, source_target_pairs={{0,1},{1,0},{2,3},{3,2},{4,5},{5,4},{6,7},{7,6},{8,9},{9,8},{10,11... | collective-permute-start | bytes 380936 | tf_op jit(solution)/shard_map/ppermute | solution.py:342
  13.1 4.9 %collective-permute-start.6 = (bf16[16,3968]{1,0:T(8,128)(2,1)S(1)}, bf16[16,3968]{1,0:T(8,128)(2,1)S(1)}, u32[]{:S(2)}, u32[]{:S(2)}) collective-permute-start(bf16[16,3968]{1,0:T(8,128)(2,1)S(1)} %get-tuple-element.13.refs_0_.refs_6_.refs_10_), channel_id=1, source_target_pairs={{0,4},{4,0},{8,12},{12,8},{16,20},{20,16},{24,28},{28,24},{1,5},{5... | collective-permute-start | bytes 380936 | tf_op jit(solution)/shard_map/ppermute | solution.py:339
  14.7 3.3 %collective-permute-start.9 = (bf16[16,3968]{1,0:T(8,128)(2,1)S(1)}, bf16[16,3968]{1,0:T(8,128)(2,1)S(1)}, u32[]{:S(2)}, u32[]{:S(2)}) collective-permute-start(bf16[16,3968]{1,0:T(8,128)(2,1)S(1)} %collective-permute-done.5.refs_3_.refs_13_), channel_id=1, source_target_pairs={{0,4},{4,0},{8,12},{12,8},{16,20},{20,16},{24,28},{28,24},{1,5},{5... | collective-permute-start | bytes 380936 | tf_op jit(solution)/shard_map/ppermute | solution.py:339
  14.8 3.2 %collective-permute-start.8 = (bf16[16,3968]{1,0:T(8,128)(2,1)S(1)}, bf16[16,3968]{1,0:T(8,128)(2,1)S(1)}, u32[]{:S(2)}, u32[]{:S(2)}) collective-permute-start(bf16[16,3968]{1,0:T(8,128)(2,1)S(1)} %collective-permute-done.4.refs_2_.refs_12_), channel_id=1, source_target_pairs={{0,4},{4,0},{8,12},{12,8},{16,20},{20,16},{24,28},{28,24},{1,5},{5... | collective-permute-start | bytes 380936 | tf_op jit(solution)/shard_map/ppermute | solution.py:339
  15.9 2.1 %collective-permute-start.7 = (bf16[16,3968]{1,0:T(8,128)(2,1)S(1)}, bf16[16,3968]{1,0:T(8,128)(2,1)S(1)}, u32[]{:S(2)}, u32[]{:S(2)}) collective-permute-start(bf16[16,3968]{1,0:T(8,128)(2,1)S(1)} %collective-permute-done.3.refs_1_.refs_11_), channel_id=1, source_target_pairs={{0,4},{4,0},{8,12},{12,8},{16,20},{20,16},{24,28},{28,24},{1,5},{5... | collective-permute-start | bytes 380936 | tf_op jit(solution)/shard_map/ppermute | solution.py:339
  23.4 5.5 %collective-permute-start.10 = (f32[16,16]{1,0:T(8,128)S(1)}, f32[16,16]{1,0:T(8,128)S(1)}, u32[]{:S(2)}, u32[]{:S(2)}) collective-permute-start(f32[16,16]{1,0:T(8,128)S(1)} %get-tuple-element.21), channel_id=1, source_target_pairs={{0,3},{1,2},{2,1},{3,0},{4,7},{5,6},{6,5},{7,4},{8,11},{9,10},{10,... | collective-permute-start | bytes 3080 | tf_op jit(solution)/shard_map/ppermute | solution.py:342
  26.9 3.7 %collective-permute-start.12 = (f32[16,16]{1,0:T(8,128)S(1)}, f32[16,16]{1,0:T(8,128)S(1)}, u32[]{:S(2)}, u32[]{:S(2)}) collective-permute-start(f32[16,16]{1,0:T(8,128)S(1)} %get-tuple-element.22), channel_id=1, source_target_pairs={{0,1},{1,0},{2,3},{3,2},{4,5},{5,4},{6,7},{7,6},{8,9},{9,8},{10,11... | collective-permute-start | bytes 3080 | tf_op jit(solution)/shard_map/ppermute | solution.py:342
  26.9 4.5 %collective-permute-start.11 = (f32[16,16]{1,0:T(8,128)S(1)}, f32[16,16]{1,0:T(8,128)S(1)}, u32[]{:S(2)}, u32[]{:S(2)}) collective-permute-start(f32[16,16]{1,0:T(8,128)S(1)} %get-tuple-element.23), channel_id=1, source_target_pairs={{0,2},{1,3},{2,0},{3,1},{4,6},{5,7},{6,4},{7,5},{8,10},{9,11},{10,... | collective-permute-start | bytes 3080 | tf_op jit(solution)/shard_map/ppermute | solution.py:342

commit v7 on v5

--- a/solution.py
+++ b/solution.py
@@ -193,12 +193,20 @@
         fits = left if most is None else jnp.where(need <= most, left, 0)
         counts.append(fits * need)
         left = left - fits
+    if len(options) == 2 and options[0][1] == 2:
+        sizes = options[0][0], options[1][0]
+        both = jnp.where((total > 2 * sizes[0]) & (total <= sum(sizes)), 1, 0)
+        counts = [jnp.where(both == 1, 1, count) for count in counts]
     return counts
 
 
 def cover(counts, options, step, carry):
+    base = 0
     for count, (size, unused) in zip(counts, options):
-        carry = lax.fori_loop(0, count, lambda k, c, size=size: step(pl.multiple_of(k * size, LANES), size, c), carry)
+        carry = lax.fori_loop(
+            0, count, lambda k, c, size=size, base=base: step(pl.multiple_of(base + k * size, LANES), size, c), carry
+        )
+        base = base + count * size
     return carry
 
 

time: 32.4 us -> 32.4 us (level)
  no operation moved by 1% of the time
where the time goes in v7:
time: 32.4 us; the launch traced here: 32.2 us
  starting transfers between devices  14.7 us (45%)
  waiting for transfers between devices  9.07 us (28%)
  Pallas kernels  6.17 us (19%)
  local copies, waits for them, and re-layouts  1.6 us (5%)
  other arithmetic  0.6 us (2%)
    ppermute x6, starting transfers between devices, across(): return lax.ppermute(array, 'narrow', [(i, i ^ apart) for i in range(subs)])  10.8 us
    ppermute x6, waiting for transfers between devices, across(): return lax.ppermute(array, 'narrow', [(i, i ^ apart) for i in range(subs)])  7.36 us
    pallas_call x1, Pallas kernels, local_terms(): pl.pallas_call(functools.partial(energies, (len(near), len(far))), out_sh...  5.11 us
    ppermute x7, starting transfers between devices, swap(): return lax.ppermute(array, 'group', [(i, i ^ apart) for i in range(groups)])  3.9 us
    ppermute x7, waiting for transfers between devices, swap(): return lax.ppermute(array, 'group', [(i, i ^ apart) for i in range(groups)])  1.7 us
    unnamed x10, local copies, waits for them, and re-layouts  1.6 us
  transfers between devices with their start and end apart: 13, of which 8 were waited for; matrix products, arithmetic and copies ran while one was open for 0% of the time, Pallas kernels for 1%

profile of v7, /device:TPU:0, one launch (start us, length us, event | category | flops | bytes accessed | tf_op | source)
XLA Modules:
  0.0 32.2 jit_solution(7299695366985895873)
XLA Ops:
  0.0 0.7 %copy-done.1 = f32[16,16]{1,0:T(8,128)S(1)} copy-done((f32[16,16]{1,0:T(8,128)S(1)}, f32[16,16]{1,0:T(8,128)}, u32[]{:S(2)}) %copy-start.1) | copy-done | bytes 1048
  0.7 0.9 %copy-done = bf16[16,3675]{1,0:T(8,128)(2,1)S(1)} copy-done((bf16[16,3675]{1,0:T(8,128)(2,1)S(1)}, bf16[16,3675]{1,0:T(8,128)(2,1)}, u32[]{:S(2)}) %copy-start) | copy-done | bytes 117624
  1.6 0.5 %pack.1 = (bf16[16,3968]{1,0:T(8,128)(2,1)S(1)}, bf16[64,128]{1,0:T(8,128)(2,1)S(1)}) custom-call(s32[1]{0:T(128)} %bitcast.mine_ref, bf16[16,3675]{1,0:T(8,128)(2,1)S(1)} %copy-done, s32[1,16]{1,0:T(1,128)S(1)} %bitcast.3, f32[1,49]{1,0:T(1,128)S(1)} %bitcast.4, f32[16,16]{1,0:T(8,128)S(1)} %copy-done.1, s32[4,8]{1,0:T(4,128)S(1)} %copy-done.2), custom_call_target="tpu_custom_call" | custom-call | tf_op jit(solution)/shard_map/pack/pallas_call | solution.py:130
  2.1 4.1 %collective-permute-start.1 = (bf16[16,3968]{1,0:T(8,128)(2,1)S(1)}, bf16[16,3968]{1,0:T(8,128)(2,1)S(1)}, u32[]{:S(2)}, u32[]{:S(2)}) collective-permute-start(bf16[16,3968]{1,0:T(8,128)(2,1)S(1)} %get-tuple-element.13.refs_0_.refs_6_.refs_10_), channel_id=1, source_target_pairs={{0,2},{1,3},{2,0},{3,1},{4,6},{5,7},{6,4},{7,5},{8,10},{9,11},{10,... | collective-permute-start | bytes 380936 | tf_op jit(solution)/shard_map/ppermute | solution.py:350
  6.2 2.4 %collective-permute-start.5 = (bf16[16,3968]{1,0:T(8,128)(2,1)S(1)}, bf16[16,3968]{1,0:T(8,128)(2,1)S(1)}, u32[]{:S(2)}, u32[]{:S(2)}) collective-permute-start(bf16[16,3968]{1,0:T(8,128)(2,1)S(1)} %get-tuple-element.13.refs_0_.refs_6_.refs_10_), channel_id=1, source_target_pairs={{0,24},{4,28},{8,16},{12,20},{16,8},{20,12},{24,0},{28,4},{1,25},{... | collective-permute-start | bytes 380936 | tf_op jit(solution)/shard_map/ppermute | solution.py:347
  8.7 0.5 %collective-permute-start.4 = (bf16[16,3968]{1,0:T(8,128)(2,1)S(1)}, bf16[16,3968]{1,0:T(8,128)(2,1)S(1)}, u32[]{:S(2)}, u32[]{:S(2)}) collective-permute-start(bf16[16,3968]{1,0:T(8,128)(2,1)S(1)} %get-tuple-element.13.refs_0_.refs_6_.refs_10_), channel_id=1, source_target_pairs={{0,16},{4,20},{8,24},{12,28},{16,0},{20,4},{24,8},{28,12},{1,17},{... | collective-permute-start | bytes 380936 | tf_op jit(solution)/shard_map/ppermute | solution.py:347
  9.2 0.5 %collective-permute-start.3 = (bf16[16,3968]{1,0:T(8,128)(2,1)S(1)}, bf16[16,3968]{1,0:T(8,128)(2,1)S(1)}, u32[]{:S(2)}, u32[]{:S(2)}) collective-permute-start(bf16[16,3968]{1,0:T(8,128)(2,1)S(1)} %get-tuple-element.13.refs_0_.refs_6_.refs_10_), channel_id=1, source_target_pairs={{0,8},{4,12},{8,0},{12,4},{16,24},{20,28},{24,16},{28,20},{1,9},{5... | collective-permute-start | bytes 380936 | tf_op jit(solution)/shard_map/ppermute | solution.py:347
  9.7 1.6 %collective-permute-start = (bf16[16,3968]{1,0:T(8,128)(2,1)S(1)}, bf16[16,3968]{1,0:T(8,128)(2,1)S(1)}, u32[]{:S(2)}, u32[]{:S(2)}) collective-permute-start(bf16[16,3968]{1,0:T(8,128)(2,1)S(1)} %get-tuple-element.13.refs_0_.refs_6_.refs_10_), channel_id=1, source_target_pairs={{0,1},{1,0},{2,3},{3,2},{4,5},{5,4},{6,7},{7,6},{8,9},{9,8},{10,11... | collective-permute-start | bytes 380936 | tf_op jit(solution)/shard_map/ppermute | solution.py:350
  11.3 1.2 %collective-permute-done.1.refs_2_.refs_8_ = bf16[16,3968]{1,0:T(8,128)(2,1)S(1)} collective-permute-done((bf16[16,3968]{1,0:T(8,128)(2,1)S(1)}, bf16[16,3968]{1,0:T(8,128)(2,1)S(1)}, u32[]{:S(2)}, u32[]{:S(2)}) %collective-permute-start.1) | collective-permute-done | bytes 127008 | tf_op jit(solution)/shard_map/ppermute | solution.py:350
  12.5 0.7 %collective-permute-start.2 = (bf16[16,3968]{1,0:T(8,128)(2,1)S(1)}, bf16[16,3968]{1,0:T(8,128)(2,1)S(1)}, u32[]{:S(2)}, u32[]{:S(2)}) collective-permute-start(bf16[16,3968]{1,0:T(8,128)(2,1)S(1)} %collective-permute-done.1.refs_2_.refs_8_), channel_id=1, source_target_pairs={{0,1},{1,0},{2,3},{3,2},{4,5},{5,4},{6,7},{7,6},{8,9},{9,8},{10,11... | collective-permute-start | bytes 380936 | tf_op jit(solution)/shard_map/ppermute | solution.py:350
  13.1 1.6 %collective-permute-done.4.refs_2_.refs_12_ = bf16[16,3968]{1,0:T(8,128)(2,1)S(1)} collective-permute-done((bf16[16,3968]{1,0:T(8,128)(2,1)S(1)}, bf16[16,3968]{1,0:T(8,128)(2,1)S(1)}, u32[]{:S(2)}, u32[]{:S(2)}) %collective-permute-start.4) | collective-permute-done | bytes 127008 | tf_op jit(solution)/shard_map/ppermute | solution.py:347
  14.7 0.1 collective-permute-done.3.refs_1_.refs_11_
  14.8 0.4 %collective-permute-start.8 = (bf16[16,3968]{1,0:T(8,128)(2,1)S(1)}, bf16[16,3968]{1,0:T(8,128)(2,1)S(1)}, u32[]{:S(2)}, u32[]{:S(2)}) collective-permute-start(bf16[16,3968]{1,0:T(8,128)(2,1)S(1)} %collective-permute-done.4.refs_2_.refs_12_), channel_id=1, source_target_pairs={{0,4},{4,0},{8,12},{12,8},{16,20},{20,16},{24,28},{28,24},{1,5},{5... | collective-permute-start | bytes 380936 | tf_op jit(solution)/shard_map/ppermute | solution.py:347
  15.2 0.7 %collective-permute-done.refs_1_.refs_7_ = bf16[16,3968]{1,0:T(8,128)(2,1)S(1)} collective-permute-done((bf16[16,3968]{1,0:T(8,128)(2,1)S(1)}, bf16[16,3968]{1,0:T(8,128)(2,1)S(1)}, u32[]{:S(2)}, u32[]{:S(2)}) %collective-permute-start) | collective-permute-done | bytes 127008 | tf_op jit(solution)/shard_map/ppermute | solution.py:350
  15.9 1.9 %collective-permute-done.2.refs_3_.refs_9_ = bf16[16,3968]{1,0:T(8,128)(2,1)S(1)} collective-permute-done((bf16[16,3968]{1,0:T(8,128)(2,1)S(1)}, bf16[16,3968]{1,0:T(8,128)(2,1)S(1)}, u32[]{:S(2)}, u32[]{:S(2)}) %collective-permute-start.2) | collective-permute-done | bytes 127008 | tf_op jit(solution)/shard_map/ppermute | solution.py:350
  17.8 0.2 rank.2
  18.0 0.4 %rank.3 = (bf16[64,64]{1,0:T(8,128)(2,1)S(1)}, s32[8,128]{1,0:T(8,128)S(1)}, bf16[64,128]{1,0:T(8,128)(2,1)S(1)}, bf16[64,128]{1,0:T(8,128)(2,1)S(1)}) custom-call(bf16[64,128]{1,0:T(8,128)(2,1)S(1)} %get-tuple-element.15.met_ref, bf16[16,3968]{1,0:T(8,128)(2,1)S(1)} %get-tuple-element.13.refs_0_.refs_6_.refs_10_, ...), custom_call_target="tpu_custom_call" | custom-call | flops 2000000000 | bytes 1000000 | tf_op jit(solution)/shard_map/rank/pallas_call | solution.py:233
  18.4 5.1 %energies.1 = f32[64,16]{1,0:T(8,128)S(1)} custom-call(s32[8,128]{1,0:T(8,128)S(1)} %get-tuple-element.14.refs_0_, s32[8,128]{1,0:T(8,128)S(1)} %get-tuple-element.16.refs_1_, bf16[64,64]{1,0:T(8,128)(2,1)S(1)} %get-tuple-element.17.refs_2_, bf16[64,64]{1,0:T(8,128)(2,1)S(1)} %get-tuple-element.18.refs_3_, bf16[64,128]{1,0:T(8,128)(2,1)S(1)} %get-tuple-element.19.refs_4_, ...), custom_call_target="tpu_custom_call" | custom-call | tf_op jit(solution)/shard_map/energies/pallas_call | solution.py:318
  23.5 3.5 %collective-permute-start.10 = (f32[16,16]{1,0:T(8,128)S(1)}, f32[16,16]{1,0:T(8,128)S(1)}, u32[]{:S(2)}, u32[]{:S(2)}) collective-permute-start(f32[16,16]{1,0:T(8,128)S(1)} %get-tuple-element.21), channel_id=1, source_target_pairs={{0,3},{1,2},{2,1},{3,0},{4,7},{5,6},{6,5},{7,4},{8,11},{9,10},{10,... | collective-permute-start | bytes 3080 | tf_op jit(solution)/shard_map/ppermute | solution.py:350
  27.0 0.9 %collective-permute-start.11 = (f32[16,16]{1,0:T(8,128)S(1)}, f32[16,16]{1,0:T(8,128)S(1)}, u32[]{:S(2)}, u32[]{:S(2)}) collective-permute-start(f32[16,16]{1,0:T(8,128)S(1)} %get-tuple-element.23), channel_id=1, source_target_pairs={{0,2},{1,3},{2,0},{3,1},{4,6},{5,7},{6,4},{7,5},{8,10},{9,11},{10,... | collective-permute-start | bytes 3080 | tf_op jit(solution)/shard_map/ppermute | solution.py:350
  28.0 1.1 %collective-permute-done.10 = f32[16,16]{1,0:T(8,128)S(1)} collective-permute-done((f32[16,16]{1,0:T(8,128)S(1)}, f32[16,16]{1,0:T(8,128)S(1)}, u32[]{:S(2)}, u32[]{:S(2)}) %collective-permute-start.10) | collective-permute-done | bytes 1056 | tf_op jit(solution)/shard_map/ppermute | solution.py:350
  29.0 1.7 %collective-permute-done.12 = f32[16,16]{1,0:T(8,128)S(1)} collective-permute-done((f32[16,16]{1,0:T(8,128)S(1)}, f32[16,16]{1,0:T(8,128)S(1)}, u32[]{:S(2)}, u32[]{:S(2)}) %collective-permute-start.12) | collective-permute-done | bytes 1056 | tf_op jit(solution)/shard_map/ppermute | solution.py:350
  30.7 0.9 %collective-permute-done.11 = f32[16,16]{1,0:T(8,128)S(1)} collective-permute-done((f32[16,16]{1,0:T(8,128)S(1)}, f32[16,16]{1,0:T(8,128)S(1)}, u32[]{:S(2)}, u32[]{:S(2)}) %collective-permute-start.11) | collective-permute-done | bytes 1056 | tf_op jit(solution)/shard_map/ppermute | solution.py:350
  31.6 0.6 %fusion.1 = f32[16,16]{1,0:T(8,128)} fusion(f32[16,16]{1,0:T(8,128)S(1)} %collective-permute-done.12, f32[16,16]{1,0:T(8,128)S(1)} %collective-permute-done.11, f32[16,16]{1,0:T(8,128)S(1)} %collective-permute-done.10, f32[64,16]{1,0:T(8,128)S(1)} %energies.1), kind=kLoop, calls=%fused_computation.2 | loop fusion | flops 768 | bytes 5120 | tf_op jit(solution)/shard_map/add | solution.py:364
  (18 shorter events, 0.0 us)
Async XLA Ops:
  0.0 0.7 %copy-start.1 = (f32[16,16]{1,0:T(8,128)S(1)}, f32[16,16]{1,0:T(8,128)}, u32[]{:S(2)}) copy-start(f32[16,16]{1,0:T(8,128)} %refs_3_.1) | copy-start | bytes 3076
  0.0 0.7 %copy-start.2 = (s32[4,8]{1,0:T(4,128)S(1)}, s32[4,8]{1,0:T(4,128)}, u32[]{:S(2)}) copy-start(s32[4,8]{1,0:T(4,128)} %refs_4_.1) | copy-start | bytes 388
  0.0 0.7 %copy-start.3 = (s32[16]{0:T(128)S(1)}, s32[16]{0:T(128)}, u32[]{:S(2)}) copy-start(s32[16]{0:T(128)} %param.6) | copy-start | bytes 196
  0.0 0.7 %copy-start.4 = (f32[49]{0:T(128)S(1)}, f32[49]{0:T(128)}, u32[]{:S(2)}) copy-start(f32[49]{0:T(128)} %param.7) | copy-start | bytes 592
  0.7 0.9 %copy-start = (bf16[16,3675]{1,0:T(8,128)(2,1)S(1)}, bf16[16,3675]{1,0:T(8,128)(2,1)}, u32[]{:S(2)}) copy-start(bf16[16,3675]{1,0:T(8,128)(2,1)} %refs_0_.1) | copy-start | bytes 352804
  2.1 10.3 %collective-permute-start.1 = (bf16[16,3968]{1,0:T(8,128)(2,1)S(1)}, bf16[16,3968]{1,0:T(8,128)(2,1)S(1)}, u32[]{:S(2)}, u32[]{:S(2)}) collective-permute-start(bf16[16,3968]{1,0:T(8,128)(2,1)S(1)} %get-tuple-element.13.refs_0_.refs_6_.refs_10_), channel_id=1, source_target_pairs={{0,2},{1,3},{2,0},{3,1},{4,6},{5,7},{6,4},{7,5},{8,10},{9,11},{10,... | collective-permute-start | bytes 380936 | tf_op jit(solution)/shard_map/ppermute | solution.py:350
  6.2 6.9 %collective-permute-start.5 = (bf16[16,3968]{1,0:T(8,128)(2,1)S(1)}, bf16[16,3968]{1,0:T(8,128)(2,1)S(1)}, u32[]{:S(2)}, u32[]{:S(2)}) collective-permute-start(bf16[16,3968]{1,0:T(8,128)(2,1)S(1)} %get-tuple-element.13.refs_0_.refs_6_.refs_10_), channel_id=1, source_target_pairs={{0,24},{4,28},{8,16},{12,20},{16,8},{20,12},{24,0},{28,4},{1,25},{... | collective-permute-start | bytes 380936 | tf_op jit(solution)/shard_map/ppermute | solution.py:347
  8.7 6.0 %collective-permute-start.4 = (bf16[16,3968]{1,0:T(8,128)(2,1)S(1)}, bf16[16,3968]{1,0:T(8,128)(2,1)S(1)}, u32[]{:S(2)}, u32[]{:S(2)}) collective-permute-start(bf16[16,3968]{1,0:T(8,128)(2,1)S(1)} %get-tuple-element.13.refs_0_.refs_6_.refs_10_), channel_id=1, source_target_pairs={{0,16},{4,20},{8,24},{12,28},{16,0},{20,4},{24,8},{28,12},{1,17},{... | collective-permute-start | bytes 380936 | tf_op jit(solution)/shard_map/ppermute | solution.py:347
  9.2 5.6 %collective-permute-start.3 = (bf16[16,3968]{1,0:T(8,128)(2,1)S(1)}, bf16[16,3968]{1,0:T(8,128)(2,1)S(1)}, u32[]{:S(2)}, u32[]{:S(2)}) collective-permute-start(bf16[16,3968]{1,0:T(8,128)(2,1)S(1)} %get-tuple-element.13.refs_0_.refs_6_.refs_10_), channel_id=1, source_target_pairs={{0,8},{4,12},{8,0},{12,4},{16,24},{20,28},{24,16},{28,20},{1,9},{5... | collective-permute-start | bytes 380936 | tf_op jit(solution)/shard_map/ppermute | solution.py:347
  9.7 6.2 %collective-permute-start = (bf16[16,3968]{1,0:T(8,128)(2,1)S(1)}, bf16[16,3968]{1,0:T(8,128)(2,1)S(1)}, u32[]{:S(2)}, u32[]{:S(2)}) collective-permute-start(bf16[16,3968]{1,0:T(8,128)(2,1)S(1)} %get-tuple-element.13.refs_0_.refs_6_.refs_10_), channel_id=1, source_target_pairs={{0,1},{1,0},{2,3},{3,2},{4,5},{5,4},{6,7},{7,6},{8,9},{9,8},{10,11... | collective-permute-start | bytes 380936 | tf_op jit(solution)/shard_map/ppermute | solution.py:350
  12.5 5.3 %collective-permute-start.2 = (bf16[16,3968]{1,0:T(8,128)(2,1)S(1)}, bf16[16,3968]{1,0:T(8,128)(2,1)S(1)}, u32[]{:S(2)}, u32[]{:S(2)}) collective-permute-start(bf16[16,3968]{1,0:T(8,128)(2,1)S(1)} %collective-permute-done.1.refs_2_.refs_8_), channel_id=1, source_target_pairs={{0,1},{1,0},{2,3},{3,2},{4,5},{5,4},{6,7},{7,6},{8,9},{9,8},{10,11... | collective-permute-start | bytes 380936 | tf_op jit(solution)/shard_map/ppermute | solution.py:350
  13.1 4.9 %collective-permute-start.6 = (bf16[16,3968]{1,0:T(8,128)(2,1)S(1)}, bf16[16,3968]{1,0:T(8,128)(2,1)S(1)}, u32[]{:S(2)}, u32[]{:S(2)}) collective-permute-start(bf16[16,3968]{1,0:T(8,128)(2,1)S(1)} %get-tuple-element.13.refs_0_.refs_6_.refs_10_), channel_id=1, source_target_pairs={{0,4},{4,0},{8,12},{12,8},{16,20},{20,16},{24,28},{28,24},{1,5},{5... | collective-permute-start | bytes 380936 | tf_op jit(solution)/shard_map/ppermute | solution.py:347
  14.7 3.3 %collective-permute-start.9 = (bf16[16,3968]{1,0:T(8,128)(2,1)S(1)}, bf16[16,3968]{1,0:T(8,128)(2,1)S(1)}, u32[]{:S(2)}, u32[]{:S(2)}) collective-permute-start(bf16[16,3968]{1,0:T(8,128)(2,1)S(1)} %collective-permute-done.5.refs_3_.refs_13_), channel_id=1, source_target_pairs={{0,4},{4,0},{8,12},{12,8},{16,20},{20,16},{24,28},{28,24},{1,5},{5... | collective-permute-start | bytes 380936 | tf_op jit(solution)/shard_map/ppermute | solution.py:347
  14.8 3.2 %collective-permute-start.8 = (bf16[16,3968]{1,0:T(8,128)(2,1)S(1)}, bf16[16,3968]{1,0:T(8,128)(2,1)S(1)}, u32[]{:S(2)}, u32[]{:S(2)}) collective-permute-start(bf16[16,3968]{1,0:T(8,128)(2,1)S(1)} %collective-permute-done.4.refs_2_.refs_12_), channel_id=1, source_target_pairs={{0,4},{4,0},{8,12},{12,8},{16,20},{20,16},{24,28},{28,24},{1,5},{5... | collective-permute-start | bytes 380936 | tf_op jit(solution)/shard_map/ppermute | solution.py:347
  15.9 2.1 %collective-permute-start.7 = (bf16[16,3968]{1,0:T(8,128)(2,1)S(1)}, bf16[16,3968]{1,0:T(8,128)(2,1)S(1)}, u32[]{:S(2)}, u32[]{:S(2)}) collective-permute-start(bf16[16,3968]{1,0:T(8,128)(2,1)S(1)} %collective-permute-done.3.refs_1_.refs_11_), channel_id=1, source_target_pairs={{0,4},{4,0},{8,12},{12,8},{16,20},{20,16},{24,28},{28,24},{1,5},{5... | collective-permute-start | bytes 380936 | tf_op jit(solution)/shard_map/ppermute | solution.py:347
  23.5 5.5 %collective-permute-start.10 = (f32[16,16]{1,0:T(8,128)S(1)}, f32[16,16]{1,0:T(8,128)S(1)}, u32[]{:S(2)}, u32[]{:S(2)}) collective-permute-start(f32[16,16]{1,0:T(8,128)S(1)} %get-tuple-element.21), channel_id=1, source_target_pairs={{0,3},{1,2},{2,1},{3,0},{4,7},{5,6},{6,5},{7,4},{8,11},{9,10},{10,... | collective-permute-start | bytes 3080 | tf_op jit(solution)/shard_map/ppermute | solution.py:350
  27.0 3.7 %collective-permute-start.12 = (f32[16,16]{1,0:T(8,128)S(1)}, f32[16,16]{1,0:T(8,128)S(1)}, u32[]{:S(2)}, u32[]{:S(2)}) collective-permute-start(f32[16,16]{1,0:T(8,128)S(1)} %get-tuple-element.22), channel_id=1, source_target_pairs={{0,1},{1,0},{2,3},{3,2},{4,5},{5,4},{6,7},{7,6},{8,9},{9,8},{10,11... | collective-permute-start | bytes 3080 | tf_op jit(solution)/shard_map/ppermute | solution.py:350
  27.0 4.5 %collective-permute-start.11 = (f32[16,16]{1,0:T(8,128)S(1)}, f32[16,16]{1,0:T(8,128)S(1)}, u32[]{:S(2)}, u32[]{:S(2)}) collective-permute-start(f32[16,16]{1,0:T(8,128)S(1)} %get-tuple-element.23), channel_id=1, source_target_pairs={{0,2},{1,3},{2,0},{3,1},{4,6},{5,7},{6,4},{7,5},{8,10},{9,11},{10,... | collective-permute-start | bytes 3080 | tf_op jit(solution)/shard_map/ppermute | solution.py:350

commit v8 on v5

--- a/solution.py
+++ b/solution.py
@@ -352,7 +352,7 @@
     cols_rank = rank(rank_cols_kernel, [met, *far], cols, (met.shape, (cols, LANES)), 2 * 10**9)
     terms = local_terms(rows_rank, cols_rank, near, far)
     total = terms[:images]
-    for apart in range(subs - 1, 0, -1):
+    for apart in (subs - 1, *range(1, subs - 1)):
         total = total + across(terms[apart * images : (apart + 1) * images], apart)
     return total
 

time: 32.4 us -> 32.4 us (level)
  waiting for transfers between devices: 9.06 us -> 8.73 us
    ppermute x6, waiting for transfers between devices: 7.36 us -> 7.03 us  [across(): return lax.ppermute(array, 'narrow', [(i, i ^ apart) for i in range(subs)])]
  transfers between devices with their start and end apart: 13 -> 13, of which waited for: 8 -> 7; matrix products, arithmetic and copies ran while one was open for 0% -> 0% of each run, Pallas kernels for 1% -> 1%
where the time goes in v8:
time: 32.4 us; the launch traced here: 32.2 us
  starting transfers between devices  14.7 us (45%)
  waiting for transfers between devices  8.73 us (27%)
  Pallas kernels  6.5 us (20%)
  local copies, waits for them, and re-layouts  1.6 us (5%)
  other arithmetic  0.6 us (2%)
    ppermute x6, starting transfers between devices, across(): return lax.ppermute(array, 'narrow', [(i, i ^ apart) for i in range(subs)])  10.8 us
    ppermute x6, waiting for transfers between devices, across(): return lax.ppermute(array, 'narrow', [(i, i ^ apart) for i in range(subs)])  7.03 us
    pallas_call x1, Pallas kernels, local_terms(): pl.pallas_call(functools.partial(energies, (len(near), len(far))), out_sh...  5.44 us
    ppermute x7, starting transfers between devices, swap(): return lax.ppermute(array, 'group', [(i, i ^ apart) for i in range(groups)])  3.9 us
    ppermute x7, waiting for transfers between devices, swap(): return lax.ppermute(array, 'group', [(i, i ^ apart) for i in range(groups)])  1.7 us
    unnamed x10, local copies, waits for them, and re-layouts  1.6 us
  transfers between devices with their start and end apart: 13, of which 7 were waited for; matrix products, arithmetic and copies ran while one was open for 0% of the time, Pallas kernels for 1%

profile of v8, /device:TPU:0, one launch (start us, length us, event | category | flops | bytes accessed | tf_op | source)
XLA Modules:
  0.0 32.2 jit_solution(2017897582189535059)
XLA Ops:
  0.0 0.7 %copy-done.1 = f32[16,16]{1,0:T(8,128)S(1)} copy-done((f32[16,16]{1,0:T(8,128)S(1)}, f32[16,16]{1,0:T(8,128)}, u32[]{:S(2)}) %copy-start.1) | copy-done | bytes 1048
  0.7 0.9 %copy-done = bf16[16,3675]{1,0:T(8,128)(2,1)S(1)} copy-done((bf16[16,3675]{1,0:T(8,128)(2,1)S(1)}, bf16[16,3675]{1,0:T(8,128)(2,1)}, u32[]{:S(2)}) %copy-start) | copy-done | bytes 117624
  1.6 0.5 %pack.1 = (bf16[16,3968]{1,0:T(8,128)(2,1)S(1)}, bf16[64,128]{1,0:T(8,128)(2,1)S(1)}) custom-call(s32[1]{0:T(128)} %bitcast.mine_ref, bf16[16,3675]{1,0:T(8,128)(2,1)S(1)} %copy-done, s32[1,16]{1,0:T(1,128)S(1)} %bitcast.3, f32[1,49]{1,0:T(1,128)S(1)} %bitcast.4, f32[16,16]{1,0:T(8,128)S(1)} %copy-done.1, s32[4,8]{1,0:T(4,128)S(1)} %copy-done.2), custom_call_target="tpu_custom_call" | custom-call | tf_op jit(solution)/shard_map/pack/pallas_call | solution.py:130
  2.1 4.1 %collective-permute-start.1 = (bf16[16,3968]{1,0:T(8,128)(2,1)S(1)}, bf16[16,3968]{1,0:T(8,128)(2,1)S(1)}, u32[]{:S(2)}, u32[]{:S(2)}) collective-permute-start(bf16[16,3968]{1,0:T(8,128)(2,1)S(1)} %get-tuple-element.13.refs_0_.refs_6_.refs_10_), channel_id=1, source_target_pairs={{0,2},{1,3},{2,0},{3,1},{4,6},{5,7},{6,4},{7,5},{8,10},{9,11},{10,... | collective-permute-start | bytes 380936 | tf_op jit(solution)/shard_map/ppermute | solution.py:342
  6.2 2.4 %collective-permute-start.5 = (bf16[16,3968]{1,0:T(8,128)(2,1)S(1)}, bf16[16,3968]{1,0:T(8,128)(2,1)S(1)}, u32[]{:S(2)}, u32[]{:S(2)}) collective-permute-start(bf16[16,3968]{1,0:T(8,128)(2,1)S(1)} %get-tuple-element.13.refs_0_.refs_6_.refs_10_), channel_id=1, source_target_pairs={{0,24},{4,28},{8,16},{12,20},{16,8},{20,12},{24,0},{28,4},{1,25},{... | collective-permute-start | bytes 380936 | tf_op jit(solution)/shard_map/ppermute | solution.py:339
  8.7 0.5 %collective-permute-start.4 = (bf16[16,3968]{1,0:T(8,128)(2,1)S(1)}, bf16[16,3968]{1,0:T(8,128)(2,1)S(1)}, u32[]{:S(2)}, u32[]{:S(2)}) collective-permute-start(bf16[16,3968]{1,0:T(8,128)(2,1)S(1)} %get-tuple-element.13.refs_0_.refs_6_.refs_10_), channel_id=1, source_target_pairs={{0,16},{4,20},{8,24},{12,28},{16,0},{20,4},{24,8},{28,12},{1,17},{... | collective-permute-start | bytes 380936 | tf_op jit(solution)/shard_map/ppermute | solution.py:339
  9.2 0.5 %collective-permute-start.3 = (bf16[16,3968]{1,0:T(8,128)(2,1)S(1)}, bf16[16,3968]{1,0:T(8,128)(2,1)S(1)}, u32[]{:S(2)}, u32[]{:S(2)}) collective-permute-start(bf16[16,3968]{1,0:T(8,128)(2,1)S(1)} %get-tuple-element.13.refs_0_.refs_6_.refs_10_), channel_id=1, source_target_pairs={{0,8},{4,12},{8,0},{12,4},{16,24},{20,28},{24,16},{28,20},{1,9},{5... | collective-permute-start | bytes 380936 | tf_op jit(solution)/shard_map/ppermute | solution.py:339
  9.7 1.6 %collective-permute-start = (bf16[16,3968]{1,0:T(8,128)(2,1)S(1)}, bf16[16,3968]{1,0:T(8,128)(2,1)S(1)}, u32[]{:S(2)}, u32[]{:S(2)}) collective-permute-start(bf16[16,3968]{1,0:T(8,128)(2,1)S(1)} %get-tuple-element.13.refs_0_.refs_6_.refs_10_), channel_id=1, source_target_pairs={{0,1},{1,0},{2,3},{3,2},{4,5},{5,4},{6,7},{7,6},{8,9},{9,8},{10,11... | collective-permute-start | bytes 380936 | tf_op jit(solution)/shard_map/ppermute | solution.py:342
  11.3 1.2 %collective-permute-done.1.refs_2_.refs_8_ = bf16[16,3968]{1,0:T(8,128)(2,1)S(1)} collective-permute-done((bf16[16,3968]{1,0:T(8,128)(2,1)S(1)}, bf16[16,3968]{1,0:T(8,128)(2,1)S(1)}, u32[]{:S(2)}, u32[]{:S(2)}) %collective-permute-start.1) | collective-permute-done | bytes 127008 | tf_op jit(solution)/shard_map/ppermute | solution.py:342
  12.5 0.7 %collective-permute-start.2 = (bf16[16,3968]{1,0:T(8,128)(2,1)S(1)}, bf16[16,3968]{1,0:T(8,128)(2,1)S(1)}, u32[]{:S(2)}, u32[]{:S(2)}) collective-permute-start(bf16[16,3968]{1,0:T(8,128)(2,1)S(1)} %collective-permute-done.1.refs_2_.refs_8_), channel_id=1, source_target_pairs={{0,1},{1,0},{2,3},{3,2},{4,5},{5,4},{6,7},{7,6},{8,9},{9,8},{10,11... | collective-permute-start | bytes 380936 | tf_op jit(solution)/shard_map/ppermute | solution.py:342
  13.1 1.6 %collective-permute-done.4.refs_2_.refs_12_ = bf16[16,3968]{1,0:T(8,128)(2,1)S(1)} collective-permute-done((bf16[16,3968]{1,0:T(8,128)(2,1)S(1)}, bf16[16,3968]{1,0:T(8,128)(2,1)S(1)}, u32[]{:S(2)}, u32[]{:S(2)}) %collective-permute-start.4) | collective-permute-done | bytes 127008 | tf_op jit(solution)/shard_map/ppermute | solution.py:339
  14.7 0.0 collective-permute-start.9
  14.7 0.1 collective-permute-done.3.refs_1_.refs_11_
  14.8 0.4 %collective-permute-start.8 = (bf16[16,3968]{1,0:T(8,128)(2,1)S(1)}, bf16[16,3968]{1,0:T(8,128)(2,1)S(1)}, u32[]{:S(2)}, u32[]{:S(2)}) collective-permute-start(bf16[16,3968]{1,0:T(8,128)(2,1)S(1)} %collective-permute-done.4.refs_2_.refs_12_), channel_id=1, source_target_pairs={{0,4},{4,0},{8,12},{12,8},{16,20},{20,16},{24,28},{28,24},{1,5},{5... | collective-permute-start | bytes 380936 | tf_op jit(solution)/shard_map/ppermute | solution.py:339
  15.2 0.7 %collective-permute-done.refs_1_.refs_7_ = bf16[16,3968]{1,0:T(8,128)(2,1)S(1)} collective-permute-done((bf16[16,3968]{1,0:T(8,128)(2,1)S(1)}, bf16[16,3968]{1,0:T(8,128)(2,1)S(1)}, u32[]{:S(2)}, u32[]{:S(2)}) %collective-permute-start) | collective-permute-done | bytes 127008 | tf_op jit(solution)/shard_map/ppermute | solution.py:342
  15.9 1.9 %collective-permute-done.2.refs_3_.refs_9_ = bf16[16,3968]{1,0:T(8,128)(2,1)S(1)} collective-permute-done((bf16[16,3968]{1,0:T(8,128)(2,1)S(1)}, bf16[16,3968]{1,0:T(8,128)(2,1)S(1)}, u32[]{:S(2)}, u32[]{:S(2)}) %collective-permute-start.2) | collective-permute-done | bytes 127008 | tf_op jit(solution)/shard_map/ppermute | solution.py:342
  17.8 0.2 rank.2
  18.0 0.4 %rank.3 = (bf16[64,64]{1,0:T(8,128)(2,1)S(1)}, s32[8,128]{1,0:T(8,128)S(1)}, bf16[64,128]{1,0:T(8,128)(2,1)S(1)}, bf16[64,128]{1,0:T(8,128)(2,1)S(1)}) custom-call(bf16[64,128]{1,0:T(8,128)(2,1)S(1)} %get-tuple-element.15.met_ref, bf16[16,3968]{1,0:T(8,128)(2,1)S(1)} %get-tuple-element.13.refs_0_.refs_6_.refs_10_, ...), custom_call_target="tpu_custom_call" | custom-call | flops 2000000000 | bytes 1000000 | tf_op jit(solution)/shard_map/rank/pallas_call | solution.py:225
  18.4 5.4 %energies.1 = f32[64,16]{1,0:T(8,128)S(1)} custom-call(s32[8,128]{1,0:T(8,128)S(1)} %get-tuple-element.14.refs_0_, s32[8,128]{1,0:T(8,128)S(1)} %get-tuple-element.16.refs_1_, bf16[64,64]{1,0:T(8,128)(2,1)S(1)} %get-tuple-element.17.refs_2_, bf16[64,64]{1,0:T(8,128)(2,1)S(1)} %get-tuple-element.18.refs_3_, bf16[64,128]{1,0:T(8,128)(2,1)S(1)} %get-tuple-element.19.refs_4_, ...), custom_call_target="tpu_custom_call" | custom-call | tf_op jit(solution)/shard_map/energies/pallas_call | solution.py:310
  23.8 3.2 %collective-permute-start.10 = (f32[16,16]{1,0:T(8,128)S(1)}, f32[16,16]{1,0:T(8,128)S(1)}, u32[]{:S(2)}, u32[]{:S(2)}) collective-permute-start(f32[16,16]{1,0:T(8,128)S(1)} %get-tuple-element.21), channel_id=1, source_target_pairs={{0,3},{1,2},{2,1},{3,0},{4,7},{5,6},{6,5},{7,4},{8,11},{9,10},{10,... | collective-permute-start | bytes 3080 | tf_op jit(solution)/shard_map/ppermute | solution.py:342
  27.0 1.3 %collective-permute-start.11 = (f32[16,16]{1,0:T(8,128)S(1)}, f32[16,16]{1,0:T(8,128)S(1)}, u32[]{:S(2)}, u32[]{:S(2)}) collective-permute-start(f32[16,16]{1,0:T(8,128)S(1)} %get-tuple-element.23), channel_id=1, source_target_pairs={{0,1},{1,0},{2,3},{3,2},{4,5},{5,4},{6,7},{7,6},{8,9},{9,8},{10,11... | collective-permute-start | bytes 3080 | tf_op jit(solution)/shard_map/ppermute | solution.py:342
  28.3 1.1 %collective-permute-done.10 = f32[16,16]{1,0:T(8,128)S(1)} collective-permute-done((f32[16,16]{1,0:T(8,128)S(1)}, f32[16,16]{1,0:T(8,128)S(1)}, u32[]{:S(2)}, u32[]{:S(2)}) %collective-permute-start.10) | collective-permute-done | bytes 1056 | tf_op jit(solution)/shard_map/ppermute | solution.py:342
  29.4 2.2 %collective-permute-done.12 = f32[16,16]{1,0:T(8,128)S(1)} collective-permute-done((f32[16,16]{1,0:T(8,128)S(1)}, f32[16,16]{1,0:T(8,128)S(1)}, u32[]{:S(2)}, u32[]{:S(2)}) %collective-permute-start.12) | collective-permute-done | bytes 1056 | tf_op jit(solution)/shard_map/ppermute | solution.py:342
  31.6 0.6 %fusion.1 = f32[16,16]{1,0:T(8,128)} fusion(f32[16,16]{1,0:T(8,128)S(1)} %collective-permute-done.12, f32[16,16]{1,0:T(8,128)S(1)} %collective-permute-done.11, f32[16,16]{1,0:T(8,128)S(1)} %collective-permute-done.10, f32[64,16]{1,0:T(8,128)S(1)} %energies.1), kind=kLoop, calls=%fused_computation.2 | loop fusion | flops 768 | bytes 5120 | tf_op jit(solution)/shard_map/add | solution.py:356
  (18 shorter events, 0.0 us)
Async XLA Ops:
  0.0 0.7 %copy-start.1 = (f32[16,16]{1,0:T(8,128)S(1)}, f32[16,16]{1,0:T(8,128)}, u32[]{:S(2)}) copy-start(f32[16,16]{1,0:T(8,128)} %refs_3_.1) | copy-start | bytes 3076
  0.0 0.7 %copy-start.2 = (s32[4,8]{1,0:T(4,128)S(1)}, s32[4,8]{1,0:T(4,128)}, u32[]{:S(2)}) copy-start(s32[4,8]{1,0:T(4,128)} %refs_4_.1) | copy-start | bytes 388
  0.0 0.7 %copy-start.3 = (s32[16]{0:T(128)S(1)}, s32[16]{0:T(128)}, u32[]{:S(2)}) copy-start(s32[16]{0:T(128)} %param.6) | copy-start | bytes 196
  0.0 0.7 %copy-start.4 = (f32[49]{0:T(128)S(1)}, f32[49]{0:T(128)}, u32[]{:S(2)}) copy-start(f32[49]{0:T(128)} %param.7) | copy-start | bytes 592
  0.7 0.9 %copy-start = (bf16[16,3675]{1,0:T(8,128)(2,1)S(1)}, bf16[16,3675]{1,0:T(8,128)(2,1)}, u32[]{:S(2)}) copy-start(bf16[16,3675]{1,0:T(8,128)(2,1)} %refs_0_.1) | copy-start | bytes 352804
  2.1 10.3 %collective-permute-start.1 = (bf16[16,3968]{1,0:T(8,128)(2,1)S(1)}, bf16[16,3968]{1,0:T(8,128)(2,1)S(1)}, u32[]{:S(2)}, u32[]{:S(2)}) collective-permute-start(bf16[16,3968]{1,0:T(8,128)(2,1)S(1)} %get-tuple-element.13.refs_0_.refs_6_.refs_10_), channel_id=1, source_target_pairs={{0,2},{1,3},{2,0},{3,1},{4,6},{5,7},{6,4},{7,5},{8,10},{9,11},{10,... | collective-permute-start | bytes 380936 | tf_op jit(solution)/shard_map/ppermute | solution.py:342
  6.2 6.9 %collective-permute-start.5 = (bf16[16,3968]{1,0:T(8,128)(2,1)S(1)}, bf16[16,3968]{1,0:T(8,128)(2,1)S(1)}, u32[]{:S(2)}, u32[]{:S(2)}) collective-permute-start(bf16[16,3968]{1,0:T(8,128)(2,1)S(1)} %get-tuple-element.13.refs_0_.refs_6_.refs_10_), channel_id=1, source_target_pairs={{0,24},{4,28},{8,16},{12,20},{16,8},{20,12},{24,0},{28,4},{1,25},{... | collective-permute-start | bytes 380936 | tf_op jit(solution)/shard_map/ppermute | solution.py:339
  8.7 6.0 %collective-permute-start.4 = (bf16[16,3968]{1,0:T(8,128)(2,1)S(1)}, bf16[16,3968]{1,0:T(8,128)(2,1)S(1)}, u32[]{:S(2)}, u32[]{:S(2)}) collective-permute-start(bf16[16,3968]{1,0:T(8,128)(2,1)S(1)} %get-tuple-element.13.refs_0_.refs_6_.refs_10_), channel_id=1, source_target_pairs={{0,16},{4,20},{8,24},{12,28},{16,0},{20,4},{24,8},{28,12},{1,17},{... | collective-permute-start | bytes 380936 | tf_op jit(solution)/shard_map/ppermute | solution.py:339
  9.2 5.6 %collective-permute-start.3 = (bf16[16,3968]{1,0:T(8,128)(2,1)S(1)}, bf16[16,3968]{1,0:T(8,128)(2,1)S(1)}, u32[]{:S(2)}, u32[]{:S(2)}) collective-permute-start(bf16[16,3968]{1,0:T(8,128)(2,1)S(1)} %get-tuple-element.13.refs_0_.refs_6_.refs_10_), channel_id=1, source_target_pairs={{0,8},{4,12},{8,0},{12,4},{16,24},{20,28},{24,16},{28,20},{1,9},{5... | collective-permute-start | bytes 380936 | tf_op jit(solution)/shard_map/ppermute | solution.py:339
  9.7 6.2 %collective-permute-start = (bf16[16,3968]{1,0:T(8,128)(2,1)S(1)}, bf16[16,3968]{1,0:T(8,128)(2,1)S(1)}, u32[]{:S(2)}, u32[]{:S(2)}) collective-permute-start(bf16[16,3968]{1,0:T(8,128)(2,1)S(1)} %get-tuple-element.13.refs_0_.refs_6_.refs_10_), channel_id=1, source_target_pairs={{0,1},{1,0},{2,3},{3,2},{4,5},{5,4},{6,7},{7,6},{8,9},{9,8},{10,11... | collective-permute-start | bytes 380936 | tf_op jit(solution)/shard_map/ppermute | solution.py:342
  12.5 5.3 %collective-permute-start.2 = (bf16[16,3968]{1,0:T(8,128)(2,1)S(1)}, bf16[16,3968]{1,0:T(8,128)(2,1)S(1)}, u32[]{:S(2)}, u32[]{:S(2)}) collective-permute-start(bf16[16,3968]{1,0:T(8,128)(2,1)S(1)} %collective-permute-done.1.refs_2_.refs_8_), channel_id=1, source_target_pairs={{0,1},{1,0},{2,3},{3,2},{4,5},{5,4},{6,7},{7,6},{8,9},{9,8},{10,11... | collective-permute-start | bytes 380936 | tf_op jit(solution)/shard_map/ppermute | solution.py:342
  13.1 4.9 %collective-permute-start.6 = (bf16[16,3968]{1,0:T(8,128)(2,1)S(1)}, bf16[16,3968]{1,0:T(8,128)(2,1)S(1)}, u32[]{:S(2)}, u32[]{:S(2)}) collective-permute-start(bf16[16,3968]{1,0:T(8,128)(2,1)S(1)} %get-tuple-element.13.refs_0_.refs_6_.refs_10_), channel_id=1, source_target_pairs={{0,4},{4,0},{8,12},{12,8},{16,20},{20,16},{24,28},{28,24},{1,5},{5... | collective-permute-start | bytes 380936 | tf_op jit(solution)/shard_map/ppermute | solution.py:339
  14.7 3.3 %collective-permute-start.9 = (bf16[16,3968]{1,0:T(8,128)(2,1)S(1)}, bf16[16,3968]{1,0:T(8,128)(2,1)S(1)}, u32[]{:S(2)}, u32[]{:S(2)}) collective-permute-start(bf16[16,3968]{1,0:T(8,128)(2,1)S(1)} %collective-permute-done.5.refs_3_.refs_13_), channel_id=1, source_target_pairs={{0,4},{4,0},{8,12},{12,8},{16,20},{20,16},{24,28},{28,24},{1,5},{5... | collective-permute-start | bytes 380936 | tf_op jit(solution)/shard_map/ppermute | solution.py:339
  14.8 3.2 %collective-permute-start.8 = (bf16[16,3968]{1,0:T(8,128)(2,1)S(1)}, bf16[16,3968]{1,0:T(8,128)(2,1)S(1)}, u32[]{:S(2)}, u32[]{:S(2)}) collective-permute-start(bf16[16,3968]{1,0:T(8,128)(2,1)S(1)} %collective-permute-done.4.refs_2_.refs_12_), channel_id=1, source_target_pairs={{0,4},{4,0},{8,12},{12,8},{16,20},{20,16},{24,28},{28,24},{1,5},{5... | collective-permute-start | bytes 380936 | tf_op jit(solution)/shard_map/ppermute | solution.py:339
  15.9 2.1 %collective-permute-start.7 = (bf16[16,3968]{1,0:T(8,128)(2,1)S(1)}, bf16[16,3968]{1,0:T(8,128)(2,1)S(1)}, u32[]{:S(2)}, u32[]{:S(2)}) collective-permute-start(bf16[16,3968]{1,0:T(8,128)(2,1)S(1)} %collective-permute-done.3.refs_1_.refs_11_), channel_id=1, source_target_pairs={{0,4},{4,0},{8,12},{12,8},{16,20},{20,16},{24,28},{28,24},{1,5},{5... | collective-permute-start | bytes 380936 | tf_op jit(solution)/shard_map/ppermute | solution.py:339
  23.8 5.5 %collective-permute-start.10 = (f32[16,16]{1,0:T(8,128)S(1)}, f32[16,16]{1,0:T(8,128)S(1)}, u32[]{:S(2)}, u32[]{:S(2)}) collective-permute-start(f32[16,16]{1,0:T(8,128)S(1)} %get-tuple-element.21), channel_id=1, source_target_pairs={{0,3},{1,2},{2,1},{3,0},{4,7},{5,6},{6,5},{7,4},{8,11},{9,10},{10,... | collective-permute-start | bytes 3080 | tf_op jit(solution)/shard_map/ppermute | solution.py:342
  27.0 4.5 %collective-permute-start.12 = (f32[16,16]{1,0:T(8,128)S(1)}, f32[16,16]{1,0:T(8,128)S(1)}, u32[]{:S(2)}, u32[]{:S(2)}) collective-permute-start(f32[16,16]{1,0:T(8,128)S(1)} %get-tuple-element.22), channel_id=1, source_target_pairs={{0,2},{1,3},{2,0},{3,1},{4,6},{5,7},{6,4},{7,5},{8,10},{9,11},{10,... | collective-permute-start | bytes 3080 | tf_op jit(solution)/shard_map/ppermute | solution.py:342
  27.0 4.5 %collective-permute-start.11 = (f32[16,16]{1,0:T(8,128)S(1)}, f32[16,16]{1,0:T(8,128)S(1)}, u32[]{:S(2)}, u32[]{:S(2)}) collective-permute-start(f32[16,16]{1,0:T(8,128)S(1)} %get-tuple-element.23), channel_id=1, source_target_pairs={{0,1},{1,0},{2,3},{3,2},{4,5},{5,4},{6,7},{7,6},{8,9},{9,8},{10,11... | collective-permute-start | bytes 3080 | tf_op jit(solution)/shard_map/ppermute | solution.py:342
